TPU v7x, 32 devices: a whole 2x2x4 slice. The times are simulated.
32 devices in a mesh: dp: 4 (over x, core), region: 4 (over z), heads: 2 (over y).
Axes of the slice: x: 2, y: 2, z: 4, core: 2. Of those that a mesh axis runs over, the one named last changes fastest.
Arguments:
- enc_in: bfloat16 [8, 192, 1152], P('dp', 'region'), may hold values from -6 to 6
- kept_pos: int32 [8, 192], P('dp', 'region'), may hold values from 0 to 63, as said below
- slot_live: int32 [8, 192], P('dp', 'region'), may hold values from 0 to 1, as said below
- condition: bfloat16 [8, 1152], P('dp'), may hold values from -6 to 6
- mask_token: bfloat16 [1152], replicated, may hold values from -6 to 6
- enc_ada: bfloat16 [1152, 6912], P(None, ('region', 'heads')), may hold values from -0.1875 to 0.1875
- enc_qkv: bfloat16 [1152, 3, 1152], P(None, None, 'heads'), may hold values from -0.1875 to 0.1875
- enc_proj: bfloat16 [1152, 1152], P('heads'), may hold values from -0.5 to 0.5
- enc_up: bfloat16 [1152, 4608], P(None, 'heads'), may hold values from -0.1875 to 0.1875
- enc_down: bfloat16 [4608, 1152], P('heads'), may hold values from -0.09375 to 0.09375
- dec_ada: bfloat16 [1152, 6912], P(None, ('region', 'heads')), may hold values from -0.1875 to 0.1875
- dec_qkv: bfloat16 [1152, 3, 1152], P(None, None, 'heads'), may hold values from -0.1875 to 0.1875
- dec_proj: bfloat16 [1152, 1152], P('heads'), may hold values from -0.5 to 0.5
- dec_up: bfloat16 [1152, 4608], P(None, 'heads'), may hold values from -0.1875 to 0.1875
- dec_down: bfloat16 [4608, 1152], P('heads'), may hold values from -0.09375 to 0.09375
- cotangent: bfloat16 [8, 256, 1152], P('dp', 'region'), may hold values from -6 to 6
Outputs:
- out: bfloat16 [8, 256, 1152], P('dp', 'region')
- input_grad: float32 [8, 192, 1152], P('dp', 'region')
- mask_grad: float32 [1152], P(('dp', 'region'))
- enc_ada_grad: float32 [1152, 6912], P('dp', ('region', 'heads'))
- enc_qkv_grad: float32 [1152, 3, 1152], P(('dp', 'region'), None, 'heads')
- enc_proj_grad: float32 [1152, 1152], P('heads', ('dp', 'region'))
- enc_up_grad: float32 [1152, 4608], P(('dp', 'region'), 'heads')
- enc_down_grad: float32 [4608, 1152], P('heads', ('dp', 'region'))
- dec_ada_grad: float32 [1152, 6912], P('dp', ('region', 'heads'))
- dec_qkv_grad: float32 [1152, 3, 1152], P(('dp', 'region'), None, 'heads')
- dec_proj_grad: float32 [1152, 1152], P('heads', ('dp', 'region'))
- dec_up_grad: float32 [1152, 4608], P(('dp', 'region'), 'heads')
- dec_down_grad: float32 [4608, 1152], P('heads', ('dp', 'region'))
Inputs may be any that keep to these rules, and one draw needn't show every extreme that they name: `kept_pos`: positions are counted within the image's region of 64 tokens; the 48 slots of one image in one region hold distinct positions. `slot_live`: in each image and region the live slots come first and number from 16 to 48; each image has 128 live slots in all, and in every image one region has all 48 slots live.
All inputs are finite; a program needn't handle non-finite values.
Results may differ from a plain program's by a relative error of at most 0.035.
Values may be sent and summed in bfloat16 or wider, within the bound.
No kernel may reach another device: no remote copies, remote signals or barrier semaphores. Data moves between devices by JAX's collectives and lax.ppermute only.
A program may use at most 320 MiB of HBM per device.

v0:
```python
import functools
import math

import jax
import jax.numpy as jnp
from jax import lax
from jax.experimental import pallas as pl
from jax.experimental.pallas import tpu as pltpu
from jax.sharding import PartitionSpec as P

HS = 72
SCALE = 1.0 / math.sqrt(HS)
EPSILON = 1e-06
BF16 = jnp.bfloat16
F32 = jnp.float32
VMEM_LIMIT = 28 * 2**20
NT = ((1,), (1,))
TN = ((0,), (0,))


def dot(a, b, dims=((1,), (0,)), **kw):
    return lax.dot_general(a, b, (dims, ((), ())), preferred_element_type=F32, **kw)


class Late:
    def __init__(self, copy, ref):
        self.copy, self.ref, self.waited = copy, ref, False
        copy.start()

    def get(self):
        if not self.waited:
            self.copy.wait()
            self.waited = True
        return self.ref


def here(ref):
    return ref.get() if isinstance(ref, Late) else ref


def call(kernel, outs, *ins, flops=0, scratch=(), late=(), limit=VMEM_LIMIT):
    shapes = [jax.ShapeDtypeStruct(shape, dtype) for shape, dtype in outs]
    moved = sum(math.prod(a.shape) * a.dtype.itemsize for a in list(ins) + shapes)
    fetched = [pltpu.VMEM(ins[i].shape, ins[i].dtype) for i in late]
    semaphores = [pltpu.SemaphoreType.DMA((len(late),))] if late else []

    def body(*refs):
        refs = list(refs)
        own = len(refs) - len(late) - len(semaphores)
        for at, i in enumerate(late):
            refs[i] = Late(pltpu.make_async_copy(refs[i], refs[own + at], refs[-1].at[at]), refs[own + at])
        kernel(*refs[:own])
        for i in late:
            refs[i].get()

    vmem, hbm = pl.BlockSpec(memory_space=pltpu.VMEM), pl.BlockSpec(memory_space=pl.ANY)
    return pl.pallas_call(
        body,
        out_shape=shapes,
        in_specs=[hbm if i in late else vmem for i in range(len(ins))],
        out_specs=[vmem] * len(outs),
        scratch_shapes=list(scratch) + fetched + semaphores,
        compiler_params=pltpu.CompilerParams(vmem_limit_bytes=limit),
        cost_estimate=pl.CostEstimate(flops=flops, bytes_accessed=0, transcendentals=0),
    )(*ins)


def load_kernel(*refs):
    count = len(refs) // 2
    copies = [
        pltpu.make_async_copy(refs[i], refs[count + i], refs[-1].at[i]) for i in range(count)
    ]
    for copy in copies:
        copy.start()
    for copy in copies:
        copy.wait()


def load(anchor, *weights):
    anchor, *weights = tie(anchor, *weights)
    loaded = pl.pallas_call(
        load_kernel,
        out_shape=[jax.ShapeDtypeStruct(w.shape, w.dtype) for w in weights],
        in_specs=[pl.BlockSpec(memory_space=pl.ANY)] * len(weights),
        out_specs=[pl.BlockSpec(memory_space=pltpu.VMEM)] * len(weights),
        scratch_shapes=[pltpu.SemaphoreType.DMA((len(weights),))],
        compiler_params=pltpu.CompilerParams(vmem_limit_bytes=VMEM_LIMIT),
        cost_estimate=pl.CostEstimate(
            flops=3*10**9, bytes_accessed=0, transcendentals=0
        ),
    )(*weights)
    return anchor, *loaded


def tie(*arrays):
    return lax.optimization_barrier(arrays)


def norm(rows):
    mean = jnp.mean(rows, axis=-1, keepdims=True)
    centered = rows - mean
    inverse = lax.rsqrt(jnp.mean(centered * centered, axis=-1, keepdims=True) + EPSILON)
    return centered * inverse, inverse


def norm_back(grad, normed, inverse):
    return inverse * (
        grad
        - jnp.mean(grad, axis=-1, keepdims=True)
        - normed * jnp.mean(grad * normed, axis=-1, keepdims=True)
    )


def padded(width):
    return -(-width // 128) * 128


def side(a):
    more = padded(a.shape[1]) - a.shape[1]
    return jnp.concatenate([a, jnp.zeros((a.shape[0], more), a.dtype)], axis=1) if more else a


def wide(ref):
    return here(ref)[...].astype(F32)


def row(ref, i):
    return ref[i : i + 1, :]


def total(ref, *columns):
    return jnp.sum(ref, axis=0, keepdims=True)


def qkv_rows(x, mod, qkv, hidden_ref, q_ref, kv_ref):
    width = q_ref.shape[1]
    hidden = (norm(x)[0] * (1.0 + row(mod, 1)) + row(mod, 0)).astype(BF16)
    hidden_ref[...] = hidden
    projected = dot(hidden, qkv[...], NT).astype(BF16)
    q_ref[...] = projected[:, :width]
    kv_ref[:, : 2 * width] = projected[:, width:]


def enc_qkv_kernel(first, second, mod, qkv, x_ref, hidden_ref, q_ref, kv_ref):
    features = x_ref.shape[1]
    both = jnp.concatenate([first[...], second[...]])
    x = both[:, :features].astype(F32)
    x_ref[...] = x
    qkv_rows(x, mod, qkv, hidden_ref, q_ref, kv_ref)
    width = q_ref.shape[1]
    kv_ref[:, 2 * width :] = (both[:, features:].astype(F32) >= 0.0).astype(F32).astype(BF16)


def block_end(residual, part, other, mod):
    return residual[...] + row(mod, 5) * (wide(part) + wide(other))


def dec_qkv_kernel(
    residual, part, other, enc_mod, matches, mask, mod, qkv, x_ref, hidden_ref, q_ref, kv_ref
):
    enc_out = block_end(residual, part, other, enc_mod)
    found = matches[...]
    uncovered = 1.0 - jnp.sum(found, axis=1, keepdims=True)
    x = dot(found, enc_out, precision=lax.Precision.HIGHEST) + uncovered * wide(mask)
    x_ref[...] = x
    qkv_rows(x, mod, qkv, hidden_ref, q_ref, kv_ref)


def window(head, width):
    first, last = head * HS, (head + 1) * HS
    start, stop = first // 128 * 128, min(-(-last // 128) * 128, width)
    lanes = lax.broadcasted_iota(jnp.int32, (1, stop - start), 1) + start
    return slice(start, stop), ((lanes >= first) & (lanes < last)).astype(F32)


def probs_of(queries, keys, live):
    scores = dot(keys, queries, NT) * SCALE
    if live is not None:
        scores = jnp.where(live, scores, -1e30)
    exponent = jnp.exp(scores - jnp.max(scores, axis=0, keepdims=True))
    return exponent / jnp.sum(exponent, axis=0, keepdims=True)


def live_of(kv, kv_other, width):
    if kv.shape[1] == 2 * width:
        return None
    own, other = (a[:, 2 * width : 2 * width + 128].astype(F32)[:, :1] for a in (kv, kv_other))
    return jnp.concatenate([own, other]) > 0.5


def attention_kernel(q, kv, kv_other, proj, hidden, *refs):
    width, features = q.shape[1], hidden.shape[1]
    if len(refs) > 3:
        first, second, mod, rows_ref, part_ref, grad_ref, total_ref = refs
        grad_out = jnp.concatenate([first[...], second[...]])
        grad_ref[...] = grad_out
        rows_ref[:, features : 2 * features] = (row(mod, 5) * grad_out.astype(F32)).astype(BF16)
    else:
        rows_ref, part_ref, total_ref = refs
    rows_ref[:, :features] = hidden[...]
    live = live_of(kv, kv_other, width)
    total_ref[...] = jnp.zeros_like(total_ref)
    for head in range(width // HS):
        at, mask = window(head, width)
        beside = slice(width + at.start, width + at.stop)
        queries = (wide(q.at[:, at]) * mask).astype(BF16)
        keys = jnp.concatenate([kv[:, at], kv_other[:, at]])
        values = jnp.concatenate([kv[:, beside], kv_other[:, beside]])
        probs = probs_of(queries, keys, live).astype(BF16)
        total_ref[:, at] += dot(probs, values, TN) * mask
    attended = total_ref[...].astype(BF16)
    rows_ref[:, rows_ref.shape[1] - padded(width) :] = side(attended)
    part_ref[...] = dot(attended, here(proj)[...]).astype(BF16)


def mlp_kernel(x, part, other, mod, up, down, *refs):
    before, (residual_ref, pre_ref, rows_ref, part_ref) = refs[:-4], refs[-4:]
    features = x.shape[1]
    if before:
        rows_ref[:, up.shape[1] + features :] = before[0][...]
    hidden_units = up.shape[1]
    residual = x[...] + row(mod, 2) * (wide(part) + wide(other))
    residual_ref[...] = residual
    mlp_input = (norm(residual)[0] * (1.0 + row(mod, 4)) + row(mod, 3)).astype(BF16)
    rows_ref[:, hidden_units : hidden_units + features] = mlp_input
    pre = dot(mlp_input, up[...])
    pre_ref[...] = pre
    activated = jax.nn.gelu(pre, approximate=True).astype(BF16)
    rows_ref[:, :hidden_units] = activated
    part_ref[...] = dot(activated, down[...]).astype(BF16)


def gelu_slope(u):
    c = math.sqrt(2.0 / math.pi)
    t = jnp.tanh(c * (u + 0.044715 * u * u * u))
    return 0.5 * (1.0 + t) + 0.5 * u * (1.0 - t * t) * c * (1.0 + 3 * 0.044715 * u * u)


def enc_mlp_back_kernel(grad_out, pre, mod, up, down, rows_ref, part_ref):
    hidden_units = up.shape[1]
    grad_mlp = (row(mod, 5) * wide(grad_out)).astype(BF16)
    rows_ref[:, hidden_units:] = grad_mlp
    mlp_back(grad_mlp, pre, up, down, rows_ref, part_ref)


def dec_mlp_back_kernel(attn_rows, pre, up, down, rows_ref, part_ref):
    features = up.shape[0]
    mlp_back(attn_rows[:, features : 2 * features], pre, up, down, rows_ref, part_ref)


def mlp_back(grad_mlp, pre, up, down, rows_ref, part_ref):
    hidden_units = up.shape[1]
    grad_pre = (dot(grad_mlp, down[...], NT) * gelu_slope(here(pre)[...])).astype(BF16)
    rows_ref[:, :hidden_units] = grad_pre
    part_ref[...] = dot(grad_pre, up[...], NT).astype(BF16)


def attention_back_kernel(
    grad_out, part, other, residual, branch, branch_other, mod, proj, q, kv, kv_other,
    grad_residual_ref, grad_branch_ref, dq_ref, dkv_ref, dkv_other_ref, sums_ref,
    dk_ref, dv_ref,
):
    rows, width = dq_ref.shape
    grad_input = wide(part) + wide(other)
    normed, inverse = norm(here(residual)[...])
    sums_ref[0:1, :] = jnp.sum(grad_input, axis=0, keepdims=True)
    sums_ref[1:2, :] = jnp.sum(grad_input * normed, axis=0, keepdims=True)
    grad_residual = wide(grad_out) + norm_back(grad_input * (1.0 + row(mod, 4)), normed, inverse)
    grad_residual_ref[...] = grad_residual
    sums_ref[2:3, :] = jnp.sum(
        grad_residual * (wide(branch) + wide(branch_other)), axis=0, keepdims=True
    )
    grad_branch = (row(mod, 2) * grad_residual).astype(BF16)
    grad_branch_ref[...] = grad_branch
    grad_attended = dot(grad_branch, here(proj)[...], NT).astype(BF16).astype(F32)
    q, kv, kv_other = here(q), here(kv), here(kv_other)

    live = live_of(kv, kv_other, width)
    dk_ref[...] = jnp.zeros_like(dk_ref)
    dv_ref[...] = jnp.zeros_like(dv_ref)
    dq_total = []
    for head in range(width // HS):
        at, mask = window(head, width)
        beside = slice(width + at.start, width + at.stop)
        queries = (wide(q.at[:, at]) * mask).astype(BF16)
        grad_head = (grad_attended[:, at] * mask).astype(BF16)
        keys = jnp.concatenate([kv[:, at], kv_other[:, at]])
        values = jnp.concatenate([kv[:, beside], kv_other[:, beside]])
        probs = probs_of(queries, keys, live)
        grad_probs = dot(values, grad_head, NT)
        inner = jnp.sum(probs * grad_probs, axis=0, keepdims=True)
        grad_scores = (probs * (grad_probs - inner)).astype(BF16)
        dk_ref[:, at] += dot(grad_scores, queries)
        dv_ref[:, at] += dot(probs.astype(BF16), grad_head)
        dq_total.append((at, dot(grad_scores, keys, TN) * (mask * SCALE)))
    for tile in range(0, width, 128):
        stop = min(tile + 128, width)
        terms = [
            part_[:, tile - at.start : stop - at.start]
            for at, part_ in dq_total
            if at.start <= tile and stop <= at.stop
        ]
        dq_ref[:, tile:stop] = functools.reduce(lambda a, b: a + b, terms).astype(BF16)
    dkv_ref[:, :width] = dk_ref[:rows, :] * SCALE
    dkv_ref[:, width:] = dv_ref[:rows, :]
    dkv_other_ref[:, :width] = (dk_ref[rows:, :] * SCALE).astype(BF16)
    dkv_other_ref[:, width:] = dv_ref[rows:, :].astype(BF16)


def qkv_back_kernel(dq, dkv, dkv_other, grad_branch, qkv, rows_ref, part_ref):
    features = grad_branch.shape[1]
    grad_projected = jnp.concatenate(
        [dq[...], (dkv[...] + wide(dkv_other)).astype(BF16)], axis=1
    )
    rows_ref[:, :features] = grad_branch[...]
    rows_ref[:, features:] = side(grad_projected)
    part_ref[...] = dot(grad_projected, here(qkv)[...]).astype(BF16)


def block_back(part, other, grad_residual, x, mod, grad_out, mlp, mlp_other, sums_ref):
    grad_hidden = wide(part) + wide(other)
    normed, inverse = norm(here(x)[...])
    sums_ref[0:1, :] = jnp.sum(grad_hidden, axis=0, keepdims=True)
    sums_ref[1:2, :] = jnp.sum(grad_hidden * normed, axis=0, keepdims=True)
    sums_ref[2:3, :] = jnp.sum(wide(grad_out) * (wide(mlp) + wide(mlp_other)), axis=0, keepdims=True)
    return grad_residual[...] + norm_back(grad_hidden * (1.0 + row(mod, 1)), normed, inverse)


def dec_end_kernel(
    part, other, grad_residual, x, mod, grad_out, mlp, mlp_other, matches, grad_ref, sums_ref
):
    grad_x = block_back(part, other, grad_residual, x, mod, grad_out, mlp, mlp_other, sums_ref)
    found = matches[...]
    uncovered = 1.0 - jnp.sum(found, axis=1, keepdims=True)
    sums_ref[3:4, :] = jnp.sum(uncovered * grad_x, axis=0, keepdims=True)
    grad_ref[...] = dot(found, grad_x, TN, precision=lax.Precision.HIGHEST)


def enc_end_kernel(
    part, other, grad_residual, x, mod, grad_out, mlp, mlp_other, grad_ref, sums_ref
):
    grad_ref[...] = block_back(
        part, other, grad_residual, x, mod, grad_out, mlp, mlp_other, sums_ref
    )
    sums_ref[3:4, :] = jnp.zeros_like(sums_ref[3:4, :])


def out_kernel(residual, part, other, mod, out_ref):
    out_ref[...] = block_end(residual, part, other, mod).astype(BF16)


def weight_grad_kernel(products, *refs):
    count = 1 + max(max(p[0][0], p[1][0]) for p in products)
    bundles, refs = refs[: 4 * count], refs[4 * count :]
    select, sent_ref, kept_ref, *buffers, semaphores = refs
    features = select.shape[1]
    half = sent_ref.shape[0]
    copies = []
    for at, ((narrow, first), (full, start, span)) in enumerate(products):
        for bundle, begin, size, buffer in (
            (narrow, first, features, buffers[2 * at]),
            (full, start, padded(span), buffers[2 * at + 1]),
        ):
            for part in range(4):
                source = bundles[4 * bundle + part]
                rows = source.shape[0]
                copies.append(
                    pltpu.make_async_copy(
                        source.at[:, begin : begin + size],
                        buffer.at[part * rows : (part + 1) * rows, :],
                        semaphores.at[len(copies)],
                    )
                )
                copies[-1].start()
    column = 0
    for at, (_, (_, _, span)) in enumerate(products):
        features_all, rows_all = buffers[2 * at], buffers[2 * at + 1]
        for copy in copies[8 * at : 8 * at + 4]:
            copy.wait()
        chosen = dot(select[...], features_all[...], NT).astype(BF16)
        for copy in copies[8 * at + 4 : 8 * at + 8]:
            copy.wait()
        sent_ref[:, column : column + span] = dot(chosen[:half], rows_all[:, :span]).astype(BF16)
        kept_ref[:, column : column + span] = dot(chosen[half:], rows_all[:, :span])
        column += span


def halve_kernel(kept, got, sent_ref, kept_ref):
    rows = kept_ref.shape[0]
    sums = kept[...] + wide(got)
    kept_ref[...] = sums[:rows]
    sent_ref[...] = sums[rows:].astype(BF16)


def finish_kernel(kept, got, *outs):
    at = 0
    for out in outs:
        for part in range(out.shape[0] if len(out.shape) == 3 else 1):
            span = out.shape[-1]
            place = (part,) if len(out.shape) == 3 else ()
            out[place + (...,)] = kept[:, at : at + span] + wide(got.at[:, at : at + span])
            at += span


def in_order(mine, other, bit):
    return jnp.stack([jnp.where(bit == 0, mine, other), jnp.where(bit == 0, other, mine)])


class Net:
    def __init__(self, mesh):
        self.ndp, self.nreg, self.nhead = (mesh.shape[a] for a in ("dp", "region", "heads"))
        assert self.nreg == 4 and self.nhead == 2 and self.ndp % 2 == 0
        self.nhi = self.ndp // 2
        self.core_perm = [(d, d ^ 1) for d in range(self.ndp)]
        self.near = [(z, z ^ 1) for z in range(4)]
        self.far = [(z, z ^ 2) for z in range(4)]
        self.spread = [
            [
                (d * 4 + r, (d - d % 2 + r // 2) * 4 + 2 * (d % 2) + (r + j) % 2)
                for d in range(self.ndp)
                for r in range(4)
            ]
            for j in range(2)
        ]

    def place(self):
        self.dp = lax.axis_index("dp")
        self.hi, self.core = self.dp // 2, self.dp % 2
        self.z = lax.axis_index("region")
        self.z1, self.z0 = self.z // 2, self.z % 2
        self.y = lax.axis_index("heads")

    def to_core(self, a):
        return lax.ppermute(a, "dp", self.core_perm)

    def to_near(self, a):
        return lax.ppermute(a, "region", self.near)

    def to_far(self, a):
        return lax.ppermute(a, "region", self.far)

    def to_heads(self, a):
        return lax.ppermute(a, "heads", [(0, 1), (1, 0)])

    def to_hi(self, a):
        return lax.ppermute(a, "dp", [(d, d ^ 2) for d in range(self.ndp)])

    def hi_groups(self):
        return [[c + 2 * h for h in range(self.nhi)] for c in range(2)]

    def gather_hi(self, a):
        if self.nhi == 1:
            return a[None]
        if self.nhi == 2:
            return in_order(a, self.to_hi(a), self.hi)
        return lax.all_gather(a, "dp", axis_index_groups=self.hi_groups(), axis=0)

    def spread_images(self, a):
        even = self.z0 == 0
        first, second = jnp.where(even, a[0], a[1]), jnp.where(even, a[1], a[0])
        return [
            lax.ppermute(part, ("dp", "region"), perm)
            for part, perm in zip((first, second), self.spread)
        ]

    def collect_parts(self, parts):
        return [
            lax.ppermute(part, ("dp", "region"), [(t, s) for s, t in perm])
            for part, perm in zip(parts, self.spread)
        ]

    def collected(self, back):
        even = self.z0 == 0
        return jnp.stack([jnp.where(even, back[0], back[1]), jnp.where(even, back[1], back[0])])

    def gather(self, rows):
        if self.nhi == 2:
            return rows, self.to_near(rows)
        if self.nhi > 2:
            rows = lax.all_gather(
                rows, "dp", axis_index_groups=self.hi_groups(), axis=0, tiled=True
            )
        half = rows.shape[0] // 2
        return rows[:half], rows[half:]

    def selection(self, features):
        own = features // (self.ndp * 4)
        step = jnp.arange(4 * own)
        if self.nhi == 2:
            block = jnp.array([8, 10, 0, 2])[step // own]
        else:
            block = jnp.array([1, 3, 0, 2])[step // own]
        feature = ((self.dp * 4 + self.z) ^ block) * own + step % own
        return (feature[:, None] == jnp.arange(features)[None, :]).astype(BF16)

    def first_half(self, sent):
        return self.to_hi(sent) if self.nhi == 2 else self.to_near(sent)


def weight_grads(products, bundles, select):
    half = select.shape[0] // 2
    features = select.shape[1]
    width = sum(full[2] for _, full in products)
    rows = 4 * bundles[0][0].shape[0]
    operands = [a for bundle in bundles for a in bundle]
    vmem, hbm = pl.BlockSpec(memory_space=pltpu.VMEM), pl.BlockSpec(memory_space=pl.ANY)
    buffers = [
        pltpu.VMEM((rows, padded(span)), BF16)
        for _, (_, _, size) in products
        for span in (features, size)
    ]
    held = sum(2 * math.prod(buffer.shape) for buffer in buffers) + 16 * 2**20
    return pl.pallas_call(
        functools.partial(weight_grad_kernel, products),
        out_shape=[
            jax.ShapeDtypeStruct((half, width), BF16), jax.ShapeDtypeStruct((half, width), F32)
        ],
        in_specs=[hbm] * len(operands) + [vmem],
        out_specs=[vmem] * 2,
        scratch_shapes=buffers + [pltpu.SemaphoreType.DMA((8 * len(products),))],
        compiler_params=pltpu.CompilerParams(vmem_limit_bytes=max(VMEM_LIMIT, held)),
        cost_estimate=pl.CostEstimate(
            flops=4 * half * rows * (width + len(products) * features),
            bytes_accessed=0,
            transcendentals=0,
        ),
    )(*operands, select)


def finish(kept, got, *shapes):
    return call(finish_kernel, [(shape, F32) for shape in shapes], kept, got)


def halve(kept, got):
    rows, width = kept.shape
    return call(halve_kernel, [((rows // 2, width), BF16), ((rows // 2, width), F32)], kept, got)


def shards(
    net, enc_in, kept_pos, slot_live, condition, mask_token, enc_ada, enc_qkv, enc_proj, enc_up,
    enc_down, dec_ada, dec_qkv, dec_proj, dec_up, dec_down, cotangent,
):
    net.place()
    cap, features = enc_in.shape[1:]
    tokens = cotangent.shape[1]
    assert enc_in.shape[0] == 2
    width, units = enc_proj.shape[0], enc_up.shape[1]
    select = net.selection(features)
    enc_qkv, dec_qkv = (
        jnp.transpose(a, (1, 2, 0)).reshape(3 * width, features) for a in (enc_qkv, dec_qkv)
    )

    code = jnp.where(slot_live > 0, kept_pos, -1).astype(BF16)
    sent = jnp.concatenate([enc_in, jnp.broadcast_to(code[..., None], code.shape + (128,))], axis=2)
    slots = net.spread_images(sent)
    code = jnp.concatenate([part[:, features] for part in slots]).astype(jnp.int32)
    place = jnp.arange(2 * tokens)
    matches = (place[:, None] // tokens == jnp.arange(2 * cap)[None, :] // cap) & (
        code[None, :] == place[:, None] % tokens
    )
    matches = matches.astype(F32)

    silu = jax.nn.silu(condition.astype(F32)).astype(BF16)
    silu = in_order(silu, net.to_core(silu), net.core).reshape(4, features)
    cols = jnp.concatenate([dot(silu, enc_ada), dot(silu, dec_ada)], axis=1)
    block = enc_ada.shape[1]
    cols = cols.reshape(2, 2, 2 * block)
    got = net.to_near(lax.dynamic_index_in_dim(cols, 1 - net.z0, 1, False))
    cols = in_order(lax.dynamic_index_in_dim(cols, net.z0, 1, False), got, net.z0)
    got = net.to_far(lax.dynamic_index_in_dim(cols, 1 - net.z1, 1, False))
    cols = in_order(lax.dynamic_index_in_dim(cols, net.z1, 1, False), got, net.z1)
    cols = in_order(cols, net.to_heads(cols), net.y)
    cols = jnp.moveaxis(cols, 0, 2).reshape(8, 2, block)
    enc_mod = cols[:, 0].reshape(6, features)
    dec_mod = cols[:, 1].reshape(6, features)

    def attention(q, kv, kv_other, proj, hidden, *more):
        rows = q.shape[0]
        beside = [((rows, features), BF16)] if more else []
        return call(
            attention_kernel,
            [((rows, padded(width) + (1 + len(beside)) * features), BF16), ((rows, features), BF16)] + beside,
            q, kv, kv_other, proj, hidden, *more, late=(3,),
            flops=2 * rows * width * (features + 4 * rows), scratch=[pltpu.VMEM((rows, width), F32)],
        )

    def mlp(x, part, other, mod, up, down, *more):
        rows = x.shape[0]
        beside = units + features + sum(a.shape[1] for a in more)
        return call(
            mlp_kernel,
            [((rows, features), F32), ((rows, units), F32), ((rows, beside), BF16), ((rows, features), BF16)],
            x, part, other, mod, up, down, *more, flops=4 * rows * features * units,
        )

    def attention_back(grad_out, part, other, s, mod, proj):
        rows = grad_out.shape[0]
        return call(
            attention_back_kernel,
            [
                ((rows, features), F32), ((rows, features), BF16), ((rows, width), BF16),
                ((rows, 2 * width), F32), ((rows, 2 * width), BF16), ((3, features), F32),
            ],
            grad_out, part, other, s["residual"], s["branch"], s["branch_other"], mod, proj,
            s["q"], s["kv"], s["kv_other"], late=(3, 4, 5, 8, 9, 10),
            flops=2 * rows * width * (features + 10 * rows),
            scratch=[pltpu.VMEM((2 * rows, width), F32)] * 2,
        )

    def qkv_back(dq, dkv, dkv_other, grad_branch, qkv):
        rows = dq.shape[0]
        return call(
            qkv_back_kernel, [((rows, padded(3 * width) + features), BF16), ((rows, features), BF16)],
            dq, dkv, dkv_other, grad_branch, qkv, flops=6 * rows * features * width,
        )

    def end(kernel, grad_residual, part, other, grad_out, s, mod, *extra):
        return call(
            kernel, [((2 * cap, features), F32), ((4, features), F32)],
            part, other, grad_residual, s["x"], mod, grad_out, s["mlp"], s["mlp_other"], *extra,
            late=(3, 6, 7),
        )

    rows = 2 * cap
    x, hidden, q, kv = call(
        enc_qkv_kernel,
        [((rows, features), F32), ((rows, features), BF16), ((rows, width), BF16), ((rows, 2 * width + 128), BF16)],
        *slots, enc_mod, enc_qkv, flops=6 * rows * features * width,
    )
    kv_other = net.to_core(kv)
    enc_attn_rows, branch = attention(q, kv, kv_other, enc_proj, hidden)
    branch, up, down = load(branch, enc_up, enc_down)
    branch_other = net.to_heads(branch)
    residual, pre, enc_rows, mlp_part = mlp(
        x, branch, branch_other, enc_mod, up, down, enc_attn_rows
    )
    mlp_part, qkv = load(mlp_part, dec_qkv)
    mlp_other = net.to_heads(mlp_part)
    enc = dict(
        x=x, q=q, kv=kv, kv_other=kv_other, branch=branch, branch_other=branch_other,
        residual=residual, pre=pre, mlp=mlp_part, mlp_other=mlp_other,
    )
    enc_rows, enc_rows_near = net.gather(enc_rows)
    cotangent, _ = tie(cotangent, branch)
    grad_parts = net.spread_images(cotangent)

    rows = 2 * tokens
    mlp_other, *grad_parts = tie(mlp_other, *grad_parts)
    x, hidden, q, kv = call(
        dec_qkv_kernel,
        [((rows, features), F32), ((rows, features), BF16), ((rows, width), BF16), ((rows, 2 * width), BF16)],
        residual, mlp_part, mlp_other, enc_mod, matches, mask_token[None], dec_mod, qkv,
        flops=6 * rows * features * width,
    )
    kv_other = net.to_core(kv)
    attn_rows, branch, grad_out = attention(q, kv, kv_other, dec_proj, hidden, *grad_parts, dec_mod)
    branch, up, down = load(branch, dec_up, dec_down)
    branch_other = net.to_heads(branch)
    own_rows = attn_rows
    attn_rows, attn_rows_near = net.gather(attn_rows)
    residual, pre, mlp_rows, mlp_part = mlp(x, branch, branch_other, dec_mod, up, down)
    mlp_other = net.to_heads(mlp_part)
    dec = dict(
        x=x, q=q, kv=kv, kv_other=kv_other, branch=branch, branch_other=branch_other,
        residual=residual, pre=pre, mlp=mlp_part, mlp_other=mlp_other,
    )
    mlp_rows, mlp_rows_near = net.gather(mlp_rows)

    grad_rows, part = call(
        dec_mlp_back_kernel, [((rows, units), BF16), ((rows, features), BF16)],
        own_rows, pre, up, down, flops=4 * rows * features * units,
    )
    part, qkv, proj = load(part, dec_qkv, dec_proj)
    other = net.to_heads(part)
    (dec_out,) = call(
        out_kernel, [((rows, features), BF16)], residual, mlp_part, mlp_other, dec_mod
    )
    out_parts = net.collect_parts([dec_out[:tokens], dec_out[tokens:]])
    grad_rows, grad_rows_near = net.gather(grad_rows)
    other, attn_rows_near, enc_rows_near = tie(other, attn_rows_near, enc_rows_near)
    attn_rows = attn_rows, attn_rows_near, net.to_core(attn_rows), net.to_core(attn_rows_near)
    grad_residual, grad_branch, dq, dkv, dkv_other, dec_sums = attention_back(
        grad_out, part, other, dec, dec_mod, proj
    )
    dkv_other, *attn_rows = tie(net.to_core(dkv_other), *attn_rows)
    enc_rows = enc_rows, enc_rows_near, net.to_core(enc_rows), net.to_core(enc_rows_near)
    grad_attn_rows, part = qkv_back(dq, dkv, dkv_other, grad_branch, qkv)
    part, up, down = load(part, enc_up, enc_down)
    other = net.to_heads(part)
    grad_attn_rows, grad_attn_rows_near = net.gather(grad_attn_rows)
    other, mlp_rows_near, *rest = tie(other, mlp_rows_near, *out_parts, *enc_rows)
    out_parts, enc_rows = rest[:2], rest[2:]
    mlp_rows = mlp_rows, mlp_rows_near, net.to_core(mlp_rows), net.to_core(mlp_rows_near)
    grad_enc, dec_more = end(
        dec_end_kernel, grad_residual, part, other, grad_out, dec, dec_mod, matches
    )

    rows = 2 * cap
    grad_out, *mlp_rows = tie(grad_enc, *mlp_rows)
    enc_grad_rows, part = call(
        enc_mlp_back_kernel, [((rows, units + features), BF16), ((rows, features), BF16)],
        grad_out, enc["pre"], enc_mod, up, down, flops=4 * rows * features * units, late=(1,),
    )
    part, qkv, proj = load(part, enc_qkv, enc_proj)
    other = net.to_heads(part)
    enc_grad_rows, enc_grad_rows_near = net.gather(enc_grad_rows)
    down_sent, down_kept = weight_grads(
        (((0, features), (1, 0, units)),), (attn_rows, mlp_rows), select
    )
    down_got = net.first_half(down_sent)
    other, grad_rows_near, down_sent = tie(other, grad_rows_near, down_sent)
    grad_rows = grad_rows, grad_rows_near, net.to_core(grad_rows), net.to_core(grad_rows_near)
    grad_residual, grad_branch, dq, dkv, dkv_other, enc_sums = attention_back(
        grad_out, part, other, enc, enc_mod, proj
    )
    dkv_other, *grad_rows = tie(net.to_core(dkv_other), *grad_rows)
    enc_grad_attn_rows, part = qkv_back(dq, dkv, dkv_other, grad_branch, qkv)
    other = net.to_heads(part)
    enc_grad_attn_rows, enc_grad_attn_rows_near = net.gather(enc_grad_attn_rows)
    up_sent, up_kept = weight_grads(
        (((0, units), (1, 0, units)),), (mlp_rows, grad_rows), select
    )
    up_got = net.first_half(up_sent)
    other, up_sent, down_got, grad_attn_rows_near = tie(other, up_sent, down_got, grad_attn_rows_near)
    grad_attn_rows = (
        grad_attn_rows, grad_attn_rows_near, net.to_core(grad_attn_rows), net.to_core(grad_attn_rows_near)
    )
    down_sent, down_kept = halve(down_kept, down_got)
    down_got = net.to_far(down_sent)
    grad_in, enc_more = end(enc_end_kernel, grad_residual, part, other, grad_out, enc, enc_mod)

    grad_in, down_sent, *grad_attn_rows = tie(grad_in, down_sent, *grad_attn_rows)
    attn_sent, attn_kept = weight_grads(
        (((0, 0), (1, features, 3 * width)), ((1, 0), (0, 2 * features, width))),
        (attn_rows, grad_attn_rows), select,
    )
    attn_got = net.first_half(attn_sent)
    attn_sent, enc_grad_rows_near = tie(attn_sent, enc_grad_rows_near)
    enc_grad_rows = (
        enc_grad_rows, enc_grad_rows_near, net.to_core(enc_grad_rows), net.to_core(enc_grad_rows_near)
    )
    enc_up_sent, enc_up_kept = weight_grads(
        (((0, units), (1, 0, units)),), (enc_rows, enc_grad_rows), select
    )
    enc_up_got = net.first_half(enc_up_sent)
    up_got, enc_up_sent = tie(up_got, enc_up_sent)
    up_sent, up_kept = halve(up_kept, up_got)
    up_got = net.to_far(up_sent)
    up_sent, *enc_grad_rows = tie(up_sent, *enc_grad_rows)
    enc_down_sent, enc_down_kept = weight_grads(
        (((1, units), (0, 0, units)),), (enc_rows, enc_grad_rows), select
    )
    enc_down_got = net.first_half(enc_down_sent)
    enc_down_sent, enc_grad_attn_rows_near = tie(enc_down_sent, enc_grad_attn_rows_near)
    enc_grad_attn_rows = (
        enc_grad_attn_rows, enc_grad_attn_rows_near,
        net.to_core(enc_grad_attn_rows), net.to_core(enc_grad_attn_rows_near),
    )
    enc_attn_sent, enc_attn_kept = weight_grads(
        (
            ((0, units + features), (1, features, 3 * width)),
            ((1, 0), (0, units + 2 * features, width)),
        ),
        (enc_rows, enc_grad_attn_rows), select,
    )
    enc_attn_got = net.first_half(enc_attn_sent)
    attn_got, enc_attn_sent = tie(attn_got, enc_attn_sent)
    attn_sent, attn_kept = halve(attn_kept, attn_got)
    attn_got = net.to_far(attn_sent)
    enc_up_sent, enc_up_kept = halve(enc_up_kept, enc_up_got)
    enc_up_got = net.to_far(enc_up_sent)
    enc_down_sent, enc_down_kept = halve(enc_down_kept, enc_down_got)
    enc_down_got = net.to_far(enc_down_sent)
    enc_attn_sent, enc_attn_kept = halve(enc_attn_kept, enc_attn_got)
    enc_attn_got = net.to_far(enc_attn_sent)

    out = net.collected(out_parts)
    input_grad = net.collected(net.collect_parts([grad_in[:cap], grad_in[cap:]]))
    mask_part = dec_more[3]

    enc_mod_grad, dec_mod_grad = (
        jnp.concatenate([more[0], more[1], sums[2], sums[0], sums[1], more[2]])
        for more, sums in ((enc_more, enc_sums), (dec_more, dec_sums))
    )

    share = features // (net.ndp * 4)

    def attn_outs(kept, got):
        qkv_grad, proj_grad = finish(kept, got, (3, share, width), (share, width))
        return jnp.transpose(qkv_grad, (1, 0, 2)), proj_grad.T

    def mlp_outs(up_kept, up_got, down_kept, down_got):
        return (
            finish(up_kept, up_got, (share, units))[0], finish(down_kept, down_got, (share, units))[0].T
        )

    enc_grads = attn_outs(enc_attn_kept, enc_attn_got) + mlp_outs(
        enc_up_kept, enc_up_got, enc_down_kept, enc_down_got
    )
    dec_grads = attn_outs(attn_kept, attn_got) + mlp_outs(up_kept, up_got, down_kept, down_got)

    vector = jnp.concatenate([enc_mod_grad, dec_mod_grad, mask_part])
    vector = vector + net.to_core(vector)
    split = 6 * features
    own = features // (net.ndp * 4)
    rows = jnp.concatenate(
        [
            lax.dynamic_index_in_dim(vector[:split].reshape(4, 2, block), net.y, 1, False),
            lax.dynamic_index_in_dim(vector[split : 2 * split].reshape(4, 2, block), net.y, 1, False),
            jnp.moveaxis(vector[2 * split :].reshape(net.ndp, 4, own), 0, 1).reshape(4, -1),
        ],
        axis=1,
    )
    rows = rows.reshape(2, 2, -1)
    got = net.to_near(lax.dynamic_index_in_dim(rows, 1 - net.z0, 1, False))
    rows = in_order(lax.dynamic_index_in_dim(rows, net.z0, 1, False), got, net.z0)
    got = net.to_far(lax.dynamic_index_in_dim(rows, 1 - net.z1, 1, False))
    rows = in_order(lax.dynamic_index_in_dim(rows, net.z1, 1, False), got, net.z1)
    rows = net.gather_hi(rows.reshape(4, -1)).reshape(net.nhi * 4, -1)
    silu_all = net.gather_hi(silu).reshape(net.nhi * 4, features)
    share = features // net.ndp
    silu_own = lax.dynamic_slice_in_dim(silu_all, net.dp * share, share, 1)
    enc_ada_grad = dot(silu_own, rows[:, :block].astype(BF16), TN)
    dec_ada_grad = dot(silu_own, rows[:, block : 2 * block].astype(BF16), TN)
    mask_grad = lax.dynamic_slice_in_dim(jnp.sum(rows[:, 2 * block :], axis=0), net.dp * own, own, 0)
    return (out, input_grad, mask_grad, enc_ada_grad) + enc_grads + (dec_ada_grad,) + dec_grads

def solution(mesh):
    net = Net(mesh)
    in_specs = (
        P("dp", "region", None),
        P("dp", "region"),
        P("dp", "region"),
        P("dp", None),
        P(),
    ) + 2 * (
        P(None, ("region", "heads")),
        P(None, None, "heads"),
        P("heads", None),
        P(None, "heads"),
        P("heads", None),
    ) + (P("dp", "region", None),)
    out_specs = (
        P("dp", "region", None),
        P("dp", "region", None),
        P(("dp", "region")),
    ) + 2 * (
        P("dp", ("region", "heads")),
        P(("dp", "region"), None, "heads"),
        P("heads", ("dp", "region")),
        P(("dp", "region"), "heads"),
        P("heads", ("dp", "region")),
    )
    return jax.shard_map(
        lambda *args: shards(net, *args),
        mesh=mesh, in_specs=in_specs, out_specs=out_specs, check_vma=False,
    )
```

profile of v0, /device:TPU:0, one launch (start us, length us, event | category | flops | bytes accessed | tf_op | source)
XLA Modules:
  0.0 342.1 jit_solution(5724226871587408540)
XLA Ops:
  6.0 3.0 collective-permute-start.3
  10.8 4.7 %collective-permute-start.4 = (f32[2,1728]{1,0:T(2,128)S(1)}, f32[2,1728]{1,0:T(2,128)S(1)}, u32[]{:S(2)}, u32[]{:S(2)}) collective-permute-start(f32[2,1728]{1,0:T(2,128)S(1)} %fusion.9), channel_id=1, source_target_pairs={{0,4},{2,6},{4,0},{6,2},{1,5},{3,7},{5,1},{7,3},{8,12},{10,14},{12... | collective-permute-start | bytes 41480 | tf_op jit(solution)/shard_map/ppermute | solution.py:440
  15.5 5.5 %collective-permute-done.4 = f32[2,1728]{1,0:T(2,128)S(1)} collective-permute-done((f32[2,1728]{1,0:T(2,128)S(1)}, f32[2,1728]{1,0:T(2,128)S(1)}, u32[]{:S(2)}, u32[]{:S(2)}) %collective-permute-start.4) | collective-permute-done | bytes 13856 | tf_op jit(solution)/shard_map/ppermute | solution.py:440
  44.6 5.8 %collective-permute-done.8.refs_2_.refs_7_ = bf16[96,1152]{1,0:T(8,128)(2,1)S(1)} collective-permute-done((bf16[96,1152]{1,0:T(8,128)(2,1)S(1)}, bf16[96,1152]{1,0:T(8,128)(2,1)S(1)}, u32[]{:S(2)}, u32[]{:S(2)}) %collective-permute-start.8) | collective-permute-done | bytes 221216 | tf_op jit(solution)/shard_map/ppermute | solution.py:443
  54.5 2.6 shard_map.270
  59.4 2.5 copy-done.84
  68.8 4.0 %shard_map.273 = (bf16[128,2304]{1,0:T(8,128)(2,1)}, bf16[128,1152]{1,0:T(8,128)(2,1)S(1)}) custom-call(bf16[128,2944]{1,0:T(8,128)(2,1)S(1)} %get-tuple-element.228.refs_0_, f32[128,2304]{1,0:T(8,128)S(1)} %get-tuple-element.192.refs_1_, bf16[1152,2304]{1,0:T(8,128)(2,1)S(1)} %get-tuple-element.190.refs_4_.refs_2_, ...), custom_call_target="tpu_custom_call" | custom-call | flops 1358954496 | tf_op jit(solution)/shard_map/pallas_call | solution.py:57
  74.2 4.2 %collective-permute-done.15.refs_1_ = bf16[96,5248]{1,0:T(8,128)(2,1)S(1)} collective-permute-done((bf16[96,5248]{1,0:T(8,128)(2,1)S(1)}, bf16[96,5248]{1,0:T(8,128)(2,1)S(1)}, u32[]{:S(2)}, u32[]{:S(2)}) %collective-permute-start.15) | collective-permute-done | bytes 1007648 | tf_op jit(solution)/shard_map/ppermute | solution.py:437
  78.4 2.8 collective-permute-done.13.refs_2_
  81.2 12.5 %collective-permute-done.14.refs_1_ = bf16[128,2944]{1,0:T(8,128)(2,1)S(1)} collective-permute-done((bf16[128,2944]{1,0:T(8,128)(2,1)S(1)}, bf16[128,2944]{1,0:T(8,128)(2,1)S(1)}, u32[]{:S(2)}, u32[]{:S(2)}) %collective-permute-start.14) | collective-permute-done | bytes 753696 | tf_op jit(solution)/shard_map/ppermute | solution.py:437
  96.5 5.1 %shard_map.275 = (f32[128,1152]{1,0:T(8,128)S(1)}, bf16[128,1152]{1,0:T(8,128)(2,1)S(1)}, bf16[128,576]{1,0:T(8,128)(2,1)S(1)}, f32[128,1152]{1,0:T(8,128)S(1)},...) custom-call(bf16[128,1152]{1,0:T(8,128)(2,1)S(1)} %get-tuple-element.183.refs_0_.refs_5_, ...), custom_call_target="tpu_custom_call" | custom-call | flops 358612992 | tf_op jit(solution)/shard_map/pallas_call | solution.py:57
  110.6 15.7 %collective-permute-start.26 = (bf16[128,3456]{1,0:T(8,128)(2,1)}, bf16[128,3456]{1,0:T(8,128)(2,1)}, u32[]{:S(2)}, u32[]{:S(2)}) collective-permute-start(bf16[128,3456]{1,0:T(8,128)(2,1)} %get-tuple-element.232.refs_4_.refs_0_), channel_id=1, source_target_pairs={{0,8},{8,0},{16,24},{24,16},{1,9},{9,1},{17,25},{25,17},{2,10},{10... | collective-permute-start | bytes 2654216 | tf_op jit(solution)/shard_map/ppermute | solution.py:434
  132.6 2.6 copy-done.87
  140.4 3.9 %shard_map.280 = (bf16[96,3456]{1,0:T(8,128)(2,1)S(1)}, bf16[96,1152]{1,0:T(8,128)(2,1)S(1)}) custom-call(f32[96,1152]{1,0:T(8,128)S(1)} %get-tuple-element.219.refs_0_.refs_5_, f32[96,2304]{1,0:T(8,128)S(1)} %copy-done.57, f32[6,1152]{1,0:T(8,128)S(1)} %reshape_squeeze.6.refs_2_.refs_3_.refs_6_.refs_4_, bf16[1152,2304]{1,0:T(8,128)(2,1)S(1)} %get-tuple-element.223.refs_3_, ...), custom_call_target="tpu_custom_call" | custom-call | flops 1019215872 | tf_op jit(solution)/shard_map/pallas_call | solution.py:57
  147.1 3.4 shard_map.281
  158.4 5.9 %shard_map.283 = (f32[96,1152]{1,0:T(8,128)S(1)}, bf16[96,1152]{1,0:T(8,128)(2,1)S(1)}, bf16[96,576]{1,0:T(8,128)(2,1)S(1)}, f32[96,1152]{1,0:T(8,128)S(1)}, bf1...) custom-call(f32[96,1152]{1,0:T(8,128)S(1)} %get-tuple-element.219.refs_0_.refs_5_, ...), custom_call_target="tpu_custom_call" | custom-call | flops 233570304 | tf_op jit(solution)/shard_map/pallas_call | solution.py:57
  174.0 2.5 shard_map.284
  178.4 3.5 %shard_map.285 = (bf16[144,2304]{1,0:T(8,128)(2,1)}, f32[144,2304]{1,0:T(8,128)S(1)}) custom-call(bf16[128,3456]{1,0:T(8,128)(2,1)} %get-tuple-element.232.refs_4_.refs_0_, bf16[128,3456]{1,0:T(8,128)(2,1)} %collective-permute-done.20.refs_5_.refs_1_, bf16[128,3456]{1,0:T(8,128)(2,1)} %collective-permute-done.26.refs_6_.refs_2_, ...), custom_call_target="tpu_custom_call" | custom-call | flops 1019215872 | tf_op jit(solution)/shard_map/pallas_call | solution.py:513
  189.9 2.8 collective-permute-done.41
  207.8 3.6 %shard_map.288 = (bf16[144,2304]{1,0:T(8,128)(2,1)S(1)}, f32[144,2304]{1,0:T(8,128)S(1)}) custom-call(bf16[128,2944]{1,0:T(8,128)(2,1)S(1)} %get-tuple-element.228.refs_0_, bf16[128,2944]{1,0:T(8,128)(2,1)S(1)} %copy-done.16, bf16[128,2944]{1,0:T(8,128)(2,1)S(1)} %copy-done.19, bf16[128,2944]{1,0:T(8,128)(2,1)S(1)} %copy-done.22, ...), custom_call_target="tpu_custom_call" | custom-call | flops 1358954496 | tf_op jit(solution)/shard_map/pallas_call | solution.py:513
  214.7 5.7 %collective-permute-done.43 = f32[4,2016]{1,0:T(4,128)S(1)} collective-permute-done((f32[4,2016]{1,0:T(4,128)S(1)}, f32[4,2016]{1,0:T(4,128)S(1)}, u32[]{:S(2)}, u32[]{:S(2)}) %collective-permute-start.43) | collective-permute-done | bytes 32288 | tf_op jit(solution)/shard_map/ppermute | solution.py:446
  225.1 2.6 shard_map.291
  229.7 4.1 %collective-permute-done.49.refs_5_ = bf16[96,2944]{1,0:T(8,128)(2,1)} collective-permute-done((bf16[96,2944]{1,0:T(8,128)(2,1)}, bf16[96,2944]{1,0:T(8,128)(2,1)}, u32[]{:S(2)}, u32[]{:S(2)}) %collective-permute-start.49) | collective-permute-done | bytes 565280 | tf_op jit(solution)/shard_map/ppermute | solution.py:437
  240.9 3.4 shard_map.292
  246.6 6.6 %collective-permute-done.58.refs_1_ = bf16[144,2304]{1,0:T(8,128)(2,1)S(1)} collective-permute-done((bf16[144,2304]{1,0:T(8,128)(2,1)}, bf16[144,2304]{1,0:T(8,128)(2,1)S(1)}, u32[]{:S(2)}, u32[]{:S(2)}) %collective-permute-start.58) | collective-permute-done | bytes 663584 | tf_op jit(solution)/shard_map/ppermute | solution.py:446
  256.7 10.7 %collective-permute-done.54.refs_1_ = bf16[144,2304]{1,0:T(8,128)(2,1)S(1)} collective-permute-done((bf16[144,2304]{1,0:T(8,128)(2,1)}, bf16[144,2304]{1,0:T(8,128)(2,1)S(1)}, u32[]{:S(2)}, u32[]{:S(2)}) %collective-permute-start.54) | collective-permute-done | bytes 663584 | tf_op jit(solution)/shard_map/ppermute | solution.py:446
  267.9 13.7 %collective-permute-done.56.refs_1_ = bf16[144,2304]{1,0:T(8,128)(2,1)S(1)} collective-permute-done((bf16[144,2304]{1,0:T(8,128)(2,1)}, bf16[144,2304]{1,0:T(8,128)(2,1)S(1)}, u32[]{:S(2)}, u32[]{:S(2)}) %collective-permute-start.56) | collective-permute-done | bytes 663584 | tf_op jit(solution)/shard_map/ppermute | solution.py:446
  282.1 13.3 %collective-permute-done.52.refs_1_ = bf16[144,2304]{1,0:T(8,128)(2,1)S(1)} collective-permute-done((bf16[144,2304]{1,0:T(8,128)(2,1)S(1)}, bf16[144,2304]{1,0:T(8,128)(2,1)S(1)}, u32[]{:S(2)}, u32[]{:S(2)}) %collective-permute-start.52) | collective-permute-done | bytes 663584 | tf_op jit(solution)/shard_map/ppermute | solution.py:446
  295.9 2.6 collective-permute-start.57
  301.7 25.2 %collective-permute-done.55.refs_1_ = bf16[72,2304]{1,0:T(8,128)(2,1)S(1)} collective-permute-done((bf16[72,2304]{1,0:T(8,128)(2,1)S(1)}, bf16[72,2304]{1,0:T(8,128)(2,1)S(1)}, u32[]{:S(2)}, u32[]{:S(2)}) %collective-permute-start.55) | collective-permute-done | bytes 331808 | tf_op jit(solution)/shard_map/ppermute | solution.py:440
  327.7 6.2 %collective-permute-done.57.refs_1_ = bf16[72,2304]{1,0:T(8,128)(2,1)S(1)} collective-permute-done((bf16[72,2304]{1,0:T(8,128)(2,1)S(1)}, bf16[72,2304]{1,0:T(8,128)(2,1)S(1)}, u32[]{:S(2)}, u32[]{:S(2)}) %collective-permute-start.57) | collective-permute-done | bytes 331808 | tf_op jit(solution)/shard_map/ppermute | solution.py:440
  334.8 6.1 %collective-permute-done.53.refs_1_ = bf16[72,2304]{1,0:T(8,128)(2,1)S(1)} collective-permute-done((bf16[72,2304]{1,0:T(8,128)(2,1)S(1)}, bf16[72,2304]{1,0:T(8,128)(2,1)S(1)}, u32[]{:S(2)}, u32[]{:S(2)}) %collective-permute-start.53) | collective-permute-done | bytes 331808 | tf_op jit(solution)/shard_map/ppermute | solution.py:440
  (439 shorter events, 142.7 us)
Async XLA Ops:
  9.1 16.5 %collective-permute-start = (bf16[48,1280]{1,0:T(8,128)(2,1)S(1)}, bf16[48,1280]{1,0:T(8,128)(2,1)S(1)}, u32[]{:S(2)}, u32[]{:S(2)}) collective-permute-start(bf16[48,1280]{1,0:T(8,128)(2,1)S(1)} %get-tuple-element.335), channel_id=1, source_target_pairs={{0,0},{2,2},{4,8},{6,10},{8,4},{10,6},{12,12},{14,14},{16,16},{18,... | collective-permute-start | bytes 368648 | tf_op jit(solution)/shard_map/ppermute | solution.py:462
  53.3 25.1 %collective-permute-start.15 = (bf16[96,5248]{1,0:T(8,128)(2,1)S(1)}, bf16[96,5248]{1,0:T(8,128)(2,1)S(1)}, u32[]{:S(2)}, u32[]{:S(2)}) collective-permute-start(bf16[96,5248]{1,0:T(8,128)(2,1)S(1)} %get-tuple-element.267.refs_0_), channel_id=1, source_target_pairs={{0,2},{2,0},{4,6},{6,4},{1,3},{3,1},{5,7},{7,5},{8,10},{10,8},{12,... | collective-permute-start | bytes 3022856 | tf_op jit(solution)/shard_map/ppermute | solution.py:437
  58.9 34.8 %collective-permute-start.14 = (bf16[128,2944]{1,0:T(8,128)(2,1)S(1)}, bf16[128,2944]{1,0:T(8,128)(2,1)S(1)}, u32[]{:S(2)}, u32[]{:S(2)}) collective-permute-start(bf16[128,2944]{1,0:T(8,128)(2,1)S(1)} %get-tuple-element.228.refs_0_), channel_id=1, source_target_pairs={{0,2},{2,0},{4,6},{6,4},{1,3},{3,1},{5,7},{7,5},{8,10},{10,8},{12,... | collective-permute-start | bytes 2261000 | tf_op jit(solution)/shard_map/ppermute | solution.py:437
  74.2 28.9 %collective-permute-start.17 = (bf16[128,2944]{1,0:T(8,128)(2,1)S(1)}, bf16[128,2944]{1,0:T(8,128)(2,1)S(1)}, u32[]{:S(2)}, u32[]{:S(2)}) collective-permute-start(bf16[128,2944]{1,0:T(8,128)(2,1)S(1)} %get-tuple-element.228.refs_0_), channel_id=1, source_target_pairs={{0,8},{8,0},{16,24},{24,16},{1,9},{9,1},{17,25},{25,17},{2,10},{10... | collective-permute-start | bytes 2261000 | tf_op jit(solution)/shard_map/ppermute | solution.py:434
  96.0 32.6 %collective-permute-start.25 = (bf16[96,5248]{1,0:T(8,128)(2,1)S(1)}, bf16[96,5248]{1,0:T(8,128)(2,1)S(1)}, u32[]{:S(2)}, u32[]{:S(2)}) collective-permute-start(bf16[96,5248]{1,0:T(8,128)(2,1)S(1)} %collective-permute-done.15.refs_1_), channel_id=1, source_target_pairs={{0,8},{8,0},{16,24},{24,16},{1,9},{9,1},{17,25},{25,17},{2,10},{10... | collective-permute-start | bytes 3022856 | tf_op jit(solution)/shard_map/ppermute | solution.py:434
  103.2 25.4 %collective-permute-start.20 = (bf16[128,3456]{1,0:T(8,128)(2,1)}, bf16[128,3456]{1,0:T(8,128)(2,1)}, u32[]{:S(2)}, u32[]{:S(2)}) collective-permute-start(bf16[128,3456]{1,0:T(8,128)(2,1)} %get-tuple-element.232.refs_4_.refs_0_), channel_id=1, source_target_pairs={{0,2},{2,0},{4,6},{6,4},{1,3},{3,1},{5,7},{7,5},{8,10},{10,8},{12,... | collective-permute-start | bytes 2654216 | tf_op jit(solution)/shard_map/ppermute | solution.py:437
  106.4 23.3 %collective-permute-start.19 = (bf16[128,1152]{1,0:T(8,128)(2,1)S(1)}, bf16[128,1152]{1,0:T(8,128)(2,1)S(1)}, u32[]{:S(2)}, u32[]{:S(2)}) collective-permute-start(bf16[128,1152]{1,0:T(8,128)(2,1)S(1)} %get-tuple-element.209.refs_0_), channel_id=1, source_target_pairs={{0,1},{1,0},{2,3},{3,2},{4,5},{5,4},{6,7},{7,6},{8,9},{9,8},{10,11... | collective-permute-start | bytes 884744 | tf_op jit(solution)/shard_map/ppermute | solution.py:443
  109.9 18.7 %collective-permute-start.23 = (bf16[64,1152]{1,0:T(8,128)(2,1)S(1)}, bf16[64,1152]{1,0:T(8,128)(2,1)S(1)}, u32[]{:S(2)}, u32[]{:S(2)}) collective-permute-start(bf16[64,1152]{1,0:T(8,128)(2,1)S(1)} %get-tuple-element.330), channel_id=1, source_target_pairs={{2,0},{0,2},{10,4},{8,6},{6,8},{4,10},{14,12},{12,14},{18,16},{16,... | collective-permute-start | bytes 442376 | tf_op jit(solution)/shard_map/ppermute | solution.py:468
  110.6 29.8 %collective-permute-start.26 = (bf16[128,3456]{1,0:T(8,128)(2,1)}, bf16[128,3456]{1,0:T(8,128)(2,1)}, u32[]{:S(2)}, u32[]{:S(2)}) collective-permute-start(bf16[128,3456]{1,0:T(8,128)(2,1)} %get-tuple-element.232.refs_4_.refs_0_), channel_id=1, source_target_pairs={{0,8},{8,0},{16,24},{24,16},{1,9},{9,1},{17,25},{25,17},{2,10},{10... | collective-permute-start | bytes 2654216 | tf_op jit(solution)/shard_map/ppermute | solution.py:434
  132.6 17.9 %collective-permute-start.29 = (bf16[128,2304]{1,0:T(8,128)(2,1)}, bf16[128,2304]{1,0:T(8,128)(2,1)}, u32[]{:S(2)}, u32[]{:S(2)}) collective-permute-start(bf16[128,2304]{1,0:T(8,128)(2,1)} %get-tuple-element.249.refs_4_), channel_id=1, source_target_pairs={{0,2},{2,0},{4,6},{6,4},{1,3},{3,1},{5,7},{7,5},{8,10},{10,8},{12,... | collective-permute-start | bytes 1769480 | tf_op jit(solution)/shard_map/ppermute | solution.py:437
  146.8 20.4 %collective-permute-start.31 = (bf16[128,2304]{1,0:T(8,128)(2,1)}, bf16[128,2304]{1,0:T(8,128)(2,1)}, u32[]{:S(2)}, u32[]{:S(2)}) collective-permute-start(bf16[128,2304]{1,0:T(8,128)(2,1)} %get-tuple-element.249.refs_4_), channel_id=1, source_target_pairs={{0,8},{8,0},{16,24},{24,16},{1,9},{9,1},{17,25},{25,17},{2,10},{10... | collective-permute-start | bytes 1769480 | tf_op jit(solution)/shard_map/ppermute | solution.py:434
  152.7 16.3 %collective-permute-start.32 = (bf16[128,2304]{1,0:T(8,128)(2,1)}, bf16[128,2304]{1,0:T(8,128)(2,1)}, u32[]{:S(2)}, u32[]{:S(2)}) collective-permute-start(bf16[128,2304]{1,0:T(8,128)(2,1)} %collective-permute-done.29.refs_5_), channel_id=1, source_target_pairs={{0,8},{8,0},{16,24},{24,16},{1,9},{9,1},{17,25},{25,17},{2,10},{10... | collective-permute-start | bytes 1769480 | tf_op jit(solution)/shard_map/ppermute | solution.py:434
  152.7 29.2 %collective-permute-start.35 = (bf16[128,2944]{1,0:T(8,128)(2,1)}, bf16[128,2944]{1,0:T(8,128)(2,1)}, u32[]{:S(2)}, u32[]{:S(2)}) collective-permute-start(bf16[128,2944]{1,0:T(8,128)(2,1)} %get-tuple-element.274.refs_4_), channel_id=1, source_target_pairs={{0,2},{2,0},{4,6},{6,4},{1,3},{3,1},{5,7},{7,5},{8,10},{10,8},{12,... | collective-permute-start | bytes 2261000 | tf_op jit(solution)/shard_map/ppermute | solution.py:437
  154.4 27.6 %collective-permute-start.34 = (bf16[144,2304]{1,0:T(8,128)(2,1)}, bf16[144,2304]{1,0:T(8,128)(2,1)}, u32[]{:S(2)}, u32[]{:S(2)}) collective-permute-start(bf16[144,2304]{1,0:T(8,128)(2,1)} %get-tuple-element.236), channel_id=1, source_target_pairs={{0,16},{8,24},{16,0},{24,8},{1,17},{9,25},{17,1},{25,9},{2,18},{10... | collective-permute-start | bytes 1990664 | tf_op jit(solution)/shard_map/ppermute | solution.py:446
  167.2 19.5 %collective-permute-start.44 = (bf16[4,1152]{1,0:T(4,128)(2,1)S(1)}, bf16[4,1152]{1,0:T(4,128)(2,1)S(1)}, u32[]{:S(2)}, u32[]{:S(2)}) collective-permute-start(bf16[4,1152]{1,0:T(4,128)(2,1)S(1)} %copy-done.102), channel_id=1, source_target_pairs={{0,16},{8,24},{16,0},{24,8},{1,17},{9,25},{17,1},{25,9},{2,18},{10... | collective-permute-start | bytes 27656 | tf_op jit(solution)/shard_map/ppermute | solution.py:446
  198.1 22.4 %collective-permute-start.47 = (bf16[96,3456]{1,0:T(8,128)(2,1)}, bf16[96,3456]{1,0:T(8,128)(2,1)}, u32[]{:S(2)}, u32[]{:S(2)}) collective-permute-start(bf16[96,3456]{1,0:T(8,128)(2,1)} %copy-done.23), channel_id=1, source_target_pairs={{0,8},{8,0},{16,24},{24,16},{1,9},{9,1},{17,25},{25,17},{2,10},{10... | collective-permute-start | bytes 1990664 | tf_op jit(solution)/shard_map/ppermute | solution.py:434
  202.2 21.1 %collective-permute-start.45 = (bf16[144,2304]{1,0:T(8,128)(2,1)}, bf16[144,2304]{1,0:T(8,128)(2,1)}, u32[]{:S(2)}, u32[]{:S(2)}) collective-permute-start(bf16[144,2304]{1,0:T(8,128)(2,1)} %get-tuple-element.253), channel_id=1, source_target_pairs={{0,16},{8,24},{16,0},{24,8},{1,17},{9,25},{17,1},{25,9},{2,18},{10... | collective-permute-start | bytes 1990664 | tf_op jit(solution)/shard_map/ppermute | solution.py:446
  202.8 17.6 %collective-permute-start.43 = (f32[4,2016]{1,0:T(4,128)S(1)}, f32[4,2016]{1,0:T(4,128)S(1)}, u32[]{:S(2)}, u32[]{:S(2)}) collective-permute-start(f32[4,2016]{1,0:T(4,128)S(1)} %reshape.235), channel_id=1, source_target_pairs={{0,16},{8,24},{16,0},{24,8},{1,17},{9,25},{17,1},{25,9},{2,18},{10... | collective-permute-start | bytes 96776 | tf_op jit(solution)/shard_map/ppermute | solution.py:446
  213.4 20.4 %collective-permute-start.49 = (bf16[96,2944]{1,0:T(8,128)(2,1)}, bf16[96,2944]{1,0:T(8,128)(2,1)}, u32[]{:S(2)}, u32[]{:S(2)}) collective-permute-start(bf16[96,2944]{1,0:T(8,128)(2,1)} %get-tuple-element.271.refs_4_), channel_id=1, source_target_pairs={{0,2},{2,0},{4,6},{6,4},{1,3},{3,1},{5,7},{7,5},{8,10},{10,8},{12,... | collective-permute-start | bytes 1695752 | tf_op jit(solution)/shard_map/ppermute | solution.py:437
  220.4 17.5 %collective-permute-start.50 = (bf16[96,2944]{1,0:T(8,128)(2,1)}, bf16[96,2944]{1,0:T(8,128)(2,1)}, u32[]{:S(2)}, u32[]{:S(2)}) collective-permute-start(bf16[96,2944]{1,0:T(8,128)(2,1)} %get-tuple-element.271.refs_4_), channel_id=1, source_target_pairs={{0,8},{8,0},{16,24},{24,16},{1,9},{9,1},{17,25},{25,17},{2,10},{10... | collective-permute-start | bytes 1695752 | tf_op jit(solution)/shard_map/ppermute | solution.py:434
  220.5 25.4 %collective-permute-start.61 = (bf16[72,2304]{1,0:T(8,128)(2,1)}, bf16[72,2304]{1,0:T(8,128)(2,1)}, u32[]{:S(2)}, u32[]{:S(2)}) collective-permute-start(bf16[72,2304]{1,0:T(8,128)(2,1)} %get-tuple-element.260), channel_id=1, source_target_pairs={{0,4},{2,6},{4,0},{6,2},{1,5},{3,7},{5,1},{7,3},{8,12},{10,14},{12... | collective-permute-start | bytes 995336 | tf_op jit(solution)/shard_map/ppermute | solution.py:440
  235.2 17.9 %collective-permute-start.58 = (bf16[144,2304]{1,0:T(8,128)(2,1)}, bf16[144,2304]{1,0:T(8,128)(2,1)S(1)}, u32[]{:S(2)}, u32[]{:S(2)}) collective-permute-start(bf16[144,2304]{1,0:T(8,128)(2,1)} %copy-done.91), channel_id=1, source_target_pairs={{0,16},{8,24},{16,0},{24,8},{1,17},{9,25},{17,1},{25,9},{2,18},{10... | collective-permute-start | bytes 1990664 | tf_op jit(solution)/shard_map/ppermute | solution.py:446
  236.5 30.9 %collective-permute-start.54 = (bf16[144,2304]{1,0:T(8,128)(2,1)}, bf16[144,2304]{1,0:T(8,128)(2,1)S(1)}, u32[]{:S(2)}, u32[]{:S(2)}) collective-permute-start(bf16[144,2304]{1,0:T(8,128)(2,1)} %copy-done.93), channel_id=1, source_target_pairs={{0,16},{8,24},{16,0},{24,8},{1,17},{9,25},{17,1},{25,9},{2,18},{10... | collective-permute-start | bytes 1990664 | tf_op jit(solution)/shard_map/ppermute | solution.py:446
  237.9 43.7 %collective-permute-start.56 = (bf16[144,2304]{1,0:T(8,128)(2,1)}, bf16[144,2304]{1,0:T(8,128)(2,1)S(1)}, u32[]{:S(2)}, u32[]{:S(2)}) collective-permute-start(bf16[144,2304]{1,0:T(8,128)(2,1)} %copy-done.92), channel_id=1, source_target_pairs={{0,16},{8,24},{16,0},{24,8},{1,17},{9,25},{17,1},{25,9},{2,18},{10... | collective-permute-start | bytes 1990664 | tf_op jit(solution)/shard_map/ppermute | solution.py:446
  244.3 51.1 %collective-permute-start.52 = (bf16[144,2304]{1,0:T(8,128)(2,1)S(1)}, bf16[144,2304]{1,0:T(8,128)(2,1)S(1)}, u32[]{:S(2)}, u32[]{:S(2)}) collective-permute-start(bf16[144,2304]{1,0:T(8,128)(2,1)S(1)} %get-tuple-element.290), channel_id=1, source_target_pairs={{0,16},{8,24},{16,0},{24,8},{1,17},{9,25},{17,1},{25,9},{2,18},{10... | collective-permute-start | bytes 1990664 | tf_op jit(solution)/shard_map/ppermute | solution.py:446
  245.9 50.0 %collective-permute-start.38 = (f32[48,1152]{1,0:T(8,128)S(1)}, f32[48,1152]{1,0:T(8,128)S(1)}, u32[]{:S(2)}, u32[]{:S(2)}) collective-permute-start(f32[48,1152]{1,0:T(8,128)S(1)} %get-tuple-element.326), channel_id=1, source_target_pairs={{0,0},{2,2},{8,4},{10,6},{4,8},{6,10},{12,12},{14,14},{16,16},{18,... | collective-permute-start | bytes 663560 | tf_op jit(solution)/shard_map/ppermute | solution.py:468
  253.2 45.4 %collective-permute-start.39 = (f32[48,1152]{1,0:T(8,128)S(1)}, f32[48,1152]{1,0:T(8,128)S(1)}, u32[]{:S(2)}, u32[]{:S(2)}) collective-permute-start(f32[48,1152]{1,0:T(8,128)S(1)} %get-tuple-element.327), channel_id=1, source_target_pairs={{2,0},{0,2},{10,4},{8,6},{6,8},{4,10},{14,12},{12,14},{18,16},{16,... | collective-permute-start | bytes 663560 | tf_op jit(solution)/shard_map/ppermute | solution.py:468
  267.4 32.4 %collective-permute-start.60 = (bf16[72,2304]{1,0:T(8,128)(2,1)S(1)}, bf16[72,2304]{1,0:T(8,128)(2,1)S(1)}, u32[]{:S(2)}, u32[]{:S(2)}) collective-permute-start(bf16[72,2304]{1,0:T(8,128)(2,1)S(1)} %copy-done.95), channel_id=1, source_target_pairs={{0,4},{2,6},{4,0},{6,2},{1,5},{3,7},{5,1},{7,3},{8,12},{10,14},{12... | collective-permute-start | bytes 995336 | tf_op jit(solution)/shard_map/ppermute | solution.py:440
  281.6 19.1 %collective-permute-start.59 = (bf16[72,2304]{1,0:T(8,128)(2,1)S(1)}, bf16[72,2304]{1,0:T(8,128)(2,1)S(1)}, u32[]{:S(2)}, u32[]{:S(2)}) collective-permute-start(bf16[72,2304]{1,0:T(8,128)(2,1)S(1)} %get-tuple-element.304), channel_id=1, source_target_pairs={{0,4},{2,6},{4,0},{6,2},{1,5},{3,7},{5,1},{7,3},{8,12},{10,14},{12... | collective-permute-start | bytes 995336 | tf_op jit(solution)/shard_map/ppermute | solution.py:440
  295.4 31.4 %collective-permute-start.55 = (bf16[72,2304]{1,0:T(8,128)(2,1)S(1)}, bf16[72,2304]{1,0:T(8,128)(2,1)S(1)}, u32[]{:S(2)}, u32[]{:S(2)}) collective-permute-start(bf16[72,2304]{1,0:T(8,128)(2,1)S(1)} %get-tuple-element.297), channel_id=1, source_target_pairs={{0,4},{2,6},{4,0},{6,2},{1,5},{3,7},{5,1},{7,3},{8,12},{10,14},{12... | collective-permute-start | bytes 995336 | tf_op jit(solution)/shard_map/ppermute | solution.py:440
  295.9 38.0 %collective-permute-start.57 = (bf16[72,2304]{1,0:T(8,128)(2,1)S(1)}, bf16[72,2304]{1,0:T(8,128)(2,1)S(1)}, u32[]{:S(2)}, u32[]{:S(2)}) collective-permute-start(bf16[72,2304]{1,0:T(8,128)(2,1)S(1)} %get-tuple-element.300), channel_id=1, source_target_pairs={{0,4},{2,6},{4,0},{6,2},{1,5},{3,7},{5,1},{7,3},{8,12},{10,14},{12... | collective-permute-start | bytes 995336 | tf_op jit(solution)/shard_map/ppermute | solution.py:440
  298.5 42.4 %collective-permute-start.53 = (bf16[72,2304]{1,0:T(8,128)(2,1)S(1)}, bf16[72,2304]{1,0:T(8,128)(2,1)S(1)}, u32[]{:S(2)}, u32[]{:S(2)}) collective-permute-start(bf16[72,2304]{1,0:T(8,128)(2,1)S(1)} %get-tuple-element.292), channel_id=1, source_target_pairs={{0,4},{2,6},{4,0},{6,2},{1,5},{3,7},{5,1},{7,3},{8,12},{10,14},{12... | collective-permute-start | bytes 995336 | tf_op jit(solution)/shard_map/ppermute | solution.py:440
  (137 other events, 868.8 us)
where the time goes:
time: 347 us; the launch traced here: 342 us
  waiting for transfers between devices  143 us (41%)
  Pallas kernels  72.9 us (21%)
  starting transfers between devices  67.2 us (19%)
  local copies, waits for them, and re-layouts  44.5 us (13%)
  other arithmetic  7.4 us (2%)
  matrix products  4.03 us (1%)
    pallas_call x27, Pallas kernels, call(): pl.pallas_call(body, out_shape=shapes, in_specs=[hbm if i in late else vm...  50.3 us
    ppermute x8, waiting for transfers between devices, to_hi(): return lax.ppermute(a, 'dp', [(d, d ^ 2) for d in range(self.ndp)])  50 us
    ppermute x8, waiting for transfers between devices, to_far(): return lax.ppermute(a, 'region', self.far)  42.9 us
    unnamed x229, local copies, waits for them, and re-layouts  42 us
    ppermute x9, waiting for transfers between devices, to_near(): return lax.ppermute(a, 'region', self.near)  24.4 us
    ppermute x20, starting transfers between devices, to_core(): return lax.ppermute(a, 'dp', self.core_perm)  20.2 us
    pallas_call x6, Pallas kernels, weight_grads(): pl.pallas_call(functools.partial(weight_grad_kernel, products), out_shape...  18.7 us
    ppermute x9, waiting for transfers between devices, to_heads(): return lax.ppermute(a, 'heads', [(0, 1), (1, 0)])  18.6 us
  transfers between devices with their start and end apart: 62, of which 29 were waited for; matrix products, arithmetic and copies ran while one was open for 3% of the time, Pallas kernels for 19%

commit v1 on v0

--- a/solution.py
+++ b/solution.py
@@ -13,7 +13,7 @@
 EPSILON = 1e-06
 BF16 = jnp.bfloat16
 F32 = jnp.float32
-VMEM_LIMIT = 28 * 2**20
+VMEM_LIMIT = 16 * 2**20
 NT = ((1,), (1,))
 TN = ((0,), (0,))
 
@@ -40,7 +40,6 @@
 
 def call(kernel, outs, *ins, flops=0, scratch=(), late=(), limit=VMEM_LIMIT):
     shapes = [jax.ShapeDtypeStruct(shape, dtype) for shape, dtype in outs]
-    moved = sum(math.prod(a.shape) * a.dtype.itemsize for a in list(ins) + shapes)
     fetched = [pltpu.VMEM(ins[i].shape, ins[i].dtype) for i in late]
     semaphores = [pltpu.SemaphoreType.DMA((len(late),))] if late else []
 
@@ -54,15 +53,21 @@
             refs[i].get()
 
     vmem, hbm = pl.BlockSpec(memory_space=pltpu.VMEM), pl.BlockSpec(memory_space=pl.ANY)
+    ins = [in_hbm(a) if i in late else a for i, a in enumerate(ins)]
     return pl.pallas_call(
         body,
         out_shape=shapes,
         in_specs=[hbm if i in late else vmem for i in range(len(ins))],
         out_specs=[vmem] * len(outs),
+        name=kernel.__name__,
         scratch_shapes=list(scratch) + fetched + semaphores,
         compiler_params=pltpu.CompilerParams(vmem_limit_bytes=limit),
         cost_estimate=pl.CostEstimate(flops=flops, bytes_accessed=0, transcendentals=0),
     )(*ins)
+
+
+def in_hbm(a):
+    return pltpu.with_memory_space_constraint(a, pltpu.HBM)
 
 
 def load_kernel(*refs):
@@ -76,20 +81,23 @@
         copy.wait()
 
 
-def load(anchor, *weights):
-    anchor, *weights = tie(anchor, *weights)
+def load(anchor, *weights, beside=()):
+    anchor, *weights = tie(anchor, *weights, *beside)
+    weights, beside = weights[: len(weights) - len(beside)], weights[len(weights) - len(beside) :]
+    weights = [in_hbm(w) for w in weights]
     loaded = pl.pallas_call(
         load_kernel,
         out_shape=[jax.ShapeDtypeStruct(w.shape, w.dtype) for w in weights],
         in_specs=[pl.BlockSpec(memory_space=pl.ANY)] * len(weights),
         out_specs=[pl.BlockSpec(memory_space=pltpu.VMEM)] * len(weights),
+        name="load",
         scratch_shapes=[pltpu.SemaphoreType.DMA((len(weights),))],
         compiler_params=pltpu.CompilerParams(vmem_limit_bytes=VMEM_LIMIT),
         cost_estimate=pl.CostEstimate(
-            flops=3*10**9, bytes_accessed=0, transcendentals=0
+            flops=3 * 10**9, bytes_accessed=0, transcendentals=0
         ),
     )(*weights)
-    return anchor, *loaded
+    return anchor, *loaded, *beside
 
 
 def tie(*arrays):
@@ -136,7 +144,7 @@
     width = q_ref.shape[1]
     hidden = (norm(x)[0] * (1.0 + row(mod, 1)) + row(mod, 0)).astype(BF16)
     hidden_ref[...] = hidden
-    projected = dot(hidden, qkv[...], NT).astype(BF16)
+    projected = dot(hidden, here(qkv)[...], NT).astype(BF16)
     q_ref[...] = projected[:, :width]
     kv_ref[:, : 2 * width] = projected[:, width:]
 
@@ -317,36 +325,32 @@
     part_ref[...] = dot(grad_projected, here(qkv)[...]).astype(BF16)
 
 
-def block_back(part, other, grad_residual, x, mod, grad_out, mlp, mlp_other, sums_ref):
+def block_back(part, other, grad_residual, x, mod, sums_ref):
     grad_hidden = wide(part) + wide(other)
     normed, inverse = norm(here(x)[...])
     sums_ref[0:1, :] = jnp.sum(grad_hidden, axis=0, keepdims=True)
     sums_ref[1:2, :] = jnp.sum(grad_hidden * normed, axis=0, keepdims=True)
-    sums_ref[2:3, :] = jnp.sum(wide(grad_out) * (wide(mlp) + wide(mlp_other)), axis=0, keepdims=True)
-    return grad_residual[...] + norm_back(grad_hidden * (1.0 + row(mod, 1)), normed, inverse)
-
-
-def dec_end_kernel(
-    part, other, grad_residual, x, mod, grad_out, mlp, mlp_other, matches, grad_ref, sums_ref
-):
-    grad_x = block_back(part, other, grad_residual, x, mod, grad_out, mlp, mlp_other, sums_ref)
+    return here(grad_residual)[...] + norm_back(grad_hidden * (1.0 + row(mod, 1)), normed, inverse)
+
+
+def dec_end_kernel(part, other, grad_residual, x, mod, matches, grad_ref, sums_ref):
+    grad_x = block_back(part, other, grad_residual, x, mod, sums_ref)
     found = matches[...]
     uncovered = 1.0 - jnp.sum(found, axis=1, keepdims=True)
-    sums_ref[3:4, :] = jnp.sum(uncovered * grad_x, axis=0, keepdims=True)
+    sums_ref[2:3, :] = jnp.sum(uncovered * grad_x, axis=0, keepdims=True)
     grad_ref[...] = dot(found, grad_x, TN, precision=lax.Precision.HIGHEST)
 
 
 def enc_end_kernel(
     part, other, grad_residual, x, mod, grad_out, mlp, mlp_other, grad_ref, sums_ref
 ):
-    grad_ref[...] = block_back(
-        part, other, grad_residual, x, mod, grad_out, mlp, mlp_other, sums_ref
-    )
-    sums_ref[3:4, :] = jnp.zeros_like(sums_ref[3:4, :])
-
-
-def out_kernel(residual, part, other, mod, out_ref):
-    out_ref[...] = block_end(residual, part, other, mod).astype(BF16)
+    grad_ref[...] = block_back(part, other, grad_residual, x, mod, sums_ref).astype(BF16)
+    sums_ref[2:3, :] = jnp.sum(wide(grad_out) * (wide(mlp) + wide(mlp_other)), axis=0, keepdims=True)
+
+
+def out_kernel(residual, part, other, mod, grad_out, out_ref, sums_ref):
+    out_ref[...] = block_end(here(residual), here(part), other, mod).astype(BF16)
+    sums_ref[...] = jnp.sum(wide(grad_out) * (wide(part) + wide(other)), axis=0, keepdims=True)
 
 
 def weight_grad_kernel(products, *refs):
@@ -387,12 +391,13 @@
 
 def halve_kernel(kept, got, sent_ref, kept_ref):
     rows = kept_ref.shape[0]
-    sums = kept[...] + wide(got)
+    sums = here(kept)[...] + wide(got)
     kept_ref[...] = sums[:rows]
     sent_ref[...] = sums[rows:].astype(BF16)
 
 
 def finish_kernel(kept, got, *outs):
+    kept = here(kept)
     at = 0
     for out in outs:
         for part in range(out.shape[0] if len(out.shape) == 3 else 1):
@@ -431,19 +436,24 @@
         self.y = lax.axis_index("heads")
 
     def to_core(self, a):
-        return lax.ppermute(a, "dp", self.core_perm)
+        with jax.named_scope("core"):
+            return lax.ppermute(a, "dp", self.core_perm)
 
     def to_near(self, a):
-        return lax.ppermute(a, "region", self.near)
+        with jax.named_scope("near"):
+            return lax.ppermute(a, "region", self.near)
 
     def to_far(self, a):
-        return lax.ppermute(a, "region", self.far)
+        with jax.named_scope("far"):
+            return lax.ppermute(a, "region", self.far)
 
     def to_heads(self, a):
-        return lax.ppermute(a, "heads", [(0, 1), (1, 0)])
+        with jax.named_scope("heads"):
+            return lax.ppermute(a, "heads", [(0, 1), (1, 0)])
 
     def to_hi(self, a):
-        return lax.ppermute(a, "dp", [(d, d ^ 2) for d in range(self.ndp)])
+        with jax.named_scope("hi"):
+            return lax.ppermute(a, "dp", [(d, d ^ 2) for d in range(self.ndp)])
 
     def hi_groups(self):
         return [[c + 2 * h for h in range(self.nhi)] for c in range(2)]
@@ -458,13 +468,15 @@
     def spread_images(self, a):
         even = self.z0 == 0
         first, second = jnp.where(even, a[0], a[1]), jnp.where(even, a[1], a[0])
-        return [
+        with jax.named_scope("spread"):
+          return [
             lax.ppermute(part, ("dp", "region"), perm)
             for part, perm in zip((first, second), self.spread)
         ]
 
     def collect_parts(self, parts):
-        return [
+        with jax.named_scope("collect"):
+          return [
             lax.ppermute(part, ("dp", "region"), [(t, s) for s, t in perm])
             for part, perm in zip(parts, self.spread)
         ]
@@ -473,9 +485,11 @@
         even = self.z0 == 0
         return jnp.stack([jnp.where(even, back[0], back[1]), jnp.where(even, back[1], back[0])])
 
-    def gather(self, rows):
+    def gather(self, rows, along_dp):
+        if not along_dp:
+            return rows, self.to_near(rows)
         if self.nhi == 2:
-            return rows, self.to_near(rows)
+            return rows, self.to_hi(rows)
         if self.nhi > 2:
             rows = lax.all_gather(
                 rows, "dp", axis_index_groups=self.hi_groups(), axis=0, tiled=True
@@ -483,18 +497,15 @@
         half = rows.shape[0] // 2
         return rows[:half], rows[half:]
 
-    def selection(self, features):
+    def selection(self, features, along_dp):
         own = features // (self.ndp * 4)
         step = jnp.arange(4 * own)
-        if self.nhi == 2:
-            block = jnp.array([8, 10, 0, 2])[step // own]
-        else:
-            block = jnp.array([1, 3, 0, 2])[step // own]
+        block = jnp.array([1, 3, 0, 2] if along_dp else [8, 10, 0, 2])[step // own]
         feature = ((self.dp * 4 + self.z) ^ block) * own + step % own
         return (feature[:, None] == jnp.arange(features)[None, :]).astype(BF16)
 
-    def first_half(self, sent):
-        return self.to_hi(sent) if self.nhi == 2 else self.to_near(sent)
+    def first_half(self, sent, along_dp):
+        return self.to_near(sent) if along_dp else self.to_hi(sent)
 
 
 def weight_grads(products, bundles, select):
@@ -502,7 +513,7 @@
     features = select.shape[1]
     width = sum(full[2] for _, full in products)
     rows = 4 * bundles[0][0].shape[0]
-    operands = [a for bundle in bundles for a in bundle]
+    operands = [in_hbm(a) for bundle in bundles for a in bundle]
     vmem, hbm = pl.BlockSpec(memory_space=pltpu.VMEM), pl.BlockSpec(memory_space=pl.ANY)
     buffers = [
         pltpu.VMEM((rows, padded(span)), BF16)
@@ -517,10 +528,11 @@
         ],
         in_specs=[hbm] * len(operands) + [vmem],
         out_specs=[vmem] * 2,
+        name="weight_grads",
         scratch_shapes=buffers + [pltpu.SemaphoreType.DMA((8 * len(products),))],
         compiler_params=pltpu.CompilerParams(vmem_limit_bytes=max(VMEM_LIMIT, held)),
         cost_estimate=pl.CostEstimate(
-            flops=4 * half * rows * (width + len(products) * features),
+            flops=0,
             bytes_accessed=0,
             transcendentals=0,
         ),
@@ -545,7 +557,8 @@
     tokens = cotangent.shape[1]
     assert enc_in.shape[0] == 2
     width, units = enc_proj.shape[0], enc_up.shape[1]
-    select = net.selection(features)
+    dec_way, enc_way = True, net.nhi != 2
+    dec_select, enc_select = net.selection(features, dec_way), net.selection(features, enc_way)
     enc_qkv, dec_qkv = (
         jnp.transpose(a, (1, 2, 0)).reshape(3 * width, features) for a in (enc_qkv, dec_qkv)
     )
@@ -566,6 +579,7 @@
     block = enc_ada.shape[1]
     cols = cols.reshape(2, 2, 2 * block)
     got = net.to_near(lax.dynamic_index_in_dim(cols, 1 - net.z0, 1, False))
+    got, *slots = tie(got, *slots)
     cols = in_order(lax.dynamic_index_in_dim(cols, net.z0, 1, False), got, net.z0)
     got = net.to_far(lax.dynamic_index_in_dim(cols, 1 - net.z1, 1, False))
     cols = in_order(lax.dynamic_index_in_dim(cols, net.z1, 1, False), got, net.z1)
@@ -580,8 +594,8 @@
         return call(
             attention_kernel,
             [((rows, padded(width) + (1 + len(beside)) * features), BF16), ((rows, features), BF16)] + beside,
-            q, kv, kv_other, proj, hidden, *more, late=(3,),
-            flops=2 * rows * width * (features + 4 * rows), scratch=[pltpu.VMEM((rows, width), F32)],
+            q, kv, kv_other, proj, hidden, *more,
+            scratch=[pltpu.VMEM((rows, width), F32)],
         )
 
     def mlp(x, part, other, mod, up, down, *more):
@@ -590,7 +604,7 @@
         return call(
             mlp_kernel,
             [((rows, features), F32), ((rows, units), F32), ((rows, beside), BF16), ((rows, features), BF16)],
-            x, part, other, mod, up, down, *more, flops=4 * rows * features * units,
+            x, part, other, mod, up, down, *more,
         )
 
     def attention_back(grad_out, part, other, s, mod, proj):
@@ -603,7 +617,6 @@
             ],
             grad_out, part, other, s["residual"], s["branch"], s["branch_other"], mod, proj,
             s["q"], s["kv"], s["kv_other"], late=(3, 4, 5, 8, 9, 10),
-            flops=2 * rows * width * (features + 10 * rows),
             scratch=[pltpu.VMEM((2 * rows, width), F32)] * 2,
         )
 
@@ -611,23 +624,18 @@
         rows = dq.shape[0]
         return call(
             qkv_back_kernel, [((rows, padded(3 * width) + features), BF16), ((rows, features), BF16)],
-            dq, dkv, dkv_other, grad_branch, qkv, flops=6 * rows * features * width,
-        )
-
-    def end(kernel, grad_residual, part, other, grad_out, s, mod, *extra):
-        return call(
-            kernel, [((2 * cap, features), F32), ((4, features), F32)],
-            part, other, grad_residual, s["x"], mod, grad_out, s["mlp"], s["mlp_other"], *extra,
-            late=(3, 6, 7),
+            dq, dkv, dkv_other, grad_branch, qkv,
         )
 
     rows = 2 * cap
     x, hidden, q, kv = call(
         enc_qkv_kernel,
         [((rows, features), F32), ((rows, features), BF16), ((rows, width), BF16), ((rows, 2 * width + 128), BF16)],
-        *slots, enc_mod, enc_qkv, flops=6 * rows * features * width,
-    )
+        *slots, enc_mod, enc_qkv, late=(3,),
+    )
+    cotangent, kv = tie(cotangent, kv)
     kv_other = net.to_core(kv)
+    grad_parts = net.spread_images(cotangent)
     enc_attn_rows, branch = attention(q, kv, kv_other, enc_proj, hidden)
     branch, up, down = load(branch, enc_up, enc_down)
     branch_other = net.to_heads(branch)
@@ -640,147 +648,168 @@
         x=x, q=q, kv=kv, kv_other=kv_other, branch=branch, branch_other=branch_other,
         residual=residual, pre=pre, mlp=mlp_part, mlp_other=mlp_other,
     )
-    enc_rows, enc_rows_near = net.gather(enc_rows)
-    cotangent, _ = tie(cotangent, branch)
-    grad_parts = net.spread_images(cotangent)
+    enc_rows, enc_rows_far = net.gather(enc_rows, enc_way)
+    mlp_other, *grad_parts = tie(mlp_other, *grad_parts)
 
     rows = 2 * tokens
-    mlp_other, *grad_parts = tie(mlp_other, *grad_parts)
     x, hidden, q, kv = call(
         dec_qkv_kernel,
         [((rows, features), F32), ((rows, features), BF16), ((rows, width), BF16), ((rows, 2 * width), BF16)],
         residual, mlp_part, mlp_other, enc_mod, matches, mask_token[None], dec_mod, qkv,
-        flops=6 * rows * features * width,
     )
     kv_other = net.to_core(kv)
     attn_rows, branch, grad_out = attention(q, kv, kv_other, dec_proj, hidden, *grad_parts, dec_mod)
     branch, up, down = load(branch, dec_up, dec_down)
     branch_other = net.to_heads(branch)
     own_rows = attn_rows
-    attn_rows, attn_rows_near = net.gather(attn_rows)
+    attn_rows, attn_rows_far = net.gather(attn_rows, dec_way)
     residual, pre, mlp_rows, mlp_part = mlp(x, branch, branch_other, dec_mod, up, down)
-    mlp_other = net.to_heads(mlp_part)
     dec = dict(
         x=x, q=q, kv=kv, kv_other=kv_other, branch=branch, branch_other=branch_other,
-        residual=residual, pre=pre, mlp=mlp_part, mlp_other=mlp_other,
-    )
-    mlp_rows, mlp_rows_near = net.gather(mlp_rows)
-
+        residual=residual, pre=pre,
+    )
+    mlp_rows, mlp_rows_far = net.gather(mlp_rows, dec_way)
+
+    mlp_other = net.to_heads(mlp_part)
+    pre, enc_rows_far = tie(pre, enc_rows_far)
     grad_rows, part = call(
         dec_mlp_back_kernel, [((rows, units), BF16), ((rows, features), BF16)],
-        own_rows, pre, up, down, flops=4 * rows * features * units,
-    )
-    part, qkv, proj = load(part, dec_qkv, dec_proj)
+        own_rows, pre, up, down,
+    )
+    part, mlp_other = tie(part, mlp_other)
+    part, proj = load(part, dec_proj)
     other = net.to_heads(part)
-    (dec_out,) = call(
-        out_kernel, [((rows, features), BF16)], residual, mlp_part, mlp_other, dec_mod
+    grad_rows, grad_rows_far = net.gather(grad_rows, dec_way)
+    other, attn_rows_far = tie(other, attn_rows_far)
+    attn_rows = attn_rows, attn_rows_far, net.to_core(attn_rows), net.to_core(attn_rows_far)
+    dec_out, dec_gate = call(
+        out_kernel, [((rows, features), BF16), ((1, features), F32)],
+        residual, mlp_part, mlp_other, dec_mod, grad_out, late=(0, 1, 4),
     )
     out_parts = net.collect_parts([dec_out[:tokens], dec_out[tokens:]])
-    grad_rows, grad_rows_near = net.gather(grad_rows)
-    other, attn_rows_near, enc_rows_near = tie(other, attn_rows_near, enc_rows_near)
-    attn_rows = attn_rows, attn_rows_near, net.to_core(attn_rows), net.to_core(attn_rows_near)
     grad_residual, grad_branch, dq, dkv, dkv_other, dec_sums = attention_back(
         grad_out, part, other, dec, dec_mod, proj
     )
-    dkv_other, *attn_rows = tie(net.to_core(dkv_other), *attn_rows)
-    enc_rows = enc_rows, enc_rows_near, net.to_core(enc_rows), net.to_core(enc_rows_near)
+    dkv_other, qkv = load(dkv_other, dec_qkv)
+    dkv_other, mlp_rows_far, *rest = tie(
+        net.to_core(dkv_other), mlp_rows_far, *attn_rows, *out_parts
+    )
+    attn_rows, out_parts = rest[:4], rest[4:]
+    mlp_rows = mlp_rows, mlp_rows_far, net.to_core(mlp_rows), net.to_core(mlp_rows_far)
+    enc_rows = enc_rows, enc_rows_far, net.to_core(enc_rows), net.to_core(enc_rows_far)
     grad_attn_rows, part = qkv_back(dq, dkv, dkv_other, grad_branch, qkv)
     part, up, down = load(part, enc_up, enc_down)
     other = net.to_heads(part)
-    grad_attn_rows, grad_attn_rows_near = net.gather(grad_attn_rows)
-    other, mlp_rows_near, *rest = tie(other, mlp_rows_near, *out_parts, *enc_rows)
-    out_parts, enc_rows = rest[:2], rest[2:]
-    mlp_rows = mlp_rows, mlp_rows_near, net.to_core(mlp_rows), net.to_core(mlp_rows_near)
-    grad_enc, dec_more = end(
-        dec_end_kernel, grad_residual, part, other, grad_out, dec, dec_mod, matches
+    grad_attn_rows, grad_attn_rows_far = net.gather(grad_attn_rows, dec_way)
+    down_sent, down_kept = weight_grads(
+        (((0, features), (1, 0, units)),), (attn_rows, mlp_rows), dec_select
+    )
+    down_got = net.first_half(down_sent, dec_way)
+    other, down_sent = tie(other, down_sent)
+    grad_enc, dec_more = call(
+        dec_end_kernel, [((2 * cap, features), F32), ((3, features), F32)],
+        part, other, grad_residual, dec["x"], dec_mod, matches, late=(2, 3),
     )
 
     rows = 2 * cap
-    grad_out, *mlp_rows = tie(grad_enc, *mlp_rows)
+    grad_out = grad_enc
     enc_grad_rows, part = call(
         enc_mlp_back_kernel, [((rows, units + features), BF16), ((rows, features), BF16)],
-        grad_out, enc["pre"], enc_mod, up, down, flops=4 * rows * features * units, late=(1,),
-    )
-    part, qkv, proj = load(part, enc_qkv, enc_proj)
+        grad_out, enc["pre"], enc_mod, up, down, late=(1,),
+    )
+    part, grad_rows_far = tie(part, grad_rows_far)
+    grad_rows = grad_rows, grad_rows_far, net.to_core(grad_rows), net.to_core(grad_rows_far)
+    part, proj = load(part, enc_proj)
     other = net.to_heads(part)
-    enc_grad_rows, enc_grad_rows_near = net.gather(enc_grad_rows)
-    down_sent, down_kept = weight_grads(
-        (((0, features), (1, 0, units)),), (attn_rows, mlp_rows), select
-    )
-    down_got = net.first_half(down_sent)
-    other, grad_rows_near, down_sent = tie(other, grad_rows_near, down_sent)
-    grad_rows = grad_rows, grad_rows_near, net.to_core(grad_rows), net.to_core(grad_rows_near)
+    enc_grad_rows, enc_grad_rows_far = net.gather(enc_grad_rows, enc_way)
+    up_sent, up_kept = weight_grads(
+        (((0, units), (1, 0, units)),), (mlp_rows, grad_rows), dec_select
+    )
+    up_got = net.first_half(up_sent, dec_way)
+    other, up_sent, down_got, *enc_rows = tie(other, up_sent, down_got, *enc_rows)
+    down_sent, down_kept = halve(down_kept, down_got)
+    down_got = net.to_far(down_sent)
     grad_residual, grad_branch, dq, dkv, dkv_other, enc_sums = attention_back(
         grad_out, part, other, enc, enc_mod, proj
     )
-    dkv_other, *grad_rows = tie(net.to_core(dkv_other), *grad_rows)
+    dkv_other, qkv = load(dkv_other, enc_qkv)
+    dkv_other, down_sent, enc_grad_rows_far, grad_attn_rows_far = tie(
+        net.to_core(dkv_other), down_sent, enc_grad_rows_far, grad_attn_rows_far
+    )
+    grad_attn_rows = (
+        grad_attn_rows, grad_attn_rows_far, net.to_core(grad_attn_rows), net.to_core(grad_attn_rows_far)
+    )
+    enc_grad_rows = (
+        enc_grad_rows, enc_grad_rows_far, net.to_core(enc_grad_rows), net.to_core(enc_grad_rows_far)
+    )
     enc_grad_attn_rows, part = qkv_back(dq, dkv, dkv_other, grad_branch, qkv)
     other = net.to_heads(part)
-    enc_grad_attn_rows, enc_grad_attn_rows_near = net.gather(enc_grad_attn_rows)
-    up_sent, up_kept = weight_grads(
-        (((0, units), (1, 0, units)),), (mlp_rows, grad_rows), select
-    )
-    up_got = net.first_half(up_sent)
-    other, up_sent, down_got, grad_attn_rows_near = tie(other, up_sent, down_got, grad_attn_rows_near)
-    grad_attn_rows = (
-        grad_attn_rows, grad_attn_rows_near, net.to_core(grad_attn_rows), net.to_core(grad_attn_rows_near)
-    )
-    down_sent, down_kept = halve(down_kept, down_got)
-    down_got = net.to_far(down_sent)
-    grad_in, enc_more = end(enc_end_kernel, grad_residual, part, other, grad_out, enc, enc_mod)
-
-    grad_in, down_sent, *grad_attn_rows = tie(grad_in, down_sent, *grad_attn_rows)
+    enc_grad_attn_rows, enc_grad_attn_rows_far = net.gather(enc_grad_attn_rows, enc_way)
     attn_sent, attn_kept = weight_grads(
         (((0, 0), (1, features, 3 * width)), ((1, 0), (0, 2 * features, width))),
-        (attn_rows, grad_attn_rows), select,
-    )
-    attn_got = net.first_half(attn_sent)
-    attn_sent, enc_grad_rows_near = tie(attn_sent, enc_grad_rows_near)
-    enc_grad_rows = (
-        enc_grad_rows, enc_grad_rows_near, net.to_core(enc_grad_rows), net.to_core(enc_grad_rows_near)
-    )
-    enc_up_sent, enc_up_kept = weight_grads(
-        (((0, units), (1, 0, units)),), (enc_rows, enc_grad_rows), select
-    )
-    enc_up_got = net.first_half(enc_up_sent)
-    up_got, enc_up_sent = tie(up_got, enc_up_sent)
+        (attn_rows, grad_attn_rows), dec_select,
+    )
+    attn_got = net.first_half(attn_sent, dec_way)
+    other, attn_sent, up_got, down_got, *enc_grad_rows = tie(
+        other, attn_sent, up_got, down_got, *enc_grad_rows
+    )
+    grad_in, enc_more = call(
+        enc_end_kernel, [((2 * cap, features), BF16), ((3, features), F32)],
+        part, other, grad_residual, enc["x"], enc_mod, grad_out, enc["mlp"], enc["mlp_other"],
+        late=(2, 3, 6, 7),
+    )
+
+    grad_in, up_got = tie(grad_in, up_got)
     up_sent, up_kept = halve(up_kept, up_got)
     up_got = net.to_far(up_sent)
     up_sent, *enc_grad_rows = tie(up_sent, *enc_grad_rows)
+    enc_up_sent, enc_up_kept = weight_grads(
+        (((0, units), (1, 0, units)),), (enc_rows, enc_grad_rows), enc_select
+    )
+    enc_up_got = net.first_half(enc_up_sent, enc_way)
+    enc_up_sent, *enc_grad_rows = tie(enc_up_sent, *enc_grad_rows)
     enc_down_sent, enc_down_kept = weight_grads(
-        (((1, units), (0, 0, units)),), (enc_rows, enc_grad_rows), select
-    )
-    enc_down_got = net.first_half(enc_down_sent)
-    enc_down_sent, enc_grad_attn_rows_near = tie(enc_down_sent, enc_grad_attn_rows_near)
+        (((1, units), (0, 0, units)),), (enc_rows, enc_grad_rows), enc_select
+    )
+    enc_down_got = net.first_half(enc_down_sent, enc_way)
+    enc_down_sent, enc_grad_attn_rows_far, attn_got = tie(
+        enc_down_sent, enc_grad_attn_rows_far, attn_got
+    )
     enc_grad_attn_rows = (
-        enc_grad_attn_rows, enc_grad_attn_rows_near,
-        net.to_core(enc_grad_attn_rows), net.to_core(enc_grad_attn_rows_near),
-    )
+        enc_grad_attn_rows, enc_grad_attn_rows_far,
+        net.to_core(enc_grad_attn_rows), net.to_core(enc_grad_attn_rows_far),
+    )
+    attn_sent, attn_kept = halve(attn_kept, attn_got)
+    attn_sent, down_got = tie(attn_sent, down_got)
+    attn_got = net.to_far(attn_sent)
     enc_attn_sent, enc_attn_kept = weight_grads(
         (
             ((0, units + features), (1, features, 3 * width)),
             ((1, 0), (0, units + 2 * features, width)),
         ),
-        (enc_rows, enc_grad_attn_rows), select,
-    )
-    enc_attn_got = net.first_half(enc_attn_sent)
-    attn_got, enc_attn_sent = tie(attn_got, enc_attn_sent)
-    attn_sent, attn_kept = halve(attn_kept, attn_got)
-    attn_got = net.to_far(attn_sent)
+        (enc_rows, enc_grad_attn_rows), enc_select,
+    )
+    enc_attn_got = net.first_half(enc_attn_sent, enc_way)
+    enc_up_got, enc_attn_sent = tie(enc_up_got, enc_attn_sent)
     enc_up_sent, enc_up_kept = halve(enc_up_kept, enc_up_got)
+    enc_up_sent, up_got = tie(enc_up_sent, up_got)
     enc_up_got = net.to_far(enc_up_sent)
+    grad_in, enc_sums, enc_more, enc_up_sent = tie(grad_in, enc_sums, enc_more, enc_up_sent)
+    grad_in_parts = net.collect_parts([grad_in[:cap], grad_in[cap:]])
     enc_down_sent, enc_down_kept = halve(enc_down_kept, enc_down_got)
+    enc_down_sent, attn_got = tie(enc_down_sent, attn_got)
     enc_down_got = net.to_far(enc_down_sent)
     enc_attn_sent, enc_attn_kept = halve(enc_attn_kept, enc_attn_got)
+    enc_attn_sent, enc_up_got, *grad_in_parts = tie(enc_attn_sent, enc_up_got, *grad_in_parts)
     enc_attn_got = net.to_far(enc_attn_sent)
 
     out = net.collected(out_parts)
-    input_grad = net.collected(net.collect_parts([grad_in[:cap], grad_in[cap:]]))
-    mask_part = dec_more[3]
+    input_grad = net.collected(grad_in_parts).astype(F32)
+    mask_part = dec_more[2]
 
     enc_mod_grad, dec_mod_grad = (
-        jnp.concatenate([more[0], more[1], sums[2], sums[0], sums[1], more[2]])
-        for more, sums in ((enc_more, enc_sums), (dec_more, dec_sums))
+        jnp.concatenate([more[0], more[1], sums[2], sums[0], sums[1], gate])
+        for more, sums, gate in ((enc_more, enc_sums, enc_more[2]), (dec_more, dec_sums, dec_gate[0]))
     )
 
     share = features // (net.ndp * 4)

time: 347 us -> 318 us (0.916)
  waiting for transfers between devices: 143 us -> 111 us
  Pallas kernels: 72.9 us -> 97.2 us
  local copies, waits for them, and re-layouts: 44.5 us -> 29.3 us
  starting transfers between devices: 67.2 us -> 59.9 us
    ppermute x8 -> x9, waiting for transfers between devices: 50 us -> 10.9 us  [to_hi(): return lax.ppermute(a, 'dp', [(d, d ^ 2) for d in range(self.ndp)])]
    unnamed x229 -> x185, local copies, waits for them, and re-layouts: 42 us -> 23.5 us
    ppermute x9 -> x8, waiting for transfers between devices: 24.4 us -> 42.5 us  [to_near(): return lax.ppermute(a, 'region', self.near)]
    pallas_call x6 -> x8, Pallas kernels: 3.95 us -> 21.4 us  [load(): pl.pallas_call(load_kernel, out_shape=[jax.ShapeDtypeStruct(w.shape, w.dt...]
    ppermute x20, starting transfers between devices: 20.2 us -> 8.48 us  [to_core(): return lax.ppermute(a, 'dp', self.core_perm)]
    ppermute x8, waiting for transfers between devices: 42.9 us -> 32.8 us  [to_far(): return lax.ppermute(a, 'region', self.far)]
    ppermute x4, starting transfers between devices: 1.67 us -> 6.46 us  [spread_images(): lax.ppermute(part, ('dp', 'region'), perm)]
    ppermute x9 -> x8, starting transfers between devices: 9.75 us -> 5.02 us  [to_near(): return lax.ppermute(a, 'region', self.near)]
  transfers between devices with their start and end apart: 62 -> 62, of which waited for: 29 -> 23; matrix products, arithmetic and copies ran while one was open for 3% -> 6% of each run, Pallas kernels for 19% -> 30%
where the time goes in v1:
time: 318 us; the launch traced here: 314 us
  waiting for transfers between devices  111 us (35%)
  Pallas kernels  97.2 us (31%)
  starting transfers between devices  59.9 us (19%)
  local copies, waits for them, and re-layouts  29.3 us (9%)
  other arithmetic  8.52 us (3%)
  matrix products  5.49 us (2%)
    pallas_call x27, Pallas kernels, call(): pl.pallas_call(body, out_shape=shapes, in_specs=[hbm if i in late else vm...  54.6 us
    ppermute x8, waiting for transfers between devices, to_near(): return lax.ppermute(a, 'region', self.near)  42.5 us
    ppermute x8, waiting for transfers between devices, to_far(): return lax.ppermute(a, 'region', self.far)  32.8 us
    unnamed x185, local copies, waits for them, and re-layouts  23.5 us
    pallas_call x8, Pallas kernels, load(): pl.pallas_call(load_kernel, out_shape=[jax.ShapeDtypeStruct(w.shape, w.dt...  21.4 us
    pallas_call x6, Pallas kernels, weight_grads(): pl.pallas_call(functools.partial(weight_grad_kernel, products), out_shape...  21.3 us
    ppermute x9, waiting for transfers between devices, to_heads(): return lax.ppermute(a, 'heads', [(0, 1), (1, 0)])  15.4 us
    ppermute x8, starting transfers between devices, to_far(): return lax.ppermute(a, 'region', self.far)  14.4 us
  transfers between devices with their start and end apart: 62, of which 23 were waited for; matrix products, arithmetic and copies ran while one was open for 6% of the time, Pallas kernels for 30%

profile of v1, /device:TPU:0, one launch (start us, length us, event | category | flops | bytes accessed | tf_op | source)
XLA Modules:
  0.0 314.1 jit_solution(9896832275006433851)
XLA Ops:
  4.6 2.7 collective-permute-start.3
  10.6 3.6 %collective-permute-done.1 = f32[2,1728]{1,0:T(2,128)S(1)} collective-permute-done((f32[2,1728]{1,0:T(2,128)S(1)}, f32[2,1728]{1,0:T(2,128)S(1)}, u32[]{:S(2)}, u32[]{:S(2)}) %collective-permute-start.1) | collective-permute-done | bytes 13856 | tf_op jit(solution)/shard_map/near/ppermute | solution.py:444
  14.3 5.1 %collective-permute-start.4 = (f32[2,1728]{1,0:T(2,128)S(1)}, f32[2,1728]{1,0:T(2,128)S(1)}, u32[]{:S(2)}, u32[]{:S(2)}) collective-permute-start(f32[2,1728]{1,0:T(2,128)S(1)} %fusion.10), channel_id=1, source_target_pairs={{0,4},{2,6},{4,0},{6,2},{1,5},{3,7},{5,1},{7,3},{8,12},{10,14},{12... | collective-permute-start | bytes 41480 | tf_op jit(solution)/shard_map/far/ppermute | solution.py:448
  25.6 3.6 %enc_qkv_kernel.1 = (f32[96,1152]{1,0:T(8,128)S(1)}, bf16[96,1152]{1,0:T(8,128)(2,1)S(1)}, bf16[96,576]{1,0:T(8,128)(2,1)S(1)}, bf16[96,1280]{1,0:T(8,128)(2,1)S(1)}) custom-call(bf16[48,1280]{1,0:T(8,128)(2,1)S(1)} %collective-permute-done.2.refs_0_, bf16[48,1280]{1,0:T(8,128)(2,1)S(1)} %collective-permute-done.3.refs_1_, ...), custom_call_target="tpu_custom_call" | custom-call | tf_op jit(solution)/shard_map/enc_qkv_kernel/pallas_call | solution.py:57
  38.4 4.1 %load.8 = (bf16[1152,2304]{1,0:T(8,128)(2,1)S(1)}, bf16[2304,1152]{1,0:T(8,128)(2,1)S(1)}) custom-call(bf16[1152,2304]{1,0:T(8,128)(2,1)} %refs_0_.3, bf16[2304,1152]{1,0:T(8,128)(2,1)} %refs_1_.2), custom_call_target="tpu_custom_call" | custom-call | flops 3000000000 | tf_op jit(solution)/shard_map/load/pallas_call | solution.py:88
  52.9 2.4 dec_qkv_kernel.1
  57.6 2.4 attention_kernel.3
  63.8 4.1 %load.10 = (bf16[1152,2304]{1,0:T(8,128)(2,1)S(1)}, bf16[2304,1152]{1,0:T(8,128)(2,1)S(1)}) custom-call(bf16[1152,2304]{1,0:T(8,128)(2,1)} %refs_0_.1, bf16[2304,1152]{1,0:T(8,128)(2,1)} %refs_1_.1), custom_call_target="tpu_custom_call" | custom-call | flops 3000000000 | tf_op jit(solution)/shard_map/load/pallas_call | solution.py:88
  74.5 3.3 %dec_mlp_back_kernel.1 = (bf16[128,2304]{1,0:T(8,128)(2,1)S(1)}, bf16[128,1152]{1,0:T(8,128)(2,1)S(1)}) custom-call(bf16[128,2944]{1,0:T(8,128)(2,1)S(1)} %get-tuple-element.240.refs_0_, f32[128,2304]{1,0:T(8,128)S(1)} %get-tuple-element.217.refs_1_, bf16[1152,2304]{1,0:T(8,128)(2,1)S(1)} %get-tuple-element.213.refs_4_.refs_2_, ...), custom_call_target="tpu_custom_call" | custom-call | tf_op jit(solution)/shard_map/dec_mlp_back_kernel/pallas_call | solution.py:57
  77.8 3.7 %collective-permute-done.14.refs_2_ = bf16[128,1152]{1,0:T(8,128)(2,1)S(1)} collective-permute-done((bf16[128,1152]{1,0:T(8,128)(2,1)S(1)}, bf16[128,1152]{1,0:T(8,128)(2,1)S(1)}, u32[]{:S(2)}, u32[]{:S(2)}) %collective-permute-start.14) | collective-permute-done | bytes 294944 | tf_op jit(solution)/shard_map/heads/ppermute | solution.py:452
  86.0 3.3 %collective-permute-done.15.refs_2_ = bf16[128,1152]{1,0:T(8,128)(2,1)S(1)} collective-permute-done((bf16[128,1152]{1,0:T(8,128)(2,1)S(1)}, bf16[128,1152]{1,0:T(8,128)(2,1)S(1)}, u32[]{:S(2)}, u32[]{:S(2)}) %collective-permute-start.15) | collective-permute-done | bytes 294944 | tf_op jit(solution)/shard_map/heads/ppermute | solution.py:452
  93.2 5.8 %attention_back_kernel.2 = (f32[128,1152]{1,0:T(8,128)S(1)}, bf16[128,1152]{1,0:T(8,128)(2,1)S(1)}, bf16[128,576]{1,0:T(8,128)(2,1)S(1)}, f32[128,1152]{1,0:T(8,...) custom-call(bf16[128,1152]{1,0:T(8,128)(2,1)S(1)} %copy-done.25, ...), custom_call_target="tpu_custom_call" | custom-call | tf_op jit(solution)/shard_map/attention_back_kernel/pallas_call | solution.py:57
  105.6 4.3 %collective-permute-done.22 = bf16[64,1152]{1,0:T(8,128)(2,1)} collective-permute-done((bf16[64,1152]{1,0:T(8,128)(2,1)}, bf16[64,1152]{1,0:T(8,128)(2,1)}, u32[]{:S(2)}, u32[]{:S(2)}) %collective-permute-start.22) | collective-permute-done | bytes 147488 | tf_op jit(solution)/shard_map/collect/ppermute | solution.py:480
  120.1 4.1 %load.13 = (bf16[1152,2304]{1,0:T(8,128)(2,1)S(1)}, bf16[2304,1152]{1,0:T(8,128)(2,1)S(1)}) custom-call(bf16[1152,2304]{1,0:T(8,128)(2,1)} %refs_0_.3, bf16[2304,1152]{1,0:T(8,128)(2,1)} %refs_1_.2), custom_call_target="tpu_custom_call" | custom-call | flops 3000000000 | tf_op jit(solution)/shard_map/load/pallas_call | solution.py:88
  124.3 2.9 weight_grads.6
  127.2 2.3 dec_end_kernel.1
  129.5 4.8 %enc_mlp_back_kernel.1 = (bf16[96,3456]{1,0:T(8,128)(2,1)S(1)}, bf16[96,1152]{1,0:T(8,128)(2,1)S(1)}) custom-call(f32[96,1152]{1,0:T(8,128)S(1)} %get-tuple-element.248.refs_0_.refs_5_, f32[96,2304]{1,0:T(8,128)} %copy-done.30, f32[6,1152]{1,0:T(8,128)S(1)} %reshape_squeeze.6.refs_2_.refs_3_.refs_6_.refs_4_, ...), custom_call_target="tpu_custom_call" | custom-call | tf_op jit(solution)/shard_map/enc_mlp_back_kernel/pallas_call | solution.py:57
  139.3 3.4 %weight_grads.7 = (bf16[144,2304]{1,0:T(8,128)(2,1)}, f32[144,2304]{1,0:T(8,128)S(1)}) custom-call(bf16[128,3456]{1,0:T(8,128)(2,1)} %copy-done.4, bf16[128,3456]{1,0:T(8,128)(2,1)} %collective-permute-done.18.refs_5_.refs_1_, bf16[128,3456]{1,0:T(8,128)(2,1)} %copy-done.71, bf16[128,3456]{1,0:T(8,128)(2,1)} %copy-done.72, bf16[128,2304]{1,0:T(8,128)(2,1)} %copy-done.47, ...), custom_call_target="tpu_custom_call" | custom-call | tf_op jit(solution)/shard_map/weight_grads/pallas_call | solution.py:524
  144.0 8.3 %collective-permute-done.30.refs_1_ = bf16[144,2304]{1,0:T(8,128)(2,1)S(1)} collective-permute-done((bf16[144,2304]{1,0:T(8,128)(2,1)S(1)}, bf16[144,2304]{1,0:T(8,128)(2,1)S(1)}, u32[]{:S(2)}, u32[]{:S(2)}) %collective-permute-start.30) | collective-permute-done | bytes 663584 | tf_op jit(solution)/shard_map/near/ppermute | solution.py:444
  152.4 4.7 %attention_back_kernel.3 = (f32[96,1152]{1,0:T(8,128)S(1)}, bf16[96,1152]{1,0:T(8,128)(2,1)S(1)}, bf16[96,576]{1,0:T(8,128)(2,1)S(1)}, f32[96,1152]{1,0:T(8,128)...) custom-call(f32[96,1152]{1,0:T(8,128)S(1)} %get-tuple-element.248.refs_0_.refs_5_, ...), custom_call_target="tpu_custom_call" | custom-call | tf_op jit(solution)/shard_map/attention_back_kernel/pallas_call | solution.py:57
  158.6 7.5 %collective-permute-done.34.refs_5_ = bf16[96,3456]{1,0:T(8,128)(2,1)} collective-permute-done((bf16[96,3456]{1,0:T(8,128)(2,1)S(1)}, bf16[96,3456]{1,0:T(8,128)(2,1)}, u32[]{:S(2)}, u32[]{:S(2)}) %collective-permute-start.34) | collective-permute-done | bytes 663584 | tf_op jit(solution)/shard_map/near/ppermute | solution.py:444
  175.4 4.5 %weight_grads.8 = (bf16[144,2304]{1,0:T(8,128)(2,1)}, f32[144,2304]{1,0:T(8,128)S(1)}) custom-call(bf16[128,2944]{1,0:T(8,128)(2,1)} %copy-done.3, bf16[128,2944]{1,0:T(8,128)(2,1)} %collective-permute-done.16.refs_1_, bf16[128,2944]{1,0:T(8,128)(2,1)} %collective-permute-done.19.refs_2_, bf16[128,2944]{1,0:T(8,128)(2,1)} %collective-permute-done.20.refs_3_, ...), custom_call_target="tpu_custom_call" | custom-call | tf_op jit(solution)/shard_map/weight_grads/pallas_call | solution.py:524
  181.2 3.3 %collective-permute-done.40.refs_1_ = bf16[72,2304]{1,0:T(8,128)(2,1)S(1)} collective-permute-done((bf16[72,2304]{1,0:T(8,128)(2,1)S(1)}, bf16[72,2304]{1,0:T(8,128)(2,1)S(1)}, u32[]{:S(2)}, u32[]{:S(2)}) %collective-permute-start.40) | collective-permute-done | bytes 331808 | tf_op jit(solution)/shard_map/far/ppermute | solution.py:448
  186.0 6.5 %collective-permute-done.39.refs_1_ = bf16[144,2304]{1,0:T(8,128)(2,1)} collective-permute-done((bf16[144,2304]{1,0:T(8,128)(2,1)}, bf16[144,2304]{1,0:T(8,128)(2,1)}, u32[]{:S(2)}, u32[]{:S(2)}) %collective-permute-start.39) | collective-permute-done | bytes 663584 | tf_op jit(solution)/shard_map/near/ppermute | solution.py:444
  198.6 3.3 %weight_grads.9 = (bf16[144,2304]{1,0:T(8,128)(2,1)}, f32[144,2304]{1,0:T(8,128)S(1)}) custom-call(bf16[96,5248]{1,0:T(8,128)(2,1)} %copy-done.2, bf16[96,5248]{1,0:T(8,128)(2,1)} %copy-done.67, bf16[96,5248]{1,0:T(8,128)(2,1)} %copy-done.69, bf16[96,5248]{1,0:T(8,128)(2,1)} %copy-done.70, bf16[96,3456]{1,0:T(8,128)(2,1)} %copy-done.5, ...), custom_call_target="tpu_custom_call" | custom-call | tf_op jit(solution)/shard_map/weight_grads/pallas_call | solution.py:524
  203.5 2.7 weight_grads.10
  208.2 16.5 %collective-permute-done.44.refs_1_ = bf16[144,2304]{1,0:T(8,128)(2,1)S(1)} collective-permute-done((bf16[144,2304]{1,0:T(8,128)(2,1)}, bf16[144,2304]{1,0:T(8,128)(2,1)S(1)}, u32[]{:S(2)}, u32[]{:S(2)}) %collective-permute-start.44) | collective-permute-done | bytes 663584 | tf_op jit(solution)/shard_map/near/ppermute | solution.py:444
  228.6 4.5 %weight_grads.11 = (bf16[144,2304]{1,0:T(8,128)(2,1)}, f32[144,2304]{1,0:T(8,128)S(1)}) custom-call(bf16[96,5248]{1,0:T(8,128)(2,1)} %copy-done.2, bf16[96,5248]{1,0:T(8,128)(2,1)} %copy-done.67, bf16[96,5248]{1,0:T(8,128)(2,1)} %copy-done.69, bf16[96,5248]{1,0:T(8,128)(2,1)} %copy-done.70, bf16[96,2944]{1,0:T(8,128)(2,1)} %get-tuple-element.279.refs_4_, ...), custom_call_target="tpu_custom_call" | custom-call | tf_op jit(solution)/shard_map/weight_grads/pallas_call | solution.py:524
  246.6 10.9 %collective-permute-done.59.refs_1_ = bf16[144,2304]{1,0:T(8,128)(2,1)S(1)} collective-permute-done((bf16[144,2304]{1,0:T(8,128)(2,1)}, bf16[144,2304]{1,0:T(8,128)(2,1)S(1)}, u32[]{:S(2)}, u32[]{:S(2)}) %collective-permute-start.59) | collective-permute-done | bytes 663584 | tf_op jit(solution)/shard_map/hi/ppermute | solution.py:456
  262.9 2.9 collective-permute-start.50
  272.3 12.5 %collective-permute-done.61.refs_1_ = bf16[72,2304]{1,0:T(8,128)(2,1)} collective-permute-done((bf16[72,2304]{1,0:T(8,128)(2,1)}, bf16[72,2304]{1,0:T(8,128)(2,1)}, u32[]{:S(2)}, u32[]{:S(2)}) %collective-permute-start.61) | collective-permute-done | bytes 331808 | tf_op jit(solution)/shard_map/far/ppermute | solution.py:448
  299.2 13.6 %collective-permute-done.58.refs_1_ = bf16[72,2304]{1,0:T(8,128)(2,1)S(1)} collective-permute-done((bf16[72,2304]{1,0:T(8,128)(2,1)S(1)}, bf16[72,2304]{1,0:T(8,128)(2,1)S(1)}, u32[]{:S(2)}, u32[]{:S(2)}) %collective-permute-start.58) | collective-permute-done | bytes 331808 | tf_op jit(solution)/shard_map/far/ppermute | solution.py:448
  (400 shorter events, 144.0 us)
Async XLA Ops:
  30.7 19.2 %collective-permute-start.9 = (bf16[64,1152]{1,0:T(8,128)(2,1)}, bf16[64,1152]{1,0:T(8,128)(2,1)S(1)}, u32[]{:S(2)}, u32[]{:S(2)}) collective-permute-start(bf16[64,1152]{1,0:T(8,128)(2,1)} %get-tuple-element.366), channel_id=1, source_target_pairs={{0,0},{2,2},{4,8},{6,10},{8,4},{10,6},{12,12},{14,14},{16,16},{18,... | collective-permute-start | bytes 442376 | tf_op jit(solution)/shard_map/spread/ppermute | solution.py:473
  32.5 17.5 %collective-permute-start.10 = (bf16[64,1152]{1,0:T(8,128)(2,1)}, bf16[64,1152]{1,0:T(8,128)(2,1)S(1)}, u32[]{:S(2)}, u32[]{:S(2)}) collective-permute-start(bf16[64,1152]{1,0:T(8,128)(2,1)} %get-tuple-element.365), channel_id=1, source_target_pairs={{0,2},{2,0},{4,10},{6,8},{8,6},{10,4},{12,14},{14,12},{16,18},{18,... | collective-permute-start | bytes 442376 | tf_op jit(solution)/shard_map/spread/ppermute | solution.py:473
  47.0 27.4 %collective-permute-start.13 = (bf16[96,5248]{1,0:T(8,128)(2,1)S(1)}, bf16[96,5248]{1,0:T(8,128)(2,1)S(1)}, u32[]{:S(2)}, u32[]{:S(2)}) collective-permute-start(bf16[96,5248]{1,0:T(8,128)(2,1)S(1)} %get-tuple-element.261.refs_0_), channel_id=1, source_target_pairs={{0,2},{2,0},{4,6},{6,4},{1,3},{3,1},{5,7},{7,5},{8,10},{10,8},{12,... | collective-permute-start | bytes 3022856 | tf_op jit(solution)/shard_map/near/ppermute | solution.py:444
  62.3 23.7 %collective-permute-start.16 = (bf16[128,2944]{1,0:T(8,128)(2,1)S(1)}, bf16[128,2944]{1,0:T(8,128)(2,1)}, u32[]{:S(2)}, u32[]{:S(2)}) collective-permute-start(bf16[128,2944]{1,0:T(8,128)(2,1)S(1)} %get-tuple-element.240.refs_0_), channel_id=1, source_target_pairs={{0,16},{8,24},{16,0},{24,8},{1,17},{9,25},{17,1},{25,9},{2,18},{10... | collective-permute-start | bytes 2261000 | tf_op jit(solution)/shard_map/hi/ppermute | solution.py:456
  83.0 28.4 %collective-permute-start.19 = (bf16[128,2944]{1,0:T(8,128)(2,1)S(1)}, bf16[128,2944]{1,0:T(8,128)(2,1)}, u32[]{:S(2)}, u32[]{:S(2)}) collective-permute-start(bf16[128,2944]{1,0:T(8,128)(2,1)S(1)} %get-tuple-element.240.refs_0_), channel_id=1, source_target_pairs={{0,8},{8,0},{16,24},{24,16},{1,9},{9,1},{17,25},{25,17},{2,10},{10... | collective-permute-start | bytes 2261000 | tf_op jit(solution)/shard_map/core/ppermute | solution.py:440
  83.0 28.4 %collective-permute-start.18 = (bf16[128,3456]{1,0:T(8,128)(2,1)S(1)}, bf16[128,3456]{1,0:T(8,128)(2,1)}, u32[]{:S(2)}, u32[]{:S(2)}) collective-permute-start(bf16[128,3456]{1,0:T(8,128)(2,1)S(1)} %get-tuple-element.227.refs_4_.refs_0_), channel_id=1, source_target_pairs={{0,16},{8,24},{16,0},{24,8},{1,17},{9,25},{17,1},{25,9},{2,18},{10... | collective-permute-start | bytes 2654216 | tf_op jit(solution)/shard_map/hi/ppermute | solution.py:456
  89.3 22.2 %collective-permute-start.20 = (bf16[128,2944]{1,0:T(8,128)(2,1)}, bf16[128,2944]{1,0:T(8,128)(2,1)}, u32[]{:S(2)}, u32[]{:S(2)}) collective-permute-start(bf16[128,2944]{1,0:T(8,128)(2,1)} %collective-permute-done.16.refs_1_), channel_id=1, source_target_pairs={{0,8},{8,0},{16,24},{24,16},{1,9},{9,1},{17,25},{25,17},{2,10},{10... | collective-permute-start | bytes 2261000 | tf_op jit(solution)/shard_map/core/ppermute | solution.py:440
  111.6 24.0 %collective-permute-start.31 = (bf16[96,5248]{1,0:T(8,128)(2,1)S(1)}, bf16[96,5248]{1,0:T(8,128)(2,1)S(1)}, u32[]{:S(2)}, u32[]{:S(2)}) collective-permute-start(bf16[96,5248]{1,0:T(8,128)(2,1)S(1)} %get-tuple-element.261.refs_0_), channel_id=1, source_target_pairs={{0,8},{8,0},{16,24},{24,16},{1,9},{9,1},{17,25},{25,17},{2,10},{10... | collective-permute-start | bytes 3022856 | tf_op jit(solution)/shard_map/core/ppermute | solution.py:440
  112.2 22.1 %collective-permute-start.26 = (bf16[128,2304]{1,0:T(8,128)(2,1)S(1)}, bf16[128,2304]{1,0:T(8,128)(2,1)S(1)}, u32[]{:S(2)}, u32[]{:S(2)}) collective-permute-start(bf16[128,2304]{1,0:T(8,128)(2,1)S(1)} %get-tuple-element.255.refs_4_), channel_id=1, source_target_pairs={{0,16},{8,24},{16,0},{24,8},{1,17},{9,25},{17,1},{25,9},{2,18},{10... | collective-permute-start | bytes 1769480 | tf_op jit(solution)/shard_map/hi/ppermute | solution.py:456
  119.5 16.6 %collective-permute-start.28 = (bf16[128,2304]{1,0:T(8,128)(2,1)S(1)}, bf16[128,2304]{1,0:T(8,128)(2,1)S(1)}, u32[]{:S(2)}, u32[]{:S(2)}) collective-permute-start(bf16[128,2304]{1,0:T(8,128)(2,1)S(1)} %get-tuple-element.255.refs_4_), channel_id=1, source_target_pairs={{0,8},{8,0},{16,24},{24,16},{1,9},{9,1},{17,25},{25,17},{2,10},{10... | collective-permute-start | bytes 1769480 | tf_op jit(solution)/shard_map/core/ppermute | solution.py:440
  119.6 23.2 %collective-permute-start.32 = (bf16[96,5248]{1,0:T(8,128)(2,1)S(1)}, bf16[96,5248]{1,0:T(8,128)(2,1)S(1)}, u32[]{:S(2)}, u32[]{:S(2)}) collective-permute-start(bf16[96,5248]{1,0:T(8,128)(2,1)S(1)} %copy-done.68), channel_id=1, source_target_pairs={{0,8},{8,0},{16,24},{24,16},{1,9},{9,1},{17,25},{25,17},{2,10},{10... | collective-permute-start | bytes 3022856 | tf_op jit(solution)/shard_map/core/ppermute | solution.py:440
  134.6 17.7 %collective-permute-start.30 = (bf16[144,2304]{1,0:T(8,128)(2,1)S(1)}, bf16[144,2304]{1,0:T(8,128)(2,1)S(1)}, u32[]{:S(2)}, u32[]{:S(2)}) collective-permute-start(bf16[144,2304]{1,0:T(8,128)(2,1)S(1)} %get-tuple-element.245), channel_id=1, source_target_pairs={{0,2},{2,0},{4,6},{6,4},{1,3},{3,1},{5,7},{7,5},{8,10},{10,8},{12,... | collective-permute-start | bytes 1990664 | tf_op jit(solution)/shard_map/near/ppermute | solution.py:444
  135.6 23.0 %collective-permute-start.35 = (bf16[128,2944]{1,0:T(8,128)(2,1)S(1)}, bf16[128,2944]{1,0:T(8,128)(2,1)S(1)}, u32[]{:S(2)}, u32[]{:S(2)}) collective-permute-start(bf16[128,2944]{1,0:T(8,128)(2,1)S(1)} %get-tuple-element.275.refs_4_), channel_id=1, source_target_pairs={{0,16},{8,24},{16,0},{24,8},{1,17},{9,25},{17,1},{25,9},{2,18},{10... | collective-permute-start | bytes 2261000 | tf_op jit(solution)/shard_map/hi/ppermute | solution.py:456
  136.1 29.9 %collective-permute-start.34 = (bf16[96,3456]{1,0:T(8,128)(2,1)S(1)}, bf16[96,3456]{1,0:T(8,128)(2,1)}, u32[]{:S(2)}, u32[]{:S(2)}) collective-permute-start(bf16[96,3456]{1,0:T(8,128)(2,1)S(1)} %get-tuple-element.300.refs_4_), channel_id=1, source_target_pairs={{0,2},{2,0},{4,6},{6,4},{1,3},{3,1},{5,7},{7,5},{8,10},{10,8},{12,... | collective-permute-start | bytes 1990664 | tf_op jit(solution)/shard_map/near/ppermute | solution.py:444
  166.5 17.9 %collective-permute-start.40 = (bf16[72,2304]{1,0:T(8,128)(2,1)S(1)}, bf16[72,2304]{1,0:T(8,128)(2,1)S(1)}, u32[]{:S(2)}, u32[]{:S(2)}) collective-permute-start(bf16[72,2304]{1,0:T(8,128)(2,1)S(1)} %get-tuple-element.273), channel_id=1, source_target_pairs={{0,4},{2,6},{4,0},{6,2},{1,5},{3,7},{5,1},{7,3},{8,12},{10,14},{12... | collective-permute-start | bytes 995336 | tf_op jit(solution)/shard_map/far/ppermute | solution.py:448
  167.8 24.8 %collective-permute-start.39 = (bf16[144,2304]{1,0:T(8,128)(2,1)}, bf16[144,2304]{1,0:T(8,128)(2,1)}, u32[]{:S(2)}, u32[]{:S(2)}) collective-permute-start(bf16[144,2304]{1,0:T(8,128)(2,1)} %get-tuple-element.259), channel_id=1, source_target_pairs={{0,2},{2,0},{4,6},{6,4},{1,3},{3,1},{5,7},{7,5},{8,10},{10,8},{12,... | collective-permute-start | bytes 1990664 | tf_op jit(solution)/shard_map/near/ppermute | solution.py:444
  174.5 18.1 %collective-permute-start.42 = (bf16[96,3456]{1,0:T(8,128)(2,1)}, bf16[96,3456]{1,0:T(8,128)(2,1)}, u32[]{:S(2)}, u32[]{:S(2)}) collective-permute-start(bf16[96,3456]{1,0:T(8,128)(2,1)} %collective-permute-done.34.refs_5_), channel_id=1, source_target_pairs={{0,8},{8,0},{16,24},{24,16},{1,9},{9,1},{17,25},{25,17},{2,10},{10... | collective-permute-start | bytes 1990664 | tf_op jit(solution)/shard_map/core/ppermute | solution.py:440
  180.9 26.4 %collective-permute-start.43 = (bf16[96,2944]{1,0:T(8,128)(2,1)}, bf16[96,2944]{1,0:T(8,128)(2,1)}, u32[]{:S(2)}, u32[]{:S(2)}) collective-permute-start(bf16[96,2944]{1,0:T(8,128)(2,1)} %get-tuple-element.279.refs_4_), channel_id=1, source_target_pairs={{0,2},{2,0},{4,6},{6,4},{1,3},{3,1},{5,7},{7,5},{8,10},{10,8},{12,... | collective-permute-start | bytes 1695752 | tf_op jit(solution)/shard_map/near/ppermute | solution.py:444
  185.2 39.6 %collective-permute-start.44 = (bf16[144,2304]{1,0:T(8,128)(2,1)}, bf16[144,2304]{1,0:T(8,128)(2,1)S(1)}, u32[]{:S(2)}, u32[]{:S(2)}) collective-permute-start(bf16[144,2304]{1,0:T(8,128)(2,1)} %get-tuple-element.283), channel_id=1, source_target_pairs={{0,2},{2,0},{4,6},{6,4},{1,3},{3,1},{5,7},{7,5},{8,10},{10,8},{12,... | collective-permute-start | bytes 1990664 | tf_op jit(solution)/shard_map/near/ppermute | solution.py:444
  185.2 40.4 %collective-permute-start.57 = (bf16[4,1152]{1,0:T(4,128)(2,1)S(1)}, bf16[4,1152]{1,0:T(4,128)(2,1)S(1)}, u32[]{:S(2)}, u32[]{:S(2)}) collective-permute-start(bf16[4,1152]{1,0:T(4,128)(2,1)S(1)} %reshape.235), channel_id=1, source_target_pairs={{0,16},{8,24},{16,0},{24,8},{1,17},{9,25},{17,1},{25,9},{2,18},{10... | collective-permute-start | bytes 27656 | tf_op jit(solution)/shard_map/hi/ppermute | solution.py:456
  192.5 33.2 %collective-permute-start.45 = (bf16[96,2944]{1,0:T(8,128)(2,1)}, bf16[96,2944]{1,0:T(8,128)(2,1)}, u32[]{:S(2)}, u32[]{:S(2)}) collective-permute-start(bf16[96,2944]{1,0:T(8,128)(2,1)} %get-tuple-element.279.refs_4_), channel_id=1, source_target_pairs={{0,8},{8,0},{16,24},{24,16},{1,9},{9,1},{17,25},{25,17},{2,10},{10... | collective-permute-start | bytes 1695752 | tf_op jit(solution)/shard_map/core/ppermute | solution.py:440
  203.0 30.1 %collective-permute-start.48 = (bf16[144,2304]{1,0:T(8,128)(2,1)}, bf16[144,2304]{1,0:T(8,128)(2,1)S(1)}, u32[]{:S(2)}, u32[]{:S(2)}) collective-permute-start(bf16[144,2304]{1,0:T(8,128)(2,1)} %get-tuple-element.299), channel_id=1, source_target_pairs={{0,16},{8,24},{16,0},{24,8},{1,17},{9,25},{17,1},{25,9},{2,18},{10... | collective-permute-start | bytes 1990664 | tf_op jit(solution)/shard_map/hi/ppermute | solution.py:456
  207.3 29.4 %collective-permute-start.49 = (bf16[72,2304]{1,0:T(8,128)(2,1)}, bf16[72,2304]{1,0:T(8,128)(2,1)}, u32[]{:S(2)}, u32[]{:S(2)}) collective-permute-start(bf16[72,2304]{1,0:T(8,128)(2,1)} %get-tuple-element.290), channel_id=1, source_target_pairs={{0,4},{2,6},{4,0},{6,2},{1,5},{3,7},{5,1},{7,3},{8,12},{10,14},{12... | collective-permute-start | bytes 995336 | tf_op jit(solution)/shard_map/far/ppermute | solution.py:448
  240.2 17.2 %collective-permute-start.59 = (bf16[144,2304]{1,0:T(8,128)(2,1)}, bf16[144,2304]{1,0:T(8,128)(2,1)S(1)}, u32[]{:S(2)}, u32[]{:S(2)}) collective-permute-start(bf16[144,2304]{1,0:T(8,128)(2,1)} %copy-done.66), channel_id=1, source_target_pairs={{0,16},{8,24},{16,0},{24,8},{1,17},{9,25},{17,1},{25,9},{2,18},{10... | collective-permute-start | bytes 1990664 | tf_op jit(solution)/shard_map/hi/ppermute | solution.py:456
  241.7 18.5 %collective-permute-start.60 = (bf16[72,2304]{1,0:T(8,128)(2,1)S(1)}, bf16[72,2304]{1,0:T(8,128)(2,1)S(1)}, u32[]{:S(2)}, u32[]{:S(2)}) collective-permute-start(bf16[72,2304]{1,0:T(8,128)(2,1)S(1)} %get-tuple-element.337), channel_id=1, source_target_pairs={{0,4},{2,6},{4,0},{6,2},{1,5},{3,7},{5,1},{7,3},{8,12},{10,14},{12... | collective-permute-start | bytes 995336 | tf_op jit(solution)/shard_map/far/ppermute | solution.py:448
  244.1 21.7 %collective-permute-start.55 = (f32[2,2016]{1,0:T(2,128)S(1)}, f32[2,2016]{1,0:T(2,128)S(1)}, u32[]{:S(2)}, u32[]{:S(2)}) collective-permute-start(f32[2,2016]{1,0:T(2,128)S(1)} %bitcast.104), channel_id=1, source_target_pairs={{0,4},{2,6},{4,0},{6,2},{1,5},{3,7},{5,1},{7,3},{8,12},{10,14},{12... | collective-permute-start | bytes 48392 | tf_op jit(solution)/shard_map/far/ppermute | solution.py:448
  260.2 24.7 %collective-permute-start.61 = (bf16[72,2304]{1,0:T(8,128)(2,1)}, bf16[72,2304]{1,0:T(8,128)(2,1)}, u32[]{:S(2)}, u32[]{:S(2)}) collective-permute-start(bf16[72,2304]{1,0:T(8,128)(2,1)} %get-tuple-element.338), channel_id=1, source_target_pairs={{0,4},{2,6},{4,0},{6,2},{1,5},{3,7},{5,1},{7,3},{8,12},{10,14},{12... | collective-permute-start | bytes 995336 | tf_op jit(solution)/shard_map/far/ppermute | solution.py:448
  261.2 30.6 %collective-permute-start.47 = (bf16[144,2304]{1,0:T(8,128)(2,1)}, bf16[144,2304]{1,0:T(8,128)(2,1)S(1)}, u32[]{:S(2)}, u32[]{:S(2)}) collective-permute-start(bf16[144,2304]{1,0:T(8,128)(2,1)} %get-tuple-element.307), channel_id=1, source_target_pairs={{0,16},{8,24},{16,0},{24,8},{1,17},{9,25},{17,1},{25,9},{2,18},{10... | collective-permute-start | bytes 1990664 | tf_op jit(solution)/shard_map/hi/ppermute | solution.py:456
  262.9 32.4 %collective-permute-start.50 = (bf16[72,2304]{1,0:T(8,128)(2,1)}, bf16[72,2304]{1,0:T(8,128)(2,1)}, u32[]{:S(2)}, u32[]{:S(2)}) collective-permute-start(bf16[72,2304]{1,0:T(8,128)(2,1)} %get-tuple-element.312), channel_id=1, source_target_pairs={{0,4},{2,6},{4,0},{6,2},{1,5},{3,7},{5,1},{7,3},{8,12},{10,14},{12... | collective-permute-start | bytes 995336 | tf_op jit(solution)/shard_map/far/ppermute | solution.py:448
  267.9 18.8 %collective-permute-start.56 = (f32[4,2016]{1,0:T(4,128)}, f32[4,2016]{1,0:T(4,128)S(1)}, u32[]{:S(2)}, u32[]{:S(2)}) collective-permute-start(f32[4,2016]{1,0:T(4,128)} %reshape.242), channel_id=1, source_target_pairs={{0,16},{8,24},{16,0},{24,8},{1,17},{9,25},{17,1},{25,9},{2,18},{10... | collective-permute-start | bytes 96776 | tf_op jit(solution)/shard_map/hi/ppermute | solution.py:456
  268.9 24.9 %collective-permute-start.51 = (bf16[48,1152]{1,0:T(8,128)(2,1)}, bf16[48,1152]{1,0:T(8,128)(2,1)S(1)}, u32[]{:S(2)}, u32[]{:S(2)}) collective-permute-start(bf16[48,1152]{1,0:T(8,128)(2,1)} %get-tuple-element.372), channel_id=1, source_target_pairs={{0,0},{2,2},{8,4},{10,6},{4,8},{6,10},{12,12},{14,14},{16,16},{18,... | collective-permute-start | bytes 331784 | tf_op jit(solution)/shard_map/collect/ppermute | solution.py:480
  295.3 17.6 %collective-permute-start.58 = (bf16[72,2304]{1,0:T(8,128)(2,1)S(1)}, bf16[72,2304]{1,0:T(8,128)(2,1)S(1)}, u32[]{:S(2)}, u32[]{:S(2)}) collective-permute-start(bf16[72,2304]{1,0:T(8,128)(2,1)S(1)} %get-tuple-element.325), channel_id=1, source_target_pairs={{0,4},{2,6},{4,0},{6,2},{1,5},{3,7},{5,1},{7,3},{8,12},{10,14},{12... | collective-permute-start | bytes 995336 | tf_op jit(solution)/shard_map/far/ppermute | solution.py:448
  (115 other events, 937.6 us)

commit v2 on v1

--- a/solution.py
+++ b/solution.py
@@ -14,6 +14,7 @@
 BF16 = jnp.bfloat16
 F32 = jnp.float32
 VMEM_LIMIT = 16 * 2**20
+LOAD_CHUNKS = 4
 NT = ((1,), (1,))
 TN = ((0,), (0,))
 
@@ -38,7 +39,7 @@
     return ref.get() if isinstance(ref, Late) else ref
 
 
-def call(kernel, outs, *ins, flops=0, scratch=(), late=(), limit=VMEM_LIMIT):
+def call(kernel, outs, *ins, scratch=(), late=(), after=()):
     shapes = [jax.ShapeDtypeStruct(shape, dtype) for shape, dtype in outs]
     fetched = [pltpu.VMEM(ins[i].shape, ins[i].dtype) for i in late]
     semaphores = [pltpu.SemaphoreType.DMA((len(late),))] if late else []
@@ -48,7 +49,7 @@
         own = len(refs) - len(late) - len(semaphores)
         for at, i in enumerate(late):
             refs[i] = Late(pltpu.make_async_copy(refs[i], refs[own + at], refs[-1].at[at]), refs[own + at])
-        kernel(*refs[:own])
+        kernel(*refs[: len(ins)], *refs[len(ins) + len(after) : own])
         for i in late:
             refs[i].get()
 
@@ -57,13 +58,13 @@
     return pl.pallas_call(
         body,
         out_shape=shapes,
-        in_specs=[hbm if i in late else vmem for i in range(len(ins))],
+        in_specs=[hbm if i in late else vmem for i in range(len(ins))] + [hbm] * len(after),
         out_specs=[vmem] * len(outs),
         name=kernel.__name__,
         scratch_shapes=list(scratch) + fetched + semaphores,
-        compiler_params=pltpu.CompilerParams(vmem_limit_bytes=limit),
-        cost_estimate=pl.CostEstimate(flops=flops, bytes_accessed=0, transcendentals=0),
-    )(*ins)
+        compiler_params=pltpu.CompilerParams(vmem_limit_bytes=VMEM_LIMIT),
+        cost_estimate=pl.CostEstimate(flops=0, bytes_accessed=0, transcendentals=0),
+    )(*ins, *after)
 
 
 def in_hbm(a):
@@ -72,11 +73,16 @@
 
 def load_kernel(*refs):
     count = len(refs) // 2
-    copies = [
-        pltpu.make_async_copy(refs[i], refs[count + i], refs[-1].at[i]) for i in range(count)
-    ]
-    for copy in copies:
-        copy.start()
+    copies = []
+    for source, target in zip(refs[:count], refs[count : 2 * count]):
+        rows = source.shape[0]
+        chunk = -(-rows // LOAD_CHUNKS // 16) * 16
+        for start in range(0, rows, chunk):
+            part = pl.ds(start, min(chunk, rows - start))
+            copies.append(
+                pltpu.make_async_copy(source.at[part], target.at[part], refs[-1].at[len(copies)])
+            )
+            copies[-1].start()
     for copy in copies:
         copy.wait()
 
@@ -91,10 +97,10 @@
         in_specs=[pl.BlockSpec(memory_space=pl.ANY)] * len(weights),
         out_specs=[pl.BlockSpec(memory_space=pltpu.VMEM)] * len(weights),
         name="load",
-        scratch_shapes=[pltpu.SemaphoreType.DMA((len(weights),))],
+        scratch_shapes=[pltpu.SemaphoreType.DMA((LOAD_CHUNKS * len(weights),))],
         compiler_params=pltpu.CompilerParams(vmem_limit_bytes=VMEM_LIMIT),
         cost_estimate=pl.CostEstimate(
-            flops=3 * 10**9, bytes_accessed=0, transcendentals=0
+            flops=0, bytes_accessed=0, transcendentals=0
         ),
     )(*weights)
     return anchor, *loaded, *beside
@@ -342,21 +348,95 @@
 
 
 def enc_end_kernel(
-    part, other, grad_residual, x, mod, grad_out, mlp, mlp_other, grad_ref, sums_ref
+    part, other, grad_residual, x, mod, grad_out, mlp, mlp_other, first_ref, second_ref, sums_ref
 ):
-    grad_ref[...] = block_back(part, other, grad_residual, x, mod, sums_ref).astype(BF16)
+    grad = block_back(part, other, grad_residual, x, mod, sums_ref).astype(BF16)
+    half = first_ref.shape[0]
+    first_ref[...], second_ref[...] = grad[:half], grad[half:]
     sums_ref[2:3, :] = jnp.sum(wide(grad_out) * (wide(mlp) + wide(mlp_other)), axis=0, keepdims=True)
 
 
-def out_kernel(residual, part, other, mod, grad_out, out_ref, sums_ref):
-    out_ref[...] = block_end(here(residual), here(part), other, mod).astype(BF16)
+def out_kernel(residual, part, other, mod, grad_out, first_ref, second_ref, sums_ref):
+    out = block_end(here(residual), here(part), other, mod).astype(BF16)
+    half = first_ref.shape[0]
+    first_ref[...], second_ref[...] = out[:half], out[half:]
     sums_ref[...] = jnp.sum(wide(grad_out) * (wide(part) + wide(other)), axis=0, keepdims=True)
 
 
-def weight_grad_kernel(products, *refs):
+def sums_kernel(enc_more, enc_sums, dec_more, dec_sums, dec_gate, out_ref):
+    out_ref[0:2, :] = enc_more[0:2, :]
+    out_ref[2:3, :] = enc_sums[2:3, :]
+    out_ref[3:5, :] = enc_sums[0:2, :]
+    out_ref[5:6, :] = enc_more[2:3, :]
+    out_ref[6:8, :] = dec_more[0:2, :]
+    out_ref[8:9, :] = dec_sums[2:3, :]
+    out_ref[9:11, :] = dec_sums[0:2, :]
+    out_ref[11:12, :] = dec_gate[...]
+    out_ref[12:13, :] = dec_more[2:3, :]
+
+
+def chosen(flags, i, first, second):
+    return jnp.where(flags[i : i + 1, :1] > 0.5, first, second)
+
+
+def columns_kernel(sums, other, flags, sent_ref, kept_ref):
+    total = sums[...] + other[...]
+    chunk = sent_ref.shape[2]
+    across = total.shape[1] // chunk
+    count = (sent_ref.shape[1] - across) // 2
+
+    def piece(first_row, i):
+        at, lane = first_row + i // across, i % across * chunk
+        return total[at : at + 1, lane : lane + chunk]
+
+    def message(z):
+        parts = [
+            chosen(
+                flags, 4, piece(first_row, 2 * z * count + i), piece(first_row, (2 * z + 1) * count + i)
+            )
+            for first_row in (0, 6)
+            for i in range(count)
+        ]
+        return jnp.concatenate(parts + [piece(12, i) for i in range(across)])
+
+    for high in range(2):
+        low, odd = message(2 * high), message(2 * high + 1)
+        sent_ref[high] = chosen(flags, 3, odd, low)
+        kept_ref[high] = chosen(flags, 3, low, odd)
+
+
+def images_kernel(kept, got, flags, sent_ref, kept_ref):
+    for bit in range(2):
+        low, high = (
+            chosen(flags, 3, kept[i], got[i]) if bit == 0 else chosen(flags, 3, got[i], kept[i])
+            for i in range(2)
+        )
+        sent_ref[bit] = chosen(flags, 2, high, low)
+        kept_ref[bit] = chosen(flags, 2, low, high)
+
+
+def all_images_kernel(kept, got, flags, out_ref):
+    for bit in range(2):
+        out_ref[bit] = chosen(flags, 2, kept[bit], got[bit])
+        out_ref[2 + bit] = chosen(flags, 2, got[bit], kept[bit])
+
+
+def ada_kernel(rows, silu, enc_ref, dec_ref, mask_ref):
+    chunk = rows.shape[2]
+    count = enc_ref.shape[1] // chunk
+    for first, out in ((0, enc_ref), (count, dec_ref)):
+        for i in range(count):
+            out[:, i * chunk : (i + 1) * chunk] = dot(
+                silu[...], rows[:, first + i, :].astype(BF16), TN
+            )
+    mask_ref[...] = jnp.sum(rows[:, 2 * count :, :], axis=0)
+
+
+def weight_grad_kernel(products, unread, *refs):
     count = 1 + max(max(p[0][0], p[1][0]) for p in products)
     bundles, refs = refs[: 4 * count], refs[4 * count :]
-    select, sent_ref, kept_ref, *buffers, semaphores = refs
+    select, refs = refs[0], refs[1 + unread :]
+    sent_ref, kept_ref, *buffers, semaphores = refs
     features = select.shape[1]
     half = sent_ref.shape[0]
     copies = []
@@ -407,8 +487,8 @@
             at += span
 
 
-def in_order(mine, other, bit):
-    return jnp.stack([jnp.where(bit == 0, mine, other), jnp.where(bit == 0, other, mine)])
+def in_order(mine, other, first):
+    return jnp.stack([jnp.where(first, mine, other), jnp.where(first, other, mine)])
 
 
 class Net:
@@ -428,12 +508,15 @@
             for j in range(2)
         ]
 
-    def place(self):
-        self.dp = lax.axis_index("dp")
-        self.hi, self.core = self.dp // 2, self.dp % 2
-        self.z = lax.axis_index("region")
-        self.z1, self.z0 = self.z // 2, self.z % 2
-        self.y = lax.axis_index("heads")
+    def place(self, anchor):
+        dp, z, y = (lax.axis_index(a) for a in ("dp", "region", "heads"))
+        numbers = (dp, z) + tuple(
+            bit == 0 for bit in (dp // 2 % 2, dp % 2, z // 2, z % 2, y)
+        )
+        flags = jnp.stack([jnp.broadcast_to(a, (128,)) for a in numbers[2:]]).astype(F32)
+        anchor, self.flags, *numbers = tie(anchor, flags, *numbers)
+        self.dp, self.z, self.hi_first, self.core_first, self.z1_first, self.z0_first, self.y_first = numbers
+        return anchor
 
     def to_core(self, a):
         with jax.named_scope("core"):
@@ -462,28 +545,28 @@
         if self.nhi == 1:
             return a[None]
         if self.nhi == 2:
-            return in_order(a, self.to_hi(a), self.hi)
+            return in_order(a, self.to_hi(a), self.hi_first)
         return lax.all_gather(a, "dp", axis_index_groups=self.hi_groups(), axis=0)
 
-    def spread_images(self, a):
-        even = self.z0 == 0
-        first, second = jnp.where(even, a[0], a[1]), jnp.where(even, a[1], a[0])
+    def spread_halves(self, a):
+        return jnp.where(self.z0_first, a[0], a[1]), jnp.where(self.z0_first, a[1], a[0])
+
+    def spread_images(self, halves):
         with jax.named_scope("spread"):
-          return [
-            lax.ppermute(part, ("dp", "region"), perm)
-            for part, perm in zip((first, second), self.spread)
-        ]
+            return [
+                lax.ppermute(part, ("dp", "region"), perm)
+                for part, perm in zip(halves, self.spread)
+            ]
 
     def collect_parts(self, parts):
         with jax.named_scope("collect"):
-          return [
-            lax.ppermute(part, ("dp", "region"), [(t, s) for s, t in perm])
-            for part, perm in zip(parts, self.spread)
-        ]
+            return [
+                lax.ppermute(part, ("dp", "region"), [(t, s) for s, t in perm])
+                for part, perm in zip(parts, self.spread)
+            ]
 
     def collected(self, back):
-        even = self.z0 == 0
-        return jnp.stack([jnp.where(even, back[0], back[1]), jnp.where(even, back[1], back[0])])
+        return in_order(back[0], back[1], self.z0_first)
 
     def gather(self, rows, along_dp):
         if not along_dp:
@@ -508,7 +591,7 @@
         return self.to_near(sent) if along_dp else self.to_hi(sent)
 
 
-def weight_grads(products, bundles, select):
+def weight_grads(products, bundles, select, after=()):
     half = select.shape[0] // 2
     features = select.shape[1]
     width = sum(full[2] for _, full in products)
@@ -522,11 +605,11 @@
     ]
     held = sum(2 * math.prod(buffer.shape) for buffer in buffers) + 16 * 2**20
     return pl.pallas_call(
-        functools.partial(weight_grad_kernel, products),
+        functools.partial(weight_grad_kernel, products, len(after)),
         out_shape=[
             jax.ShapeDtypeStruct((half, width), BF16), jax.ShapeDtypeStruct((half, width), F32)
         ],
-        in_specs=[hbm] * len(operands) + [vmem],
+        in_specs=[hbm] * len(operands) + [vmem] + [hbm] * len(after),
         out_specs=[vmem] * 2,
         name="weight_grads",
         scratch_shapes=buffers + [pltpu.SemaphoreType.DMA((8 * len(products),))],
@@ -536,57 +619,136 @@
             bytes_accessed=0,
             transcendentals=0,
         ),
-    )(*operands, select)
-
-
-def finish(kept, got, *shapes):
-    return call(finish_kernel, [(shape, F32) for shape in shapes], kept, got)
-
-
-def halve(kept, got):
+    )(*operands, select, *after)
+
+
+def finish(kept, got, *shapes, after=()):
+    return call(finish_kernel, [(shape, F32) for shape in shapes], kept, got, after=after)
+
+
+def halve(kept, got, after=()):
     rows, width = kept.shape
-    return call(halve_kernel, [((rows // 2, width), BF16), ((rows // 2, width), F32)], kept, got)
+    return call(halve_kernel, [((rows // 2, width), BF16), ((rows // 2, width), F32)], kept, got, after=after)
+
+
+DUE = {
+    "grad_parts": "e3", "F far": "d3", "A far": "b2", "M far": "b3", "G far": "c1", "H far": "c2",
+    "E far": "c4", "K far": "grads enc_attn", "mlp_other": "c4", "out_kernel": "modulation",
+    "down grads": "b4", "down first": "c3", "down halved": "c4", "up grads": "c2",
+    "up first": "halve up", "attn grads": "c4", "mlp_part": "c2", "modulation": "finish attn",
+    "silu": "e3", "images": "halve up", "parts": "finish down",
+}
+DEC_ALONG_DP, ENC_ALONG_DP, ENC_ROWS = False, False, "FEK"
+TAIL = (
+    "modulation", "collect", "halve up", "grads enc_up", "grads enc_down", "finish down",
+    "halve attn", "grads enc_attn", "finish up", "halve enc_up", "halve enc_down", "finish attn",
+    "halve enc_attn", "finish enc_up", "finish enc_down", "finish enc_attn",
+)
+
+
+class Plan:
+    def __init__(self, net, features):
+        self.net, self.values, self.makers = net, {}, {}
+        self.ways = [net.nhi != 2 or along_dp for along_dp in (DEC_ALONG_DP, ENC_ALONG_DP)]
+        self.selects = tie(*(net.selection(features, way) for way in self.ways))
+
+    def put(self, name, *arrays):
+        self.values[name] = arrays
+
+    def later(self, name, maker):
+        self.makers[name] = maker
+
+    def get(self, name):
+        if name not in self.values:
+            with jax.named_scope(name.replace(" ", "_")):
+                self.put(name, *self.makers[name]())
+        return self.values[name]
+
+    def tick(self, point, *chain):
+        names = [n for n in DUE if DUE[n] == point and (n in self.values or n in self.makers)]
+        counts = [len(self.get(name)) for name in names]
+        tied = list(tie(*chain, *(a for name in names for a in self.get(name))))
+        chain, tied = tied[: len(chain)], tied[len(chain) :]
+        for name, count in zip(names, counts):
+            self.put(name, *tied[:count])
+            tied = tied[count:]
+        return chain[0] if len(chain) == 1 else chain
+
+    def place_rows(self, name, rows):
+        with jax.named_scope(name + "_far"):
+            own, far = self.net.gather(rows, self.ways[name in ENC_ROWS])
+        self.put(name + " own", own)
+        self.put(name + " far", far)
+        self.later(name + " core", lambda: (self.net.to_core(own),))
+        self.later(name + " both", lambda: (self.net.to_core(self.get(name + " far")[0]),))
+
+    def weight_grads(self, name, products, bundles, after=()):
+        enc = bundles[0] in ENC_ROWS
+        sets = [
+            tuple(self.get(bundle + kind)[0] for kind in (" own", " far", " core", " both"))
+            for bundle in bundles
+        ]
+        sent, kept = weight_grads(products, sets, self.selects[enc], after)
+        self.put(name + " grads", sent, kept)
+        self.later(
+            name + " first", lambda: (self.net.first_half(self.get(name + " grads")[0], self.ways[enc]),)
+        )
+        self.later(name + " halved", lambda: self.halved(name))
+        self.later(name + " last", lambda: (self.net.to_far(self.get(name + " halved")[0]),))
+        return sent
+
+    def halved(self, name, after=()):
+        (got,), (_, kept) = self.get(name + " first"), self.get(name + " grads")
+        return halve(kept, got, after)
+
+    def halve(self, name, after):
+        self.put(name + " halved", *self.halved(name, after))
+        return self.get(name + " halved")[0]
+
+    def ends(self, name):
+        return self.get(name + " halved")[1], self.get(name + " last")[0]
 
 
 def shards(
     net, enc_in, kept_pos, slot_live, condition, mask_token, enc_ada, enc_qkv, enc_proj, enc_up,
     enc_down, dec_ada, dec_qkv, dec_proj, dec_up, dec_down, cotangent,
 ):
-    net.place()
+    condition = net.place(condition)
     cap, features = enc_in.shape[1:]
     tokens = cotangent.shape[1]
     assert enc_in.shape[0] == 2
-    width, units = enc_proj.shape[0], enc_up.shape[1]
-    dec_way, enc_way = True, net.nhi != 2
-    dec_select, enc_select = net.selection(features, dec_way), net.selection(features, enc_way)
+    width, units, block = enc_proj.shape[0], enc_up.shape[1], enc_ada.shape[1]
+    plan = Plan(net, features)
     enc_qkv, dec_qkv = (
         jnp.transpose(a, (1, 2, 0)).reshape(3 * width, features) for a in (enc_qkv, dec_qkv)
     )
 
     code = jnp.where(slot_live > 0, kept_pos, -1).astype(BF16)
     sent = jnp.concatenate([enc_in, jnp.broadcast_to(code[..., None], code.shape + (128,))], axis=2)
-    slots = net.spread_images(sent)
+    slots = net.spread_images(net.spread_halves(sent))
+    grad_parts = net.spread_halves(cotangent)
+
+    silu = jax.nn.silu(condition.astype(F32)).astype(BF16)
+    silu = in_order(silu, net.to_core(silu), net.core_first).reshape(4, features)
+    cols = jnp.concatenate([dot(silu, enc_ada), dot(silu, dec_ada)], axis=1)
+    cols = cols.reshape(2, 2, 2 * block)
+    got = net.to_near(jnp.where(net.z0_first, cols[:, 1], cols[:, 0]))
+    got, *rest = tie(got, *slots, *grad_parts, *plan.selects)
+    slots, grad_parts, plan.selects = rest[:2], rest[2:4], rest[4:]
     code = jnp.concatenate([part[:, features] for part in slots]).astype(jnp.int32)
     place = jnp.arange(2 * tokens)
     matches = (place[:, None] // tokens == jnp.arange(2 * cap)[None, :] // cap) & (
         code[None, :] == place[:, None] % tokens
     )
     matches = matches.astype(F32)
-
-    silu = jax.nn.silu(condition.astype(F32)).astype(BF16)
-    silu = in_order(silu, net.to_core(silu), net.core).reshape(4, features)
-    cols = jnp.concatenate([dot(silu, enc_ada), dot(silu, dec_ada)], axis=1)
-    block = enc_ada.shape[1]
-    cols = cols.reshape(2, 2, 2 * block)
-    got = net.to_near(lax.dynamic_index_in_dim(cols, 1 - net.z0, 1, False))
-    got, *slots = tie(got, *slots)
-    cols = in_order(lax.dynamic_index_in_dim(cols, net.z0, 1, False), got, net.z0)
-    got = net.to_far(lax.dynamic_index_in_dim(cols, 1 - net.z1, 1, False))
-    cols = in_order(lax.dynamic_index_in_dim(cols, net.z1, 1, False), got, net.z1)
-    cols = in_order(cols, net.to_heads(cols), net.y)
+    cols = in_order(jnp.where(net.z0_first, cols[:, 0], cols[:, 1]), got, net.z0_first)
+    got = net.to_far(jnp.where(net.z1_first, cols[:, 1], cols[:, 0]))
+    got, matches, *grad_parts = tie(got, matches, *grad_parts)
+    cols = in_order(jnp.where(net.z1_first, cols[:, 0], cols[:, 1]), got, net.z1_first)
+    grad_parts = net.spread_images(grad_parts)
+    cols = in_order(cols, net.to_heads(cols), net.y_first)
     cols = jnp.moveaxis(cols, 0, 2).reshape(8, 2, block)
-    enc_mod = cols[:, 0].reshape(6, features)
-    dec_mod = cols[:, 1].reshape(6, features)
+    enc_mod, dec_mod = tie(cols[:, 0].reshape(6, features), cols[:, 1].reshape(6, features))
 
     def attention(q, kv, kv_other, proj, hidden, *more):
         rows = q.shape[0]
@@ -627,18 +789,21 @@
             dq, dkv, dkv_other, grad_branch, qkv,
         )
 
+    tick, place_rows = plan.tick, plan.place_rows
+
     rows = 2 * cap
+    plan.put("grad_parts", *grad_parts)
+    plan.later("silu", lambda: (net.gather_hi(silu).reshape(net.nhi * 4, features),))
+    enc_mod, dec_mod = tick("e1", enc_mod, dec_mod)
     x, hidden, q, kv = call(
         enc_qkv_kernel,
         [((rows, features), F32), ((rows, features), BF16), ((rows, width), BF16), ((rows, 2 * width + 128), BF16)],
         *slots, enc_mod, enc_qkv, late=(3,),
     )
-    cotangent, kv = tie(cotangent, kv)
-    kv_other = net.to_core(kv)
-    grad_parts = net.spread_images(cotangent)
+    kv_other = tick("e2", net.to_core(kv))
     enc_attn_rows, branch = attention(q, kv, kv_other, enc_proj, hidden)
     branch, up, down = load(branch, enc_up, enc_down)
-    branch_other = net.to_heads(branch)
+    branch_other = tick("e3", net.to_heads(branch))
     residual, pre, enc_rows, mlp_part = mlp(
         x, branch, branch_other, enc_mod, up, down, enc_attn_rows
     )
@@ -648,210 +813,175 @@
         x=x, q=q, kv=kv, kv_other=kv_other, branch=branch, branch_other=branch_other,
         residual=residual, pre=pre, mlp=mlp_part, mlp_other=mlp_other,
     )
-    enc_rows, enc_rows_far = net.gather(enc_rows, enc_way)
-    mlp_other, *grad_parts = tie(mlp_other, *grad_parts)
+    place_rows("F", enc_rows)
 
     rows = 2 * tokens
+    mlp_other = tick("d1", mlp_other)
     x, hidden, q, kv = call(
         dec_qkv_kernel,
         [((rows, features), F32), ((rows, features), BF16), ((rows, width), BF16), ((rows, 2 * width), BF16)],
         residual, mlp_part, mlp_other, enc_mod, matches, mask_token[None], dec_mod, qkv,
     )
-    kv_other = net.to_core(kv)
-    attn_rows, branch, grad_out = attention(q, kv, kv_other, dec_proj, hidden, *grad_parts, dec_mod)
+    kv_other = tick("d2", net.to_core(kv))
+    attn_rows, branch, grad_out = attention(
+        q, kv, kv_other, dec_proj, hidden, *plan.get("grad_parts"), dec_mod
+    )
     branch, up, down = load(branch, dec_up, dec_down)
     branch_other = net.to_heads(branch)
-    own_rows = attn_rows
-    attn_rows, attn_rows_far = net.gather(attn_rows, dec_way)
+    place_rows("A", attn_rows)
+    branch_other = tick("d3", branch_other)
     residual, pre, mlp_rows, mlp_part = mlp(x, branch, branch_other, dec_mod, up, down)
     dec = dict(
         x=x, q=q, kv=kv, kv_other=kv_other, branch=branch, branch_other=branch_other,
-        residual=residual, pre=pre,
-    )
-    mlp_rows, mlp_rows_far = net.gather(mlp_rows, dec_way)
-
-    mlp_other = net.to_heads(mlp_part)
-    pre, enc_rows_far = tie(pre, enc_rows_far)
+        residual=residual, pre=pre, grad_out=grad_out,
+    )
+    place_rows("M", mlp_rows)
+
+    pre, mlp_part = tick("b1", pre, mlp_part)
+    plan.put("mlp_part", mlp_part)
+    plan.later("mlp_other", lambda: (net.to_heads(plan.get("mlp_part")[0]),))
     grad_rows, part = call(
         dec_mlp_back_kernel, [((rows, units), BF16), ((rows, features), BF16)],
-        own_rows, pre, up, down,
-    )
-    part, mlp_other = tie(part, mlp_other)
+        attn_rows, pre, up, down,
+    )
+    part = tick("b1x", part)
     part, proj = load(part, dec_proj)
     other = net.to_heads(part)
-    grad_rows, grad_rows_far = net.gather(grad_rows, dec_way)
-    other, attn_rows_far = tie(other, attn_rows_far)
-    attn_rows = attn_rows, attn_rows_far, net.to_core(attn_rows), net.to_core(attn_rows_far)
-    dec_out, dec_gate = call(
-        out_kernel, [((rows, features), BF16), ((1, features), F32)],
-        residual, mlp_part, mlp_other, dec_mod, grad_out, late=(0, 1, 4),
-    )
-    out_parts = net.collect_parts([dec_out[:tokens], dec_out[tokens:]])
+    place_rows("G", grad_rows)
+    plan.later(
+        "out_kernel",
+        lambda: call(
+            out_kernel, [((tokens, features), BF16)] * 2 + [((1, features), F32)],
+            dec["residual"], *plan.get("mlp_part"), *plan.get("mlp_other"), dec_mod, dec["grad_out"],
+            late=(0, 1, 4),
+        ),
+    )
+    other = tick("b2", other)
     grad_residual, grad_branch, dq, dkv, dkv_other, dec_sums = attention_back(
         grad_out, part, other, dec, dec_mod, proj
     )
     dkv_other, qkv = load(dkv_other, dec_qkv)
-    dkv_other, mlp_rows_far, *rest = tie(
-        net.to_core(dkv_other), mlp_rows_far, *attn_rows, *out_parts
-    )
-    attn_rows, out_parts = rest[:4], rest[4:]
-    mlp_rows = mlp_rows, mlp_rows_far, net.to_core(mlp_rows), net.to_core(mlp_rows_far)
-    enc_rows = enc_rows, enc_rows_far, net.to_core(enc_rows), net.to_core(enc_rows_far)
+    dkv_other = tick("b3", net.to_core(dkv_other))
     grad_attn_rows, part = qkv_back(dq, dkv, dkv_other, grad_branch, qkv)
     part, up, down = load(part, enc_up, enc_down)
     other = net.to_heads(part)
-    grad_attn_rows, grad_attn_rows_far = net.gather(grad_attn_rows, dec_way)
-    down_sent, down_kept = weight_grads(
-        (((0, features), (1, 0, units)),), (attn_rows, mlp_rows), dec_select
-    )
-    down_got = net.first_half(down_sent, dec_way)
-    other, down_sent = tie(other, down_sent)
+    place_rows("H", grad_attn_rows)
+    plan.weight_grads("down", (((0, features), (1, 0, units)),), ("A", "M"))
+    other = tick("b4", other)
     grad_enc, dec_more = call(
         dec_end_kernel, [((2 * cap, features), F32), ((3, features), F32)],
         part, other, grad_residual, dec["x"], dec_mod, matches, late=(2, 3),
     )
 
     rows = 2 * cap
-    grad_out = grad_enc
+    grad_out = tick("c1", grad_enc)
     enc_grad_rows, part = call(
         enc_mlp_back_kernel, [((rows, units + features), BF16), ((rows, features), BF16)],
         grad_out, enc["pre"], enc_mod, up, down, late=(1,),
     )
-    part, grad_rows_far = tie(part, grad_rows_far)
-    grad_rows = grad_rows, grad_rows_far, net.to_core(grad_rows), net.to_core(grad_rows_far)
+    part = tick("c1x", part)
     part, proj = load(part, enc_proj)
     other = net.to_heads(part)
-    enc_grad_rows, enc_grad_rows_far = net.gather(enc_grad_rows, enc_way)
-    up_sent, up_kept = weight_grads(
-        (((0, units), (1, 0, units)),), (mlp_rows, grad_rows), dec_select
-    )
-    up_got = net.first_half(up_sent, dec_way)
-    other, up_sent, down_got, *enc_rows = tie(other, up_sent, down_got, *enc_rows)
-    down_sent, down_kept = halve(down_kept, down_got)
-    down_got = net.to_far(down_sent)
+    place_rows("E", enc_grad_rows)
+    plan.weight_grads("up", (((0, units), (1, 0, units)),), ("M", "G"))
+    other = tick("c2", other)
     grad_residual, grad_branch, dq, dkv, dkv_other, enc_sums = attention_back(
         grad_out, part, other, enc, enc_mod, proj
     )
     dkv_other, qkv = load(dkv_other, enc_qkv)
-    dkv_other, down_sent, enc_grad_rows_far, grad_attn_rows_far = tie(
-        net.to_core(dkv_other), down_sent, enc_grad_rows_far, grad_attn_rows_far
-    )
-    grad_attn_rows = (
-        grad_attn_rows, grad_attn_rows_far, net.to_core(grad_attn_rows), net.to_core(grad_attn_rows_far)
-    )
-    enc_grad_rows = (
-        enc_grad_rows, enc_grad_rows_far, net.to_core(enc_grad_rows), net.to_core(enc_grad_rows_far)
-    )
+    dkv_other = tick("c3", net.to_core(dkv_other))
     enc_grad_attn_rows, part = qkv_back(dq, dkv, dkv_other, grad_branch, qkv)
+    part = tick("c3x", part)
     other = net.to_heads(part)
-    enc_grad_attn_rows, enc_grad_attn_rows_far = net.gather(enc_grad_attn_rows, enc_way)
-    attn_sent, attn_kept = weight_grads(
-        (((0, 0), (1, features, 3 * width)), ((1, 0), (0, 2 * features, width))),
-        (attn_rows, grad_attn_rows), dec_select,
-    )
-    attn_got = net.first_half(attn_sent, dec_way)
-    other, attn_sent, up_got, down_got, *enc_grad_rows = tie(
-        other, attn_sent, up_got, down_got, *enc_grad_rows
-    )
-    grad_in, enc_more = call(
-        enc_end_kernel, [((2 * cap, features), BF16), ((3, features), F32)],
+    place_rows("K", enc_grad_attn_rows)
+    plan.weight_grads(
+        "attn", (((0, 0), (1, features, 3 * width)), ((1, 0), (0, 2 * features, width))),
+        ("A", "H"),
+    )
+    other = tick("c4", other)
+    *grad_in, enc_more = call(
+        enc_end_kernel, [((cap, features), BF16)] * 2 + [((3, features), F32)],
         part, other, grad_residual, enc["x"], enc_mod, grad_out, enc["mlp"], enc["mlp_other"],
         late=(2, 3, 6, 7),
     )
 
-    grad_in, up_got = tie(grad_in, up_got)
-    up_sent, up_kept = halve(up_kept, up_got)
-    up_got = net.to_far(up_sent)
-    up_sent, *enc_grad_rows = tie(up_sent, *enc_grad_rows)
-    enc_up_sent, enc_up_kept = weight_grads(
-        (((0, units), (1, 0, units)),), (enc_rows, enc_grad_rows), enc_select
-    )
-    enc_up_got = net.first_half(enc_up_sent, enc_way)
-    enc_up_sent, *enc_grad_rows = tie(enc_up_sent, *enc_grad_rows)
-    enc_down_sent, enc_down_kept = weight_grads(
-        (((1, units), (0, 0, units)),), (enc_rows, enc_grad_rows), enc_select
-    )
-    enc_down_got = net.first_half(enc_down_sent, enc_way)
-    enc_down_sent, enc_grad_attn_rows_far, attn_got = tie(
-        enc_down_sent, enc_grad_attn_rows_far, attn_got
-    )
-    enc_grad_attn_rows = (
-        enc_grad_attn_rows, enc_grad_attn_rows_far,
-        net.to_core(enc_grad_attn_rows), net.to_core(enc_grad_attn_rows_far),
-    )
-    attn_sent, attn_kept = halve(attn_kept, attn_got)
-    attn_sent, down_got = tie(attn_sent, down_got)
-    attn_got = net.to_far(attn_sent)
-    enc_attn_sent, enc_attn_kept = weight_grads(
+    products = dict(
+        enc_up=((((0, units), (1, 0, units)),), ("F", "E")),
+        enc_down=((((1, units), (0, 0, units)),), ("F", "E")),
+        enc_attn=(
+            (
+                ((0, units + features), (1, features, 3 * width)),
+                ((1, 0), (0, units + 2 * features, width)),
+            ),
+            ("F", "K"),
+        ),
+    )
+    share = features // (net.ndp * 4)
+    shapes = {name: ((share, units),) for name in ("down", "up", "enc_down", "enc_up")}
+    shapes["attn"] = shapes["enc_attn"] = ((3, share, width), (share, width))
+    grads = {}
+    chunk = features // 4
+    assert 3 * chunk == block
+    message = (2, 2 * 3 + 4, chunk)
+
+    def modulation_rows(sums):
+        sent, kept = call(
+            columns_kernel, [(message, F32)] * 2, sums, net.to_core(sums), net.flags
+        )
+        sent, kept = call(images_kernel, [(message, F32)] * 2, kept, net.to_near(sent), net.flags)
+        return call(
+            all_images_kernel, [((4,) + message[1:], F32)], kept, net.to_far(sent), net.flags
+        )
+
+    plan.later(
+        "modulation",
+        lambda: (net.gather_hi(plan.get("images")[0]).reshape(net.nhi * 4, *message[1:]),),
+    )
+
+    last = enc_more
+    for step in TAIL:
+        kind, _, name = step.partition(" ")
+        last = tick(step, last)
+        if kind == "grads":
+            last = plan.weight_grads(name, *products[name], after=(last,))
+        elif kind == "halve":
+            last = plan.halve(name, after=(last,))
+        elif kind == "finish":
+            grads[name] = finish(*plan.ends(name), *shapes[name], after=(last,))
+            last = grads[name][0]
+        elif step == "collect":
+            last, *grad_in = tie(last, *grad_in)
+            plan.later("parts", functools.partial(net.collect_parts, [
+                jnp.concatenate([a, b]) for a, b in zip(plan.get("out_kernel")[:2], grad_in)
+            ]))
+        else:
+            (vector,) = call(
+                sums_kernel, [((13, features), F32)],
+                enc_more, enc_sums, dec_more, dec_sums, plan.get("out_kernel")[2], after=(last,),
+            )
+            last = vector
+            plan.later("images", functools.partial(modulation_rows, vector))
+
+    both = plan.get("parts")
+    out = net.collected([part[:tokens] for part in both])
+    input_grad = net.collected([part[tokens:] for part in both]).astype(F32)
+    enc_grads, dec_grads = (
         (
-            ((0, units + features), (1, features, 3 * width)),
-            ((1, 0), (0, units + 2 * features, width)),
-        ),
-        (enc_rows, enc_grad_attn_rows), enc_select,
-    )
-    enc_attn_got = net.first_half(enc_attn_sent, enc_way)
-    enc_up_got, enc_attn_sent = tie(enc_up_got, enc_attn_sent)
-    enc_up_sent, enc_up_kept = halve(enc_up_kept, enc_up_got)
-    enc_up_sent, up_got = tie(enc_up_sent, up_got)
-    enc_up_got = net.to_far(enc_up_sent)
-    grad_in, enc_sums, enc_more, enc_up_sent = tie(grad_in, enc_sums, enc_more, enc_up_sent)
-    grad_in_parts = net.collect_parts([grad_in[:cap], grad_in[cap:]])
-    enc_down_sent, enc_down_kept = halve(enc_down_kept, enc_down_got)
-    enc_down_sent, attn_got = tie(enc_down_sent, attn_got)
-    enc_down_got = net.to_far(enc_down_sent)
-    enc_attn_sent, enc_attn_kept = halve(enc_attn_kept, enc_attn_got)
-    enc_attn_sent, enc_up_got, *grad_in_parts = tie(enc_attn_sent, enc_up_got, *grad_in_parts)
-    enc_attn_got = net.to_far(enc_attn_sent)
-
-    out = net.collected(out_parts)
-    input_grad = net.collected(grad_in_parts).astype(F32)
-    mask_part = dec_more[2]
-
-    enc_mod_grad, dec_mod_grad = (
-        jnp.concatenate([more[0], more[1], sums[2], sums[0], sums[1], gate])
-        for more, sums, gate in ((enc_more, enc_sums, enc_more[2]), (dec_more, dec_sums, dec_gate[0]))
-    )
-
-    share = features // (net.ndp * 4)
-
-    def attn_outs(kept, got):
-        qkv_grad, proj_grad = finish(kept, got, (3, share, width), (share, width))
-        return jnp.transpose(qkv_grad, (1, 0, 2)), proj_grad.T
-
-    def mlp_outs(up_kept, up_got, down_kept, down_got):
-        return (
-            finish(up_kept, up_got, (share, units))[0], finish(down_kept, down_got, (share, units))[0].T
+            jnp.transpose(grads[prefix + "attn"][0], (1, 0, 2)), grads[prefix + "attn"][1].T,
+            grads[prefix + "up"][0], grads[prefix + "down"][0].T,
         )
-
-    enc_grads = attn_outs(enc_attn_kept, enc_attn_got) + mlp_outs(
-        enc_up_kept, enc_up_got, enc_down_kept, enc_down_got
-    )
-    dec_grads = attn_outs(attn_kept, attn_got) + mlp_outs(up_kept, up_got, down_kept, down_got)
-
-    vector = jnp.concatenate([enc_mod_grad, dec_mod_grad, mask_part])
-    vector = vector + net.to_core(vector)
-    split = 6 * features
-    own = features // (net.ndp * 4)
-    rows = jnp.concatenate(
-        [
-            lax.dynamic_index_in_dim(vector[:split].reshape(4, 2, block), net.y, 1, False),
-            lax.dynamic_index_in_dim(vector[split : 2 * split].reshape(4, 2, block), net.y, 1, False),
-            jnp.moveaxis(vector[2 * split :].reshape(net.ndp, 4, own), 0, 1).reshape(4, -1),
-        ],
-        axis=1,
-    )
-    rows = rows.reshape(2, 2, -1)
-    got = net.to_near(lax.dynamic_index_in_dim(rows, 1 - net.z0, 1, False))
-    rows = in_order(lax.dynamic_index_in_dim(rows, net.z0, 1, False), got, net.z0)
-    got = net.to_far(lax.dynamic_index_in_dim(rows, 1 - net.z1, 1, False))
-    rows = in_order(lax.dynamic_index_in_dim(rows, net.z1, 1, False), got, net.z1)
-    rows = net.gather_hi(rows.reshape(4, -1)).reshape(net.nhi * 4, -1)
-    silu_all = net.gather_hi(silu).reshape(net.nhi * 4, features)
-    share = features // net.ndp
-    silu_own = lax.dynamic_slice_in_dim(silu_all, net.dp * share, share, 1)
-    enc_ada_grad = dot(silu_own, rows[:, :block].astype(BF16), TN)
-    dec_ada_grad = dot(silu_own, rows[:, block : 2 * block].astype(BF16), TN)
-    mask_grad = lax.dynamic_slice_in_dim(jnp.sum(rows[:, 2 * block :], axis=0), net.dp * own, own, 0)
+        for prefix in ("enc_", "")
+    )
+
+    (rows,) = plan.get("modulation")
+    (silu_all,) = plan.get("silu")
+    silu_own = lax.dynamic_slice_in_dim(silu_all, net.dp * (4 * share), 4 * share, 1)
+    enc_ada_grad, dec_ada_grad, mask_sum = call(
+        ada_kernel, [((4 * share, block), F32)] * 2 + [((4, chunk), F32)], rows, silu_own
+    )
+    mask_grad = lax.dynamic_slice_in_dim(
+        mask_sum.reshape(-1), (net.dp * 4 + net.z) * share, share, 0
+    )
     return (out, input_grad, mask_grad, enc_ada_grad) + enc_grads + (dec_ada_grad,) + dec_grads
 
 def solution(mesh):

time: 318 us -> 295 us (0.928)
  local copies, waits for them, and re-layouts: 29.3 us -> 17.9 us
  matrix products: 5.49 us -> 1.24 us
  waiting for transfers between devices: 111 us -> 107 us
    ppermute x8 -> x9, waiting for transfers between devices: 42.5 us -> 19.7 us  [to_near(): return lax.ppermute(a, 'region', self.near)]
    ppermute x8, waiting for transfers between devices: 32.8 us -> 51.7 us  [to_far(): return lax.ppermute(a, 'region', self.far)]
    ppermute x8, starting transfers between devices: 14.4 us -> 5.28 us  [to_far(): return lax.ppermute(a, 'region', self.far)]
    unnamed x185 -> x148, local copies, waits for them, and re-layouts: 23.5 us -> 16.2 us
    ppermute x4 -> x2, waiting for transfers between devices: 5.76 us -> 0.01 us  [collect_parts(): lax.ppermute(part, ('dp', 'region'), [(t, s) for s, t in perm])]
    ppermute x9 -> x8, waiting for transfers between devices: 10.9 us -> 15.9 us  [to_hi(): return lax.ppermute(a, 'dp', [(d, d ^ 2) for d in range(self.ndp)])]
    ppermute x20, starting transfers between devices: 8.48 us -> 13.3 us  [to_core(): return lax.ppermute(a, 'dp', self.core_perm)]
    dot_general x4 -> x2, matrix products: 5.49 us -> 1.24 us  [dot(): lax.dot_general(a, b, (dims, ((), ())), preferred_element_type=F32, **kw)]
  transfers between devices with their start and end apart: 62 -> 60, of which waited for: 23 -> 28; matrix products, arithmetic and copies ran while one was open for 6% -> 3% of each run, Pallas kernels for 30% -> 31%
where the time goes in v2:
time: 295 us; the launch traced here: 291 us
  waiting for transfers between devices  107 us (36%)
  Pallas kernels  94.7 us (32%)
  starting transfers between devices  60 us (20%)
  local copies, waits for them, and re-layouts  17.9 us (6%)
  other arithmetic  7.48 us (3%)
    pallas_call x32, Pallas kernels, call(): pl.pallas_call(body, out_shape=shapes, in_specs=[hbm if i in late else vm...  54 us
    ppermute x8, waiting for transfers between devices, to_far(): return lax.ppermute(a, 'region', self.far)  51.7 us
    pallas_call x8, Pallas kernels, load(): pl.pallas_call(load_kernel, out_shape=[jax.ShapeDtypeStruct(w.shape, w.dt...  21.4 us
    ppermute x9, waiting for transfers between devices, to_near(): return lax.ppermute(a, 'region', self.near)  19.7 us
    pallas_call x6, Pallas kernels, weight_grads(): pl.pallas_call(functools.partial(weight_grad_kernel, products, len(after)...  19.3 us
    unnamed x148, local copies, waits for them, and re-layouts  16.2 us
    ppermute x8, waiting for transfers between devices, to_hi(): return lax.ppermute(a, 'dp', [(d, d ^ 2) for d in range(self.ndp)])  15.9 us
    ppermute x9, waiting for transfers between devices, to_heads(): return lax.ppermute(a, 'heads', [(0, 1), (1, 0)])  15.7 us
  transfers between devices with their start and end apart: 60, of which 28 were waited for; matrix products, arithmetic and copies ran while one was open for 3% of the time, Pallas kernels for 31%

profile of v2, /device:TPU:0, one launch (start us, length us, event | category | flops | bytes accessed | tf_op | source)
XLA Modules:
  0.0 290.8 jit_solution(6663972717651686418)
XLA Ops:
  3.5 3.1 %collective-permute-start.3 = (bf16[48,1280]{1,0:T(8,128)(2,1)S(1)}, bf16[48,1280]{1,0:T(8,128)(2,1)S(1)}, u32[]{:S(2)}, u32[]{:S(2)}) collective-permute-start(bf16[48,1280]{1,0:T(8,128)(2,1)S(1)} %get-tuple-element.383), channel_id=1, source_target_pairs={{0,2},{2,0},{4,10},{6,8},{8,6},{10,4},{12,14},{14,12},{16,18},{18,... | collective-permute-start | bytes 368648 | tf_op jit(solution)/shard_map/spread/ppermute | solution.py:557
  7.3 3.5 %collective-permute-start = (bf16[2,1152]{1,0:T(2,128)(2,1)S(1)}, bf16[2,1152]{1,0:T(2,128)(2,1)S(1)}, u32[]{:S(2)}, u32[]{:S(2)}) collective-permute-start(bf16[2,1152]{1,0:T(2,128)(2,1)S(1)} %fusion.8), channel_id=1, source_target_pairs={{0,8},{8,0},{16,24},{24,16},{1,9},{9,1},{17,25},{25,17},{2,10},{10... | collective-permute-start | bytes 13832 | tf_op jit(solution)/shard_map/core/ppermute | solution.py:523
  16.5 3.1 %collective-permute-done.1 = f32[2,1728]{1,0:T(2,128)S(1)} collective-permute-done((f32[2,1728]{1,0:T(2,128)S(1)}, f32[2,1728]{1,0:T(2,128)S(1)}, u32[]{:S(2)}, u32[]{:S(2)}) %collective-permute-start.1) | collective-permute-done | bytes 13856 | tf_op jit(solution)/shard_map/near/ppermute | solution.py:527
  21.7 2.8 collective-permute-done.4
  29.2 3.6 %enc_qkv_kernel.1 = (f32[96,1152]{1,0:T(8,128)S(1)}, bf16[96,1152]{1,0:T(8,128)(2,1)S(1)}, bf16[96,576]{1,0:T(8,128)(2,1)S(1)}, bf16[96,1280]{1,0:T(8,128)(2,1)S(1)}) custom-call(bf16[48,1280]{1,0:T(8,128)(2,1)S(1)} %collective-permute-done.2.refs_0_, bf16[48,1280]{1,0:T(8,128)(2,1)S(1)} %collective-permute-done.3.refs_1_, ...), custom_call_target="tpu_custom_call" | custom-call | tf_op jit(solution)/shard_map/enc_qkv_kernel/pallas_call | solution.py:58
  39.0 4.1 %load.8 = (bf16[1152,2304]{1,0:T(8,128)(2,1)S(1)}, bf16[2304,1152]{1,0:T(8,128)(2,1)S(1)}) custom-call(bf16[1152,2304]{1,0:T(8,128)(2,1)} %refs_0_.3, bf16[2304,1152]{1,0:T(8,128)(2,1)} %refs_1_.2), custom_call_target="tpu_custom_call" | custom-call | tf_op jit(solution)/shard_map/load/pallas_call | solution.py:94
  52.2 4.3 %collective-permute-done.11.refs_2_.refs_7_ = bf16[96,1152]{1,0:T(8,128)(2,1)S(1)} collective-permute-done((bf16[96,1152]{1,0:T(8,128)(2,1)S(1)}, bf16[96,1152]{1,0:T(8,128)(2,1)S(1)}, u32[]{:S(2)}, u32[]{:S(2)}) %collective-permute-start.11) | collective-permute-done | bytes 221216 | tf_op jit(solution)/shard_map/heads/ppermute | solution.py:535
  60.6 2.4 attention_kernel.3
  64.8 4.1 %load.10 = (bf16[1152,2304]{1,0:T(8,128)(2,1)S(1)}, bf16[2304,1152]{1,0:T(8,128)(2,1)S(1)}) custom-call(bf16[1152,2304]{1,0:T(8,128)(2,1)} %refs_0_.1, bf16[2304,1152]{1,0:T(8,128)(2,1)} %refs_1_.1), custom_call_target="tpu_custom_call" | custom-call | tf_op jit(solution)/shard_map/load/pallas_call | solution.py:94
  68.9 3.5 %collective-permute-done.13.refs_2_.refs_5_ = bf16[128,1152]{1,0:T(8,128)(2,1)S(1)} collective-permute-done((bf16[128,1152]{1,0:T(8,128)(2,1)S(1)}, bf16[128,1152]{1,0:T(8,128)(2,1)S(1)}, u32[]{:S(2)}, u32[]{:S(2)}) %collective-permute-start.13) | collective-permute-done | bytes 294944 | tf_op jit(solution)/shard_map/heads/ppermute | solution.py:535
  75.9 3.3 %dec_mlp_back_kernel.1 = (bf16[128,2304]{1,0:T(8,128)(2,1)S(1)}, bf16[128,1152]{1,0:T(8,128)(2,1)S(1)}) custom-call(bf16[128,2944]{1,0:T(8,128)(2,1)S(1)} %get-tuple-element.241.refs_0_, f32[128,2304]{1,0:T(8,128)S(1)} %get-tuple-element.250.refs_1_, bf16[1152,2304]{1,0:T(8,128)(2,1)S(1)} %get-tuple-element.246.refs_4_.refs_2_, ...), custom_call_target="tpu_custom_call" | custom-call | tf_op jit(solution)/shard_map/dec_mlp_back_kernel/pallas_call | solution.py:58
  82.7 4.1 %collective-permute-done.18.refs_1_ = bf16[128,2944]{1,0:T(8,128)(2,1)S(1)} collective-permute-done((bf16[128,2944]{1,0:T(8,128)(2,1)S(1)}, bf16[128,2944]{1,0:T(8,128)(2,1)S(1)}, u32[]{:S(2)}, u32[]{:S(2)}) %collective-permute-start.18) | collective-permute-done | bytes 753696 | tf_op jit(solution)/shard_map/A_far/near/ppermute | solution.py:527
  86.8 2.4 collective-permute-done.17.refs_2_
  89.1 5.2 %attention_back_kernel.2 = (f32[128,1152]{1,0:T(8,128)S(1)}, bf16[128,1152]{1,0:T(8,128)(2,1)S(1)}, bf16[128,576]{1,0:T(8,128)(2,1)S(1)}, f32[128,1152]{1,0:T(8,...) custom-call(bf16[128,1152]{1,0:T(8,128)(2,1)S(1)} %get-tuple-element.240.refs_0_.refs_4_, ...), custom_call_target="tpu_custom_call" | custom-call | tf_op jit(solution)/shard_map/attention_back_kernel/pallas_call | solution.py:58
  97.5 8.2 %collective-permute-done.20.refs_5_.refs_1_ = bf16[128,3456]{1,0:T(8,128)(2,1)S(1)} collective-permute-done((bf16[128,3456]{1,0:T(8,128)(2,1)S(1)}, bf16[128,3456]{1,0:T(8,128)(2,1)S(1)}, u32[]{:S(2)}, u32[]{:S(2)}) %collective-permute-start.20) | collective-permute-done | bytes 884768 | tf_op jit(solution)/shard_map/M_far/near/ppermute | solution.py:527
  115.5 2.9 weight_grads.6
  125.1 4.1 %load.13 = (bf16[1152,2304]{1,0:T(8,128)(2,1)S(1)}, bf16[2304,1152]{1,0:T(8,128)(2,1)S(1)}) custom-call(bf16[1152,2304]{1,0:T(8,128)(2,1)} %refs_0_.3, bf16[2304,1152]{1,0:T(8,128)(2,1)} %refs_1_.2), custom_call_target="tpu_custom_call" | custom-call | tf_op jit(solution)/shard_map/load/pallas_call | solution.py:94
  129.2 4.8 %enc_mlp_back_kernel.1 = (bf16[96,3456]{1,0:T(8,128)(2,1)S(1)}, bf16[96,1152]{1,0:T(8,128)(2,1)S(1)}) custom-call(f32[96,1152]{1,0:T(8,128)S(1)} %get-tuple-element.275.refs_0_.refs_5_, f32[96,2304]{1,0:T(8,128)} %copy-done.27, f32[6,1152]{1,0:T(8,128)S(1)} %reshape_squeeze.6.refs_2_.refs_3_.refs_6_.refs_4_, ...), custom_call_target="tpu_custom_call" | custom-call | tf_op jit(solution)/shard_map/enc_mlp_back_kernel/pallas_call | solution.py:58
  136.7 2.9 weight_grads.7
  144.9 4.8 %attention_back_kernel.3 = (f32[96,1152]{1,0:T(8,128)S(1)}, bf16[96,1152]{1,0:T(8,128)(2,1)S(1)}, bf16[96,576]{1,0:T(8,128)(2,1)S(1)}, f32[96,1152]{1,0:T(8,128)...) custom-call(f32[96,1152]{1,0:T(8,128)S(1)} %get-tuple-element.275.refs_0_.refs_5_, ...), custom_call_target="tpu_custom_call" | custom-call | tf_op jit(solution)/shard_map/attention_back_kernel/pallas_call | solution.py:58
  161.3 3.8 %weight_grads.8 = (bf16[144,2304]{1,0:T(8,128)(2,1)S(1)}, f32[144,2304]{1,0:T(8,128)S(1)}) custom-call(bf16[128,2944]{1,0:T(8,128)(2,1)} %copy-done.3, bf16[128,2944]{1,0:T(8,128)(2,1)} %copy-done.56, bf16[128,2944]{1,0:T(8,128)(2,1)} %copy-done.57, bf16[128,2944]{1,0:T(8,128)(2,1)} %copy-done.58, bf16[128,2944]{1,0:T(8,128)(2,1)} %copy-done.30, ...), custom_call_target="tpu_custom_call" | custom-call | tf_op jit(solution)/shard_map/weight_grads/pallas_call | solution.py:607
  178.8 15.5 %collective-permute-done.43.refs_1_ = f32[2,10,288]{2,1,0:T(8,128)S(1)} collective-permute-done((f32[2,10,288]{2,1,0:T(8,128)S(1)}, f32[2,10,288]{2,1,0:T(8,128)S(1)}, u32[]{:S(2)}, u32[]{:S(2)}) %collective-permute-start.43) | collective-permute-done | bytes 23072 | tf_op jit(solution)/shard_map/images/far/ppermute | solution.py:531
  197.8 3.0 %weight_grads.9 = (bf16[144,2304]{1,0:T(8,128)(2,1)S(1)}, f32[144,2304]{1,0:T(8,128)S(1)}) custom-call(bf16[96,5248]{1,0:T(8,128)(2,1)} %copy-done.2, bf16[96,5248]{1,0:T(8,128)(2,1)} %copy-done.50, bf16[96,5248]{1,0:T(8,128)(2,1)} %copy-done.51, bf16[96,5248]{1,0:T(8,128)(2,1)} %copy-done.52, bf16[96,3456]{1,0:T(8,128)(2,1)} %copy-done.11, ...), custom_call_target="tpu_custom_call" | custom-call | tf_op jit(solution)/shard_map/weight_grads/pallas_call | solution.py:607
  201.9 3.0 %weight_grads.10 = (bf16[144,2304]{1,0:T(8,128)(2,1)S(1)}, f32[144,2304]{1,0:T(8,128)S(1)}) custom-call(bf16[96,5248]{1,0:T(8,128)(2,1)} %copy-done.2, bf16[96,5248]{1,0:T(8,128)(2,1)} %copy-done.50, bf16[96,5248]{1,0:T(8,128)(2,1)} %copy-done.51, bf16[96,5248]{1,0:T(8,128)(2,1)} %copy-done.52, bf16[96,3456]{1,0:T(8,128)(2,1)} %copy-done.11, ...), custom_call_target="tpu_custom_call" | custom-call | tf_op jit(solution)/shard_map/weight_grads/pallas_call | solution.py:607
  205.0 2.5 collective-permute-start.52
  213.2 4.0 %collective-permute-done.54 = f32[4,10,288]{2,1,0:T(8,128)S(1)} collective-permute-done((f32[4,10,288]{2,1,0:T(8,128)S(1)}, f32[4,10,288]{2,1,0:T(8,128)S(1)}, u32[]{:S(2)}, u32[]{:S(2)}) %collective-permute-start.54) | collective-permute-done | bytes 46112 | tf_op jit(solution)/shard_map/modulation/hi/ppermute | solution.py:539
  220.7 3.8 %weight_grads.11 = (bf16[144,2304]{1,0:T(8,128)(2,1)S(1)}, f32[144,2304]{1,0:T(8,128)S(1)}) custom-call(bf16[96,5248]{1,0:T(8,128)(2,1)} %copy-done.2, bf16[96,5248]{1,0:T(8,128)(2,1)} %copy-done.50, bf16[96,5248]{1,0:T(8,128)(2,1)} %copy-done.51, bf16[96,5248]{1,0:T(8,128)(2,1)} %copy-done.52, bf16[96,2944]{1,0:T(8,128)(2,1)} %get-tuple-element.346.refs_4_, ...), custom_call_target="tpu_custom_call" | custom-call | tf_op jit(solution)/shard_map/weight_grads/pallas_call | solution.py:607
  225.2 12.5 %collective-permute-done.48.refs_1_ = bf16[72,2304]{1,0:T(8,128)(2,1)S(1)} collective-permute-done((bf16[72,2304]{1,0:T(8,128)(2,1)}, bf16[72,2304]{1,0:T(8,128)(2,1)S(1)}, u32[]{:S(2)}, u32[]{:S(2)}) %collective-permute-start.48) | collective-permute-done | bytes 331808 | tf_op jit(solution)/shard_map/up_last/far/ppermute | solution.py:531
  240.5 9.2 %collective-permute-done.46.refs_1_ = bf16[144,2304]{1,0:T(8,128)(2,1)S(1)} collective-permute-done((bf16[144,2304]{1,0:T(8,128)(2,1)S(1)}, bf16[144,2304]{1,0:T(8,128)(2,1)S(1)}, u32[]{:S(2)}, u32[]{:S(2)}) %collective-permute-start.46) | collective-permute-done | bytes 663584 | tf_op jit(solution)/shard_map/enc_down_first/hi/ppermute | solution.py:539
  250.8 8.2 %collective-permute-done.56.refs_1_ = bf16[72,2304]{1,0:T(8,128)(2,1)S(1)} collective-permute-done((bf16[72,2304]{1,0:T(8,128)(2,1)}, bf16[72,2304]{1,0:T(8,128)(2,1)S(1)}, u32[]{:S(2)}, u32[]{:S(2)}) %collective-permute-start.56) | collective-permute-done | bytes 331808 | tf_op jit(solution)/shard_map/attn_last/far/ppermute | solution.py:531
  271.8 8.7 %collective-permute-done.58.refs_1_ = bf16[72,2304]{1,0:T(8,128)(2,1)} collective-permute-done((bf16[72,2304]{1,0:T(8,128)(2,1)}, bf16[72,2304]{1,0:T(8,128)(2,1)}, u32[]{:S(2)}, u32[]{:S(2)}) %collective-permute-start.58) | collective-permute-done | bytes 331808 | tf_op jit(solution)/shard_map/enc_down_last/far/ppermute | solution.py:531
  283.6 3.9 %collective-permute-done.57.refs_1_ = bf16[72,2304]{1,0:T(8,128)(2,1)} collective-permute-done((bf16[72,2304]{1,0:T(8,128)(2,1)}, bf16[72,2304]{1,0:T(8,128)(2,1)}, u32[]{:S(2)}, u32[]{:S(2)}) %collective-permute-start.57) | collective-permute-done | bytes 331808 | tf_op jit(solution)/shard_map/enc_attn_last/far/ppermute | solution.py:531
  (340 shorter events, 133.2 us)
Async XLA Ops:
  2.8 16.8 %collective-permute-start.2 = (bf16[48,1280]{1,0:T(8,128)(2,1)S(1)}, bf16[48,1280]{1,0:T(8,128)(2,1)S(1)}, u32[]{:S(2)}, u32[]{:S(2)}) collective-permute-start(bf16[48,1280]{1,0:T(8,128)(2,1)S(1)} %get-tuple-element.384), channel_id=1, source_target_pairs={{0,0},{2,2},{4,8},{6,10},{8,4},{10,6},{12,12},{14,14},{16,16},{18,... | collective-permute-start | bytes 368648 | tf_op jit(solution)/shard_map/spread/ppermute | solution.py:557
  3.5 16.2 %collective-permute-start.3 = (bf16[48,1280]{1,0:T(8,128)(2,1)S(1)}, bf16[48,1280]{1,0:T(8,128)(2,1)S(1)}, u32[]{:S(2)}, u32[]{:S(2)}) collective-permute-start(bf16[48,1280]{1,0:T(8,128)(2,1)S(1)} %get-tuple-element.383), channel_id=1, source_target_pairs={{0,2},{2,0},{4,10},{6,8},{8,6},{10,4},{12,14},{14,12},{16,18},{18,... | collective-permute-start | bytes 368648 | tf_op jit(solution)/shard_map/spread/ppermute | solution.py:557
  46.8 25.7 %collective-permute-start.14 = (bf16[96,5248]{1,0:T(8,128)(2,1)S(1)}, bf16[96,5248]{1,0:T(8,128)(2,1)S(1)}, u32[]{:S(2)}, u32[]{:S(2)}) collective-permute-start(bf16[96,5248]{1,0:T(8,128)(2,1)S(1)} %get-tuple-element.225.refs_0_), channel_id=1, source_target_pairs={{0,2},{2,0},{4,6},{6,4},{1,3},{3,1},{5,7},{7,5},{8,10},{10,8},{12,... | collective-permute-start | bytes 3022856 | tf_op jit(solution)/shard_map/F_far/near/ppermute | solution.py:527
  64.6 22.2 %collective-permute-start.18 = (bf16[128,2944]{1,0:T(8,128)(2,1)S(1)}, bf16[128,2944]{1,0:T(8,128)(2,1)S(1)}, u32[]{:S(2)}, u32[]{:S(2)}) collective-permute-start(bf16[128,2944]{1,0:T(8,128)(2,1)S(1)} %get-tuple-element.241.refs_0_), channel_id=1, source_target_pairs={{0,2},{2,0},{4,6},{6,4},{1,3},{3,1},{5,7},{7,5},{8,10},{10,8},{12,... | collective-permute-start | bytes 2261000 | tf_op jit(solution)/shard_map/A_far/near/ppermute | solution.py:527
  75.3 30.5 %collective-permute-start.20 = (bf16[128,3456]{1,0:T(8,128)(2,1)S(1)}, bf16[128,3456]{1,0:T(8,128)(2,1)S(1)}, u32[]{:S(2)}, u32[]{:S(2)}) collective-permute-start(bf16[128,3456]{1,0:T(8,128)(2,1)S(1)} %get-tuple-element.260.refs_4_.refs_0_), channel_id=1, source_target_pairs={{0,2},{2,0},{4,6},{6,4},{1,3},{3,1},{5,7},{7,5},{8,10},{10,8},{12,... | collective-permute-start | bytes 2654216 | tf_op jit(solution)/shard_map/M_far/near/ppermute | solution.py:527
  96.3 17.0 %collective-permute-start.24 = (bf16[128,3456]{1,0:T(8,128)(2,1)S(1)}, bf16[128,3456]{1,0:T(8,128)(2,1)S(1)}, u32[]{:S(2)}, u32[]{:S(2)}) collective-permute-start(bf16[128,3456]{1,0:T(8,128)(2,1)S(1)} %get-tuple-element.260.refs_4_.refs_0_), channel_id=1, source_target_pairs={{0,8},{8,0},{16,24},{24,16},{1,9},{9,1},{17,25},{25,17},{2,10},{10... | collective-permute-start | bytes 2654216 | tf_op jit(solution)/shard_map/M_core/core/ppermute | solution.py:523
  96.3 15.3 %collective-permute-start.22 = (bf16[128,2944]{1,0:T(8,128)(2,1)S(1)}, bf16[128,2944]{1,0:T(8,128)(2,1)S(1)}, u32[]{:S(2)}, u32[]{:S(2)}) collective-permute-start(bf16[128,2944]{1,0:T(8,128)(2,1)S(1)} %get-tuple-element.241.refs_0_), channel_id=1, source_target_pairs={{0,8},{8,0},{16,24},{24,16},{1,9},{9,1},{17,25},{25,17},{2,10},{10... | collective-permute-start | bytes 2261000 | tf_op jit(solution)/shard_map/A_core/core/ppermute | solution.py:523
  96.8 16.6 %collective-permute-start.23 = (bf16[128,2944]{1,0:T(8,128)(2,1)S(1)}, bf16[128,2944]{1,0:T(8,128)(2,1)S(1)}, u32[]{:S(2)}, u32[]{:S(2)}) collective-permute-start(bf16[128,2944]{1,0:T(8,128)(2,1)S(1)} %collective-permute-done.18.refs_1_), channel_id=1, source_target_pairs={{0,8},{8,0},{16,24},{24,16},{1,9},{9,1},{17,25},{25,17},{2,10},{10... | collective-permute-start | bytes 2261000 | tf_op jit(solution)/shard_map/A_both/core/ppermute | solution.py:523
  106.9 16.2 %collective-permute-start.26 = (bf16[128,2304]{1,0:T(8,128)(2,1)S(1)}, bf16[128,2304]{1,0:T(8,128)(2,1)S(1)}, u32[]{:S(2)}, u32[]{:S(2)}) collective-permute-start(bf16[128,2304]{1,0:T(8,128)(2,1)S(1)} %get-tuple-element.274.refs_4_), channel_id=1, source_target_pairs={{0,2},{2,0},{4,6},{6,4},{1,3},{3,1},{5,7},{7,5},{8,10},{10,8},{12,... | collective-permute-start | bytes 1769480 | tf_op jit(solution)/shard_map/G_far/near/ppermute | solution.py:527
  113.3 20.8 %collective-permute-start.29 = (bf16[128,2304]{1,0:T(8,128)(2,1)S(1)}, bf16[128,2304]{1,0:T(8,128)(2,1)S(1)}, u32[]{:S(2)}, u32[]{:S(2)}) collective-permute-start(bf16[128,2304]{1,0:T(8,128)(2,1)S(1)} %get-tuple-element.274.refs_4_), channel_id=1, source_target_pairs={{0,8},{8,0},{16,24},{24,16},{1,9},{9,1},{17,25},{25,17},{2,10},{10... | collective-permute-start | bytes 1769480 | tf_op jit(solution)/shard_map/G_core/core/ppermute | solution.py:523
  113.4 26.2 %collective-permute-start.28 = (bf16[128,2944]{1,0:T(8,128)(2,1)S(1)}, bf16[128,2944]{1,0:T(8,128)(2,1)S(1)}, u32[]{:S(2)}, u32[]{:S(2)}) collective-permute-start(bf16[128,2944]{1,0:T(8,128)(2,1)S(1)} %get-tuple-element.284.refs_4_), channel_id=1, source_target_pairs={{0,2},{2,0},{4,6},{6,4},{1,3},{3,1},{5,7},{7,5},{8,10},{10,8},{12,... | collective-permute-start | bytes 2261000 | tf_op jit(solution)/shard_map/H_far/near/ppermute | solution.py:527
  123.1 20.1 %collective-permute-start.36 = (bf16[128,2944]{1,0:T(8,128)(2,1)S(1)}, bf16[128,2944]{1,0:T(8,128)(2,1)S(1)}, u32[]{:S(2)}, u32[]{:S(2)}) collective-permute-start(bf16[128,2944]{1,0:T(8,128)(2,1)S(1)} %get-tuple-element.284.refs_4_), channel_id=1, source_target_pairs={{0,8},{8,0},{16,24},{24,16},{1,9},{9,1},{17,25},{25,17},{2,10},{10... | collective-permute-start | bytes 2261000 | tf_op jit(solution)/shard_map/H_core/core/ppermute | solution.py:523
  123.6 26.1 %collective-permute-start.32 = (bf16[144,2304]{1,0:T(8,128)(2,1)S(1)}, bf16[144,2304]{1,0:T(8,128)(2,1)S(1)}, u32[]{:S(2)}, u32[]{:S(2)}) collective-permute-start(bf16[144,2304]{1,0:T(8,128)(2,1)S(1)} %get-tuple-element.295), channel_id=1, source_target_pairs={{0,16},{8,24},{16,0},{24,8},{1,17},{9,25},{17,1},{25,9},{2,18},{10... | collective-permute-start | bytes 1990664 | tf_op jit(solution)/shard_map/down_first/hi/ppermute | solution.py:539
  141.3 19.1 %collective-permute-start.37 = (bf16[128,2944]{1,0:T(8,128)(2,1)S(1)}, bf16[128,2944]{1,0:T(8,128)(2,1)S(1)}, u32[]{:S(2)}, u32[]{:S(2)}) collective-permute-start(bf16[128,2944]{1,0:T(8,128)(2,1)S(1)} %collective-permute-done.28.refs_5_), channel_id=1, source_target_pairs={{0,8},{8,0},{16,24},{24,16},{1,9},{9,1},{17,25},{25,17},{2,10},{10... | collective-permute-start | bytes 2261000 | tf_op jit(solution)/shard_map/H_both/core/ppermute | solution.py:523
  141.3 17.3 %collective-permute-start.34 = (bf16[96,3456]{1,0:T(8,128)(2,1)S(1)}, bf16[96,3456]{1,0:T(8,128)(2,1)S(1)}, u32[]{:S(2)}, u32[]{:S(2)}) collective-permute-start(bf16[96,3456]{1,0:T(8,128)(2,1)S(1)} %get-tuple-element.281.refs_4_), channel_id=1, source_target_pairs={{0,2},{2,0},{4,6},{6,4},{1,3},{3,1},{5,7},{7,5},{8,10},{10,8},{12,... | collective-permute-start | bytes 1990664 | tf_op jit(solution)/shard_map/E_far/near/ppermute | solution.py:527
  143.0 27.8 %collective-permute-start.15 = (bf16[96,5248]{1,0:T(8,128)(2,1)S(1)}, bf16[96,5248]{1,0:T(8,128)(2,1)S(1)}, u32[]{:S(2)}, u32[]{:S(2)}) collective-permute-start(bf16[96,5248]{1,0:T(8,128)(2,1)S(1)} %get-tuple-element.225.refs_0_), channel_id=1, source_target_pairs={{0,8},{8,0},{16,24},{24,16},{1,9},{9,1},{17,25},{25,17},{2,10},{10... | collective-permute-start | bytes 3022856 | tf_op jit(solution)/shard_map/F_core/core/ppermute | solution.py:523
  143.2 29.3 %collective-permute-start.16 = (bf16[96,5248]{1,0:T(8,128)(2,1)S(1)}, bf16[96,5248]{1,0:T(8,128)(2,1)S(1)}, u32[]{:S(2)}, u32[]{:S(2)}) collective-permute-start(bf16[96,5248]{1,0:T(8,128)(2,1)S(1)} %collective-permute-done.14.refs_1_), channel_id=1, source_target_pairs={{0,8},{8,0},{16,24},{24,16},{1,9},{9,1},{17,25},{25,17},{2,10},{10... | collective-permute-start | bytes 3022856 | tf_op jit(solution)/shard_map/F_both/core/ppermute | solution.py:523
  160.4 15.3 %collective-permute-start.38 = (bf16[96,3456]{1,0:T(8,128)(2,1)S(1)}, bf16[96,3456]{1,0:T(8,128)(2,1)S(1)}, u32[]{:S(2)}, u32[]{:S(2)}) collective-permute-start(bf16[96,3456]{1,0:T(8,128)(2,1)S(1)} %get-tuple-element.281.refs_4_), channel_id=1, source_target_pairs={{0,8},{8,0},{16,24},{24,16},{1,9},{9,1},{17,25},{25,17},{2,10},{10... | collective-permute-start | bytes 1990664 | tf_op jit(solution)/shard_map/E_core/core/ppermute | solution.py:523
  160.4 17.8 %collective-permute-start.40 = (bf16[144,2304]{1,0:T(8,128)(2,1)S(1)}, bf16[144,2304]{1,0:T(8,128)(2,1)S(1)}, u32[]{:S(2)}, u32[]{:S(2)}) collective-permute-start(bf16[144,2304]{1,0:T(8,128)(2,1)S(1)} %get-tuple-element.326), channel_id=1, source_target_pairs={{0,16},{8,24},{16,0},{24,8},{1,17},{9,25},{17,1},{25,9},{2,18},{10... | collective-permute-start | bytes 1990664 | tf_op jit(solution)/shard_map/up_first/hi/ppermute | solution.py:539
  170.4 26.2 %collective-permute-start.39 = (bf16[96,3456]{1,0:T(8,128)(2,1)S(1)}, bf16[96,3456]{1,0:T(8,128)(2,1)S(1)}, u32[]{:S(2)}, u32[]{:S(2)}) collective-permute-start(bf16[96,3456]{1,0:T(8,128)(2,1)S(1)} %collective-permute-done.34.refs_5_), channel_id=1, source_target_pairs={{0,8},{8,0},{16,24},{24,16},{1,9},{9,1},{17,25},{25,17},{2,10},{10... | collective-permute-start | bytes 1990664 | tf_op jit(solution)/shard_map/E_both/core/ppermute | solution.py:523
  172.5 37.9 %collective-permute-start.51 = (bf16[96,2944]{1,0:T(8,128)(2,1)}, bf16[96,2944]{1,0:T(8,128)(2,1)}, u32[]{:S(2)}, u32[]{:S(2)}) collective-permute-start(bf16[96,2944]{1,0:T(8,128)(2,1)} %get-tuple-element.346.refs_4_), channel_id=1, source_target_pairs={{0,2},{2,0},{4,6},{6,4},{1,3},{3,1},{5,7},{7,5},{8,10},{10,8},{12,... | collective-permute-start | bytes 1695752 | tf_op jit(solution)/shard_map/K_far/near/ppermute | solution.py:527
  174.9 33.5 %collective-permute-start.49 = (bf16[144,2304]{1,0:T(8,128)(2,1)S(1)}, bf16[144,2304]{1,0:T(8,128)(2,1)S(1)}, u32[]{:S(2)}, u32[]{:S(2)}) collective-permute-start(bf16[144,2304]{1,0:T(8,128)(2,1)S(1)} %get-tuple-element.348), channel_id=1, source_target_pairs={{0,16},{8,24},{16,0},{24,8},{1,17},{9,25},{17,1},{25,9},{2,18},{10... | collective-permute-start | bytes 1990664 | tf_op jit(solution)/shard_map/attn_first/hi/ppermute | solution.py:539
  175.7 31.7 %collective-permute-start.50 = (bf16[72,2304]{1,0:T(8,128)(2,1)S(1)}, bf16[72,2304]{1,0:T(8,128)(2,1)S(1)}, u32[]{:S(2)}, u32[]{:S(2)}) collective-permute-start(bf16[72,2304]{1,0:T(8,128)(2,1)S(1)} %get-tuple-element.350), channel_id=1, source_target_pairs={{0,4},{2,6},{4,0},{6,2},{1,5},{3,7},{5,1},{7,3},{8,12},{10,14},{12... | collective-permute-start | bytes 995336 | tf_op jit(solution)/shard_map/down_last/far/ppermute | solution.py:531
  178.2 16.1 %collective-permute-start.43 = (f32[2,10,288]{2,1,0:T(8,128)S(1)}, f32[2,10,288]{2,1,0:T(8,128)S(1)}, u32[]{:S(2)}, u32[]{:S(2)}) collective-permute-start(f32[2,10,288]{2,1,0:T(8,128)S(1)} %get-tuple-element.331), channel_id=1, source_target_pairs={{0,4},{2,6},{4,0},{6,2},{1,5},{3,7},{5,1},{7,3},{8,12},{10,14},{12... | collective-permute-start | bytes 69128 | tf_op jit(solution)/shard_map/images/far/ppermute | solution.py:531
  213.2 24.5 %collective-permute-start.48 = (bf16[72,2304]{1,0:T(8,128)(2,1)}, bf16[72,2304]{1,0:T(8,128)(2,1)S(1)}, u32[]{:S(2)}, u32[]{:S(2)}) collective-permute-start(bf16[72,2304]{1,0:T(8,128)(2,1)} %copy-done.42), channel_id=1, source_target_pairs={{0,4},{2,6},{4,0},{6,2},{1,5},{3,7},{5,1},{7,3},{8,12},{10,14},{12... | collective-permute-start | bytes 995336 | tf_op jit(solution)/shard_map/up_last/far/ppermute | solution.py:531
  217.3 21.3 %collective-permute-start.47 = (bf16[144,2304]{1,0:T(8,128)(2,1)}, bf16[144,2304]{1,0:T(8,128)(2,1)S(1)}, u32[]{:S(2)}, u32[]{:S(2)}) collective-permute-start(bf16[144,2304]{1,0:T(8,128)(2,1)} %copy-done.35), channel_id=1, source_target_pairs={{0,16},{8,24},{16,0},{24,8},{1,17},{9,25},{17,1},{25,9},{2,18},{10... | collective-permute-start | bytes 1990664 | tf_op jit(solution)/shard_map/enc_up_first/hi/ppermute | solution.py:539
  218.0 31.7 %collective-permute-start.46 = (bf16[144,2304]{1,0:T(8,128)(2,1)S(1)}, bf16[144,2304]{1,0:T(8,128)(2,1)S(1)}, u32[]{:S(2)}, u32[]{:S(2)}) collective-permute-start(bf16[144,2304]{1,0:T(8,128)(2,1)S(1)} %get-tuple-element.351.refs_2_), channel_id=1, source_target_pairs={{0,16},{8,24},{16,0},{24,8},{1,17},{9,25},{17,1},{25,9},{2,18},{10... | collective-permute-start | bytes 1990664 | tf_op jit(solution)/shard_map/enc_down_first/hi/ppermute | solution.py:539
  219.4 39.6 %collective-permute-start.56 = (bf16[72,2304]{1,0:T(8,128)(2,1)}, bf16[72,2304]{1,0:T(8,128)(2,1)S(1)}, u32[]{:S(2)}, u32[]{:S(2)}) collective-permute-start(bf16[72,2304]{1,0:T(8,128)(2,1)} %copy-done.43), channel_id=1, source_target_pairs={{0,4},{2,6},{4,0},{6,2},{1,5},{3,7},{5,1},{7,3},{8,12},{10,14},{12... | collective-permute-start | bytes 995336 | tf_op jit(solution)/shard_map/attn_last/far/ppermute | solution.py:531
  224.4 37.6 %collective-permute-start.55 = (bf16[144,2304]{1,0:T(8,128)(2,1)S(1)}, bf16[144,2304]{1,0:T(8,128)(2,1)S(1)}, u32[]{:S(2)}, u32[]{:S(2)}) collective-permute-start(bf16[144,2304]{1,0:T(8,128)(2,1)S(1)} %get-tuple-element.355.refs_2_), channel_id=1, source_target_pairs={{0,16},{8,24},{16,0},{24,8},{1,17},{9,25},{17,1},{25,9},{2,18},{10... | collective-permute-start | bytes 1990664 | tf_op jit(solution)/shard_map/enc_attn_first/hi/ppermute | solution.py:539
  240.5 28.3 %collective-permute-start.59 = (bf16[72,2304]{1,0:T(8,128)(2,1)}, bf16[72,2304]{1,0:T(8,128)(2,1)}, u32[]{:S(2)}, u32[]{:S(2)}) collective-permute-start(bf16[72,2304]{1,0:T(8,128)(2,1)} %get-tuple-element.356.refs_2_), channel_id=1, source_target_pairs={{0,4},{2,6},{4,0},{6,2},{1,5},{3,7},{5,1},{7,3},{8,12},{10,14},{12... | collective-permute-start | bytes 995336 | tf_op jit(solution)/shard_map/enc_up_last/far/ppermute | solution.py:531
  250.6 29.9 %collective-permute-start.58 = (bf16[72,2304]{1,0:T(8,128)(2,1)}, bf16[72,2304]{1,0:T(8,128)(2,1)}, u32[]{:S(2)}, u32[]{:S(2)}) collective-permute-start(bf16[72,2304]{1,0:T(8,128)(2,1)} %get-tuple-element.365.refs_2_), channel_id=1, source_target_pairs={{0,4},{2,6},{4,0},{6,2},{1,5},{3,7},{5,1},{7,3},{8,12},{10,14},{12... | collective-permute-start | bytes 995336 | tf_op jit(solution)/shard_map/enc_down_last/far/ppermute | solution.py:531
  263.9 23.6 %collective-permute-start.57 = (bf16[72,2304]{1,0:T(8,128)(2,1)}, bf16[72,2304]{1,0:T(8,128)(2,1)}, u32[]{:S(2)}, u32[]{:S(2)}) collective-permute-start(bf16[72,2304]{1,0:T(8,128)(2,1)} %get-tuple-element.368.refs_2_), channel_id=1, source_target_pairs={{0,4},{2,6},{4,0},{6,2},{1,5},{3,7},{5,1},{7,3},{8,12},{10,14},{12... | collective-permute-start | bytes 995336 | tf_op jit(solution)/shard_map/enc_attn_last/far/ppermute | solution.py:531
  (102 other events, 1004.5 us)

commit v3 on v2

--- a/solution.py
+++ b/solution.py
@@ -634,15 +634,15 @@
 DUE = {
     "grad_parts": "e3", "F far": "d3", "A far": "b2", "M far": "b3", "G far": "c1", "H far": "c2",
     "E far": "c4", "K far": "grads enc_attn", "mlp_other": "c4", "out_kernel": "modulation",
-    "down grads": "b4", "down first": "c3", "down halved": "c4", "up grads": "c2",
-    "up first": "halve up", "attn grads": "c4", "mlp_part": "c2", "modulation": "finish attn",
-    "silu": "e3", "images": "halve up", "parts": "finish down",
+    "down grads": "b4", "down first": "c1x", "down halved": "c2", "down last": "c4",
+    "up grads": "c2", "up first": "c4", "attn grads": "c4", "mlp_part": "c2",
+    "modulation": "finish enc_down", "silu": "e3", "images": "grads enc_down", "parts": "finish up",
 }
 DEC_ALONG_DP, ENC_ALONG_DP, ENC_ROWS = False, False, "FEK"
 TAIL = (
-    "modulation", "collect", "halve up", "grads enc_up", "grads enc_down", "finish down",
-    "halve attn", "grads enc_attn", "finish up", "halve enc_up", "halve enc_down", "finish attn",
-    "halve enc_attn", "finish enc_up", "finish enc_down", "finish enc_attn",
+    "halve up", "modulation", "grads enc_up", "grads enc_down", "halve attn", "collect",
+    "grads enc_attn", "finish up", "halve enc_up", "finish attn", "halve enc_down",
+    "halve enc_attn", "finish down", "finish enc_up", "finish enc_down", "finish enc_attn",
 )
 
 

time: 295 us -> 292 us (0.990)
  waiting for transfers between devices: 107 us -> 81 us
  starting transfers between devices: 60 us -> 84 us
  Pallas kernels: 94.7 us -> 91.5 us
    ppermute x8, starting transfers between devices: 5.28 us -> 39.3 us  [to_far(): return lax.ppermute(a, 'region', self.far)]
    ppermute x8, waiting for transfers between devices: 51.7 us -> 26.8 us  [to_far(): return lax.ppermute(a, 'region', self.far)]
    ppermute x8, waiting for transfers between devices: 15.9 us -> 3.09 us  [to_hi(): return lax.ppermute(a, 'dp', [(d, d ^ 2) for d in range(self.ndp)])]
    ppermute x9, waiting for transfers between devices: 19.7 us -> 31.2 us  [to_near(): return lax.ppermute(a, 'region', self.near)]
    ppermute x9, starting transfers between devices: 15.1 us -> 10.3 us  [to_heads(): return lax.ppermute(a, 'heads', [(0, 1), (1, 0)])]
    ppermute x20, starting transfers between devices: 13.3 us -> 9.16 us  [to_core(): return lax.ppermute(a, 'dp', self.core_perm)]
    pallas_call x32, Pallas kernels: 54 us -> 50.6 us  [call(): pl.pallas_call(body, out_shape=shapes, in_specs=[hbm if i in late else vm...]
    unnamed x148 -> x142, local copies, waits for them, and re-layouts: 16.2 us -> 17.2 us
  transfers between devices with their start and end apart: 60 -> 60, of which waited for: 28 -> 25; matrix products, arithmetic and copies ran while one was open for 3% -> 3% of each run, Pallas kernels for 31% -> 31%
where the time goes in v3:
time: 292 us; the launch traced here: 288 us
  Pallas kernels  91.5 us (31%)
  starting transfers between devices  84 us (29%)
  waiting for transfers between devices  81 us (28%)
  local copies, waits for them, and re-layouts  20.1 us (7%)
  other arithmetic  7.48 us (3%)
    pallas_call x32, Pallas kernels, call(): pl.pallas_call(body, out_shape=shapes, in_specs=[hbm if i in late else vm...  50.6 us
    ppermute x8, starting transfers between devices, to_far(): return lax.ppermute(a, 'region', self.far)  39.3 us
    ppermute x9, waiting for transfers between devices, to_near(): return lax.ppermute(a, 'region', self.near)  31.2 us
    ppermute x8, waiting for transfers between devices, to_far(): return lax.ppermute(a, 'region', self.far)  26.8 us
    pallas_call x8, Pallas kernels, load(): pl.pallas_call(load_kernel, out_shape=[jax.ShapeDtypeStruct(w.shape, w.dt...  21.4 us
    pallas_call x6, Pallas kernels, weight_grads(): pl.pallas_call(functools.partial(weight_grad_kernel, products, len(after)...  19.5 us
    unnamed x142, local copies, waits for them, and re-layouts  17.2 us
    ppermute x9, waiting for transfers between devices, to_heads(): return lax.ppermute(a, 'heads', [(0, 1), (1, 0)])  14.8 us
  transfers between devices with their start and end apart: 60, of which 25 were waited for; matrix products, arithmetic and copies ran while one was open for 3% of the time, Pallas kernels for 31%

profile of v3, /device:TPU:0, one launch (start us, length us, event | category | flops | bytes accessed | tf_op | source)
XLA Modules:
  0.0 287.5 jit_solution(6646262665054399522)
XLA Ops:
  3.5 3.1 %collective-permute-start.3 = (bf16[48,1280]{1,0:T(8,128)(2,1)S(1)}, bf16[48,1280]{1,0:T(8,128)(2,1)S(1)}, u32[]{:S(2)}, u32[]{:S(2)}) collective-permute-start(bf16[48,1280]{1,0:T(8,128)(2,1)S(1)} %get-tuple-element.385), channel_id=1, source_target_pairs={{0,2},{2,0},{4,10},{6,8},{8,6},{10,4},{12,14},{14,12},{16,18},{18,... | collective-permute-start | bytes 368648 | tf_op jit(solution)/shard_map/spread/ppermute | solution.py:557
  7.3 3.5 %collective-permute-start = (bf16[2,1152]{1,0:T(2,128)(2,1)S(1)}, bf16[2,1152]{1,0:T(2,128)(2,1)S(1)}, u32[]{:S(2)}, u32[]{:S(2)}) collective-permute-start(bf16[2,1152]{1,0:T(2,128)(2,1)S(1)} %fusion.8), channel_id=1, source_target_pairs={{0,8},{8,0},{16,24},{24,16},{1,9},{9,1},{17,25},{25,17},{2,10},{10... | collective-permute-start | bytes 13832 | tf_op jit(solution)/shard_map/core/ppermute | solution.py:523
  16.5 3.1 %collective-permute-done.1 = f32[2,1728]{1,0:T(2,128)S(1)} collective-permute-done((f32[2,1728]{1,0:T(2,128)S(1)}, f32[2,1728]{1,0:T(2,128)S(1)}, u32[]{:S(2)}, u32[]{:S(2)}) %collective-permute-start.1) | collective-permute-done | bytes 13856 | tf_op jit(solution)/shard_map/near/ppermute | solution.py:527
  21.7 2.8 collective-permute-done.4
  29.2 3.6 %enc_qkv_kernel.1 = (f32[96,1152]{1,0:T(8,128)S(1)}, bf16[96,1152]{1,0:T(8,128)(2,1)S(1)}, bf16[96,576]{1,0:T(8,128)(2,1)S(1)}, bf16[96,1280]{1,0:T(8,128)(2,1)S(1)}) custom-call(bf16[48,1280]{1,0:T(8,128)(2,1)S(1)} %collective-permute-done.2.refs_0_, bf16[48,1280]{1,0:T(8,128)(2,1)S(1)} %collective-permute-done.3.refs_1_, ...), custom_call_target="tpu_custom_call" | custom-call | tf_op jit(solution)/shard_map/enc_qkv_kernel/pallas_call | solution.py:58
  39.3 4.1 %load.8 = (bf16[1152,2304]{1,0:T(8,128)(2,1)S(1)}, bf16[2304,1152]{1,0:T(8,128)(2,1)S(1)}) custom-call(bf16[1152,2304]{1,0:T(8,128)(2,1)} %refs_0_.3, bf16[2304,1152]{1,0:T(8,128)(2,1)} %refs_1_.2), custom_call_target="tpu_custom_call" | custom-call | tf_op jit(solution)/shard_map/load/pallas_call | solution.py:94
  51.8 4.6 %collective-permute-done.11.refs_2_.refs_7_ = bf16[96,1152]{1,0:T(8,128)(2,1)S(1)} collective-permute-done((bf16[96,1152]{1,0:T(8,128)(2,1)S(1)}, bf16[96,1152]{1,0:T(8,128)(2,1)S(1)}, u32[]{:S(2)}, u32[]{:S(2)}) %collective-permute-start.11) | collective-permute-done | bytes 221216 | tf_op jit(solution)/shard_map/heads/ppermute | solution.py:535
  64.5 4.1 %load.10 = (bf16[1152,2304]{1,0:T(8,128)(2,1)S(1)}, bf16[2304,1152]{1,0:T(8,128)(2,1)S(1)}) custom-call(bf16[1152,2304]{1,0:T(8,128)(2,1)} %refs_0_.1, bf16[2304,1152]{1,0:T(8,128)(2,1)} %refs_1_.1), custom_call_target="tpu_custom_call" | custom-call | tf_op jit(solution)/shard_map/load/pallas_call | solution.py:94
  68.7 3.9 %collective-permute-done.13.refs_2_.refs_5_ = bf16[128,1152]{1,0:T(8,128)(2,1)S(1)} collective-permute-done((bf16[128,1152]{1,0:T(8,128)(2,1)S(1)}, bf16[128,1152]{1,0:T(8,128)(2,1)S(1)}, u32[]{:S(2)}, u32[]{:S(2)}) %collective-permute-start.13) | collective-permute-done | bytes 294944 | tf_op jit(solution)/shard_map/heads/ppermute | solution.py:535
  76.1 3.3 %dec_mlp_back_kernel.1 = (bf16[128,2304]{1,0:T(8,128)(2,1)S(1)}, bf16[128,1152]{1,0:T(8,128)(2,1)S(1)}) custom-call(bf16[128,2944]{1,0:T(8,128)(2,1)S(1)} %get-tuple-element.242.refs_0_, f32[128,2304]{1,0:T(8,128)S(1)} %get-tuple-element.251.refs_1_, bf16[1152,2304]{1,0:T(8,128)(2,1)S(1)} %get-tuple-element.247.refs_4_.refs_2_, ...), custom_call_target="tpu_custom_call" | custom-call | tf_op jit(solution)/shard_map/dec_mlp_back_kernel/pallas_call | solution.py:58
  82.4 4.2 %collective-permute-done.18.refs_1_ = bf16[128,2944]{1,0:T(8,128)(2,1)S(1)} collective-permute-done((bf16[128,2944]{1,0:T(8,128)(2,1)S(1)}, bf16[128,2944]{1,0:T(8,128)(2,1)S(1)}, u32[]{:S(2)}, u32[]{:S(2)}) %collective-permute-start.18) | collective-permute-done | bytes 753696 | tf_op jit(solution)/shard_map/A_far/near/ppermute | solution.py:527
  89.2 5.3 %attention_back_kernel.2 = (f32[128,1152]{1,0:T(8,128)S(1)}, bf16[128,1152]{1,0:T(8,128)(2,1)S(1)}, bf16[128,576]{1,0:T(8,128)(2,1)S(1)}, f32[128,1152]{1,0:T(8,...) custom-call(bf16[128,1152]{1,0:T(8,128)(2,1)S(1)} %get-tuple-element.241.refs_0_.refs_4_, ...), custom_call_target="tpu_custom_call" | custom-call | tf_op jit(solution)/shard_map/attention_back_kernel/pallas_call | solution.py:58
  97.8 7.8 %collective-permute-done.20.refs_5_.refs_1_ = bf16[128,3456]{1,0:T(8,128)(2,1)S(1)} collective-permute-done((bf16[128,3456]{1,0:T(8,128)(2,1)S(1)}, bf16[128,3456]{1,0:T(8,128)(2,1)S(1)}, u32[]{:S(2)}, u32[]{:S(2)}) %collective-permute-start.20) | collective-permute-done | bytes 884768 | tf_op jit(solution)/shard_map/M_far/near/ppermute | solution.py:527
  115.4 2.9 %weight_grads.6 = (bf16[144,2304]{1,0:T(8,128)(2,1)S(1)}, f32[144,2304]{1,0:T(8,128)S(1)}) custom-call(bf16[128,2944]{1,0:T(8,128)(2,1)} %copy-done.3, bf16[128,2944]{1,0:T(8,128)(2,1)} %copy-done.57, bf16[128,2944]{1,0:T(8,128)(2,1)} %copy-done.58, bf16[128,2944]{1,0:T(8,128)(2,1)} %copy-done.59, bf16[128,3456]{1,0:T(8,128)(2,1)} %copy-done.6, ...), custom_call_target="tpu_custom_call" | custom-call | tf_op jit(solution)/shard_map/weight_grads/pallas_call | solution.py:607
  128.0 4.1 %load.13 = (bf16[1152,2304]{1,0:T(8,128)(2,1)S(1)}, bf16[2304,1152]{1,0:T(8,128)(2,1)S(1)}) custom-call(bf16[1152,2304]{1,0:T(8,128)(2,1)} %refs_0_.3, bf16[2304,1152]{1,0:T(8,128)(2,1)} %refs_1_.2), custom_call_target="tpu_custom_call" | custom-call | tf_op jit(solution)/shard_map/load/pallas_call | solution.py:94
  132.1 4.8 %enc_mlp_back_kernel.1 = (bf16[96,3456]{1,0:T(8,128)(2,1)S(1)}, bf16[96,1152]{1,0:T(8,128)(2,1)S(1)}) custom-call(f32[96,1152]{1,0:T(8,128)S(1)} %get-tuple-element.276.refs_0_.refs_5_, f32[96,2304]{1,0:T(8,128)} %copy-done.27, f32[6,1152]{1,0:T(8,128)S(1)} %reshape_squeeze.6.refs_2_.refs_3_.refs_6_.refs_4_, ...), custom_call_target="tpu_custom_call" | custom-call | tf_op jit(solution)/shard_map/enc_mlp_back_kernel/pallas_call | solution.py:58
  140.7 2.9 %weight_grads.7 = (bf16[144,2304]{1,0:T(8,128)(2,1)S(1)}, f32[144,2304]{1,0:T(8,128)S(1)}) custom-call(bf16[128,3456]{1,0:T(8,128)(2,1)} %copy-done.6, bf16[128,3456]{1,0:T(8,128)(2,1)} %copy-done.54, bf16[128,3456]{1,0:T(8,128)(2,1)} %copy-done.55, bf16[128,3456]{1,0:T(8,128)(2,1)} %copy-done.56, bf16[128,2304]{1,0:T(8,128)(2,1)} %copy-done.34, ...), custom_call_target="tpu_custom_call" | custom-call | tf_op jit(solution)/shard_map/weight_grads/pallas_call | solution.py:607
  149.8 5.0 %attention_back_kernel.3 = (f32[96,1152]{1,0:T(8,128)S(1)}, bf16[96,1152]{1,0:T(8,128)(2,1)S(1)}, bf16[96,576]{1,0:T(8,128)(2,1)S(1)}, f32[96,1152]{1,0:T(8,128)...) custom-call(f32[96,1152]{1,0:T(8,128)S(1)} %get-tuple-element.276.refs_0_.refs_5_, ...), custom_call_target="tpu_custom_call" | custom-call | tf_op jit(solution)/shard_map/attention_back_kernel/pallas_call | solution.py:58
  164.9 4.5 %weight_grads.8 = (bf16[144,2304]{1,0:T(8,128)(2,1)}, f32[144,2304]{1,0:T(8,128)S(1)}) custom-call(bf16[128,2944]{1,0:T(8,128)(2,1)} %copy-done.3, bf16[128,2944]{1,0:T(8,128)(2,1)} %copy-done.57, bf16[128,2944]{1,0:T(8,128)(2,1)} %copy-done.58, bf16[128,2944]{1,0:T(8,128)(2,1)} %copy-done.59, bf16[128,2944]{1,0:T(8,128)(2,1)} %copy-done.30, ...), custom_call_target="tpu_custom_call" | custom-call | tf_op jit(solution)/shard_map/weight_grads/pallas_call | solution.py:607
  169.4 7.1 %collective-permute-done.36.refs_1_ = bf16[72,2304]{1,0:T(8,128)(2,1)S(1)} collective-permute-done((bf16[72,2304]{1,0:T(8,128)(2,1)S(1)}, bf16[72,2304]{1,0:T(8,128)(2,1)S(1)}, u32[]{:S(2)}, u32[]{:S(2)}) %collective-permute-start.36) | collective-permute-done | bytes 331808 | tf_op jit(solution)/shard_map/down_last/far/ppermute | solution.py:531
  183.6 3.5 %collective-permute-done.44.refs_1_ = f32[2,10,288]{2,1,0:T(8,128)S(1)} collective-permute-done((f32[2,10,288]{2,1,0:T(8,128)S(1)}, f32[2,10,288]{2,1,0:T(8,128)S(1)}, u32[]{:S(2)}, u32[]{:S(2)}) %collective-permute-start.44) | collective-permute-done | bytes 23072 | tf_op jit(solution)/shard_map/images/near/ppermute | solution.py:527
  189.3 5.0 %collective-permute-done.45.refs_1_ = f32[2,10,288]{2,1,0:T(8,128)S(1)} collective-permute-done((f32[2,10,288]{2,1,0:T(8,128)S(1)}, f32[2,10,288]{2,1,0:T(8,128)S(1)}, u32[]{:S(2)}, u32[]{:S(2)}) %collective-permute-start.45) | collective-permute-done | bytes 23072 | tf_op jit(solution)/shard_map/images/far/ppermute | solution.py:531
  198.1 2.7 weight_grads.9
  201.5 2.7 weight_grads.10
  205.7 8.5 %collective-permute-done.46.refs_5_ = bf16[96,2944]{1,0:T(8,128)(2,1)S(1)} collective-permute-done((bf16[96,2944]{1,0:T(8,128)(2,1)}, bf16[96,2944]{1,0:T(8,128)(2,1)S(1)}, u32[]{:S(2)}, u32[]{:S(2)}) %collective-permute-start.46) | collective-permute-done | bytes 565280 | tf_op jit(solution)/shard_map/K_far/near/ppermute | solution.py:527
  216.1 6.0 %collective-permute-start.56 = (bf16[72,2304]{1,0:T(8,128)(2,1)S(1)}, bf16[72,2304]{1,0:T(8,128)(2,1)S(1)}, u32[]{:S(2)}, u32[]{:S(2)}) collective-permute-start(bf16[72,2304]{1,0:T(8,128)(2,1)S(1)} %get-tuple-element.344.refs_9_), channel_id=1, source_target_pairs={{0,4},{2,6},{4,0},{6,2},{1,5},{3,7},{5,1},{7,3},{8,12},{10,14},{12... | collective-permute-start | bytes 995336 | tf_op jit(solution)/shard_map/attn_last/far/ppermute | solution.py:531
  222.1 3.8 %weight_grads.11 = (bf16[144,2304]{1,0:T(8,128)(2,1)S(1)}, f32[144,2304]{1,0:T(8,128)S(1)}) custom-call(bf16[96,5248]{1,0:T(8,128)(2,1)} %copy-done.2, bf16[96,5248]{1,0:T(8,128)(2,1)} %collective-permute-done.14.refs_1_, bf16[96,5248]{1,0:T(8,128)(2,1)} %copy-done.53, bf16[96,5248]{1,0:T(8,128)(2,1)} %collective-permute-done.16.refs_3_, ...), custom_call_target="tpu_custom_call" | custom-call | tf_op jit(solution)/shard_map/weight_grads/pallas_call | solution.py:607
  230.2 10.5 %collective-permute-start.53 = (bf16[72,2304]{1,0:T(8,128)(2,1)S(1)}, bf16[72,2304]{1,0:T(8,128)(2,1)S(1)}, u32[]{:S(2)}, u32[]{:S(2)}) collective-permute-start(bf16[72,2304]{1,0:T(8,128)(2,1)S(1)} %get-tuple-element.356.refs_2_), channel_id=1, source_target_pairs={{0,4},{2,6},{4,0},{6,2},{1,5},{3,7},{5,1},{7,3},{8,12},{10,14},{12... | collective-permute-start | bytes 995336 | tf_op jit(solution)/shard_map/enc_up_last/far/ppermute | solution.py:531
  245.2 9.7 %collective-permute-start.59 = (bf16[72,2304]{1,0:T(8,128)(2,1)S(1)}, bf16[72,2304]{1,0:T(8,128)(2,1)S(1)}, u32[]{:S(2)}, u32[]{:S(2)}) collective-permute-start(bf16[72,2304]{1,0:T(8,128)(2,1)S(1)} %get-tuple-element.363.refs_2_), channel_id=1, source_target_pairs={{0,4},{2,6},{4,0},{6,2},{1,5},{3,7},{5,1},{7,3},{8,12},{10,14},{12... | collective-permute-start | bytes 995336 | tf_op jit(solution)/shard_map/enc_down_last/far/ppermute | solution.py:531
  255.0 3.1 %collective-permute-done.54.refs_1_ = bf16[144,2304]{1,0:T(8,128)(2,1)S(1)} collective-permute-done((bf16[144,2304]{1,0:T(8,128)(2,1)S(1)}, bf16[144,2304]{1,0:T(8,128)(2,1)S(1)}, u32[]{:S(2)}, u32[]{:S(2)}) %collective-permute-start.54) | collective-permute-done | bytes 663584 | tf_op jit(solution)/shard_map/enc_attn_first/hi/ppermute | solution.py:539
  258.2 8.2 %collective-permute-start.58 = (bf16[72,2304]{1,0:T(8,128)(2,1)S(1)}, bf16[72,2304]{1,0:T(8,128)(2,1)S(1)}, u32[]{:S(2)}, u32[]{:S(2)}) collective-permute-start(bf16[72,2304]{1,0:T(8,128)(2,1)S(1)} %get-tuple-element.364.refs_2_), channel_id=1, source_target_pairs={{0,4},{2,6},{4,0},{6,2},{1,5},{3,7},{5,1},{7,3},{8,12},{10,14},{12... | collective-permute-start | bytes 995336 | tf_op jit(solution)/shard_map/enc_attn_last/far/ppermute | solution.py:531
  270.8 7.7 %collective-permute-done.59.refs_1_ = bf16[72,2304]{1,0:T(8,128)(2,1)S(1)} collective-permute-done((bf16[72,2304]{1,0:T(8,128)(2,1)S(1)}, bf16[72,2304]{1,0:T(8,128)(2,1)S(1)}, u32[]{:S(2)}, u32[]{:S(2)}) %collective-permute-start.59) | collective-permute-done | bytes 331808 | tf_op jit(solution)/shard_map/enc_down_last/far/ppermute | solution.py:531
  (334 shorter events, 129.4 us)
Async XLA Ops:
  2.8 16.8 %collective-permute-start.2 = (bf16[48,1280]{1,0:T(8,128)(2,1)S(1)}, bf16[48,1280]{1,0:T(8,128)(2,1)S(1)}, u32[]{:S(2)}, u32[]{:S(2)}) collective-permute-start(bf16[48,1280]{1,0:T(8,128)(2,1)S(1)} %get-tuple-element.386), channel_id=1, source_target_pairs={{0,0},{2,2},{4,8},{6,10},{8,4},{10,6},{12,12},{14,14},{16,16},{18,... | collective-permute-start | bytes 368648 | tf_op jit(solution)/shard_map/spread/ppermute | solution.py:557
  3.5 16.2 %collective-permute-start.3 = (bf16[48,1280]{1,0:T(8,128)(2,1)S(1)}, bf16[48,1280]{1,0:T(8,128)(2,1)S(1)}, u32[]{:S(2)}, u32[]{:S(2)}) collective-permute-start(bf16[48,1280]{1,0:T(8,128)(2,1)S(1)} %get-tuple-element.385), channel_id=1, source_target_pairs={{0,2},{2,0},{4,10},{6,8},{8,6},{10,4},{12,14},{14,12},{16,18},{18,... | collective-permute-start | bytes 368648 | tf_op jit(solution)/shard_map/spread/ppermute | solution.py:557
  47.0 25.6 %collective-permute-start.14 = (bf16[96,5248]{1,0:T(8,128)(2,1)S(1)}, bf16[96,5248]{1,0:T(8,128)(2,1)}, u32[]{:S(2)}, u32[]{:S(2)}) collective-permute-start(bf16[96,5248]{1,0:T(8,128)(2,1)S(1)} %get-tuple-element.226.refs_0_), channel_id=1, source_target_pairs={{0,2},{2,0},{4,6},{6,4},{1,3},{3,1},{5,7},{7,5},{8,10},{10,8},{12,... | collective-permute-start | bytes 3022856 | tf_op jit(solution)/shard_map/F_far/near/ppermute | solution.py:527
  64.5 22.1 %collective-permute-start.18 = (bf16[128,2944]{1,0:T(8,128)(2,1)S(1)}, bf16[128,2944]{1,0:T(8,128)(2,1)S(1)}, u32[]{:S(2)}, u32[]{:S(2)}) collective-permute-start(bf16[128,2944]{1,0:T(8,128)(2,1)S(1)} %get-tuple-element.242.refs_0_), channel_id=1, source_target_pairs={{0,2},{2,0},{4,6},{6,4},{1,3},{3,1},{5,7},{7,5},{8,10},{10,8},{12,... | collective-permute-start | bytes 2261000 | tf_op jit(solution)/shard_map/A_far/near/ppermute | solution.py:527
  75.5 30.0 %collective-permute-start.20 = (bf16[128,3456]{1,0:T(8,128)(2,1)S(1)}, bf16[128,3456]{1,0:T(8,128)(2,1)S(1)}, u32[]{:S(2)}, u32[]{:S(2)}) collective-permute-start(bf16[128,3456]{1,0:T(8,128)(2,1)S(1)} %get-tuple-element.261.refs_4_.refs_0_), channel_id=1, source_target_pairs={{0,2},{2,0},{4,6},{6,4},{1,3},{3,1},{5,7},{7,5},{8,10},{10,8},{12,... | collective-permute-start | bytes 2654216 | tf_op jit(solution)/shard_map/M_far/near/ppermute | solution.py:527
  96.6 14.3 %collective-permute-start.22 = (bf16[128,2944]{1,0:T(8,128)(2,1)S(1)}, bf16[128,2944]{1,0:T(8,128)(2,1)S(1)}, u32[]{:S(2)}, u32[]{:S(2)}) collective-permute-start(bf16[128,2944]{1,0:T(8,128)(2,1)S(1)} %get-tuple-element.242.refs_0_), channel_id=1, source_target_pairs={{0,8},{8,0},{16,24},{24,16},{1,9},{9,1},{17,25},{25,17},{2,10},{10... | collective-permute-start | bytes 2261000 | tf_op jit(solution)/shard_map/A_core/core/ppermute | solution.py:523
  96.6 16.7 %collective-permute-start.24 = (bf16[128,3456]{1,0:T(8,128)(2,1)S(1)}, bf16[128,3456]{1,0:T(8,128)(2,1)S(1)}, u32[]{:S(2)}, u32[]{:S(2)}) collective-permute-start(bf16[128,3456]{1,0:T(8,128)(2,1)S(1)} %get-tuple-element.261.refs_4_.refs_0_), channel_id=1, source_target_pairs={{0,8},{8,0},{16,24},{24,16},{1,9},{9,1},{17,25},{25,17},{2,10},{10... | collective-permute-start | bytes 2654216 | tf_op jit(solution)/shard_map/M_core/core/ppermute | solution.py:523
  110.9 16.6 %collective-permute-start.26 = (bf16[128,2304]{1,0:T(8,128)(2,1)S(1)}, bf16[128,2304]{1,0:T(8,128)(2,1)S(1)}, u32[]{:S(2)}, u32[]{:S(2)}) collective-permute-start(bf16[128,2304]{1,0:T(8,128)(2,1)S(1)} %get-tuple-element.275.refs_4_), channel_id=1, source_target_pairs={{0,2},{2,0},{4,6},{6,4},{1,3},{3,1},{5,7},{7,5},{8,10},{10,8},{12,... | collective-permute-start | bytes 1769480 | tf_op jit(solution)/shard_map/G_far/near/ppermute | solution.py:527
  119.6 17.3 %collective-permute-start.27 = (bf16[144,2304]{1,0:T(8,128)(2,1)S(1)}, bf16[144,2304]{1,0:T(8,128)(2,1)S(1)}, u32[]{:S(2)}, u32[]{:S(2)}) collective-permute-start(bf16[144,2304]{1,0:T(8,128)(2,1)S(1)} %get-tuple-element.283), channel_id=1, source_target_pairs={{0,16},{8,24},{16,0},{24,8},{1,17},{9,25},{17,1},{25,9},{2,18},{10... | collective-permute-start | bytes 1990664 | tf_op jit(solution)/shard_map/down_first/hi/ppermute | solution.py:539
  121.1 18.0 %collective-permute-start.30 = (bf16[128,2304]{1,0:T(8,128)(2,1)S(1)}, bf16[128,2304]{1,0:T(8,128)(2,1)S(1)}, u32[]{:S(2)}, u32[]{:S(2)}) collective-permute-start(bf16[128,2304]{1,0:T(8,128)(2,1)S(1)} %get-tuple-element.275.refs_4_), channel_id=1, source_target_pairs={{0,8},{8,0},{16,24},{24,16},{1,9},{9,1},{17,25},{25,17},{2,10},{10... | collective-permute-start | bytes 1769480 | tf_op jit(solution)/shard_map/G_core/core/ppermute | solution.py:523
  121.1 23.5 %collective-permute-start.29 = (bf16[128,2944]{1,0:T(8,128)(2,1)S(1)}, bf16[128,2944]{1,0:T(8,128)(2,1)S(1)}, u32[]{:S(2)}, u32[]{:S(2)}) collective-permute-start(bf16[128,2944]{1,0:T(8,128)(2,1)S(1)} %get-tuple-element.286.refs_4_), channel_id=1, source_target_pairs={{0,2},{2,0},{4,6},{6,4},{1,3},{3,1},{5,7},{7,5},{8,10},{10,8},{12,... | collective-permute-start | bytes 2261000 | tf_op jit(solution)/shard_map/H_far/near/ppermute | solution.py:527
  127.5 20.5 %collective-permute-start.38 = (bf16[128,2944]{1,0:T(8,128)(2,1)S(1)}, bf16[128,2944]{1,0:T(8,128)(2,1)S(1)}, u32[]{:S(2)}, u32[]{:S(2)}) collective-permute-start(bf16[128,2944]{1,0:T(8,128)(2,1)S(1)} %get-tuple-element.286.refs_4_), channel_id=1, source_target_pairs={{0,8},{8,0},{16,24},{24,16},{1,9},{9,1},{17,25},{25,17},{2,10},{10... | collective-permute-start | bytes 2261000 | tf_op jit(solution)/shard_map/H_core/core/ppermute | solution.py:523
  136.9 20.2 %collective-permute-start.34 = (bf16[96,3456]{1,0:T(8,128)(2,1)S(1)}, bf16[96,3456]{1,0:T(8,128)(2,1)}, u32[]{:S(2)}, u32[]{:S(2)}) collective-permute-start(bf16[96,3456]{1,0:T(8,128)(2,1)S(1)} %get-tuple-element.305.refs_4_), channel_id=1, source_target_pairs={{0,2},{2,0},{4,6},{6,4},{1,3},{3,1},{5,7},{7,5},{8,10},{10,8},{12,... | collective-permute-start | bytes 1990664 | tf_op jit(solution)/shard_map/E_far/near/ppermute | solution.py:527
  146.2 17.2 %collective-permute-start.39 = (bf16[128,2944]{1,0:T(8,128)(2,1)S(1)}, bf16[128,2944]{1,0:T(8,128)(2,1)S(1)}, u32[]{:S(2)}, u32[]{:S(2)}) collective-permute-start(bf16[128,2944]{1,0:T(8,128)(2,1)S(1)} %collective-permute-done.29.refs_5_), channel_id=1, source_target_pairs={{0,8},{8,0},{16,24},{24,16},{1,9},{9,1},{17,25},{25,17},{2,10},{10... | collective-permute-start | bytes 2261000 | tf_op jit(solution)/shard_map/H_both/core/ppermute | solution.py:523
  146.2 30.2 %collective-permute-start.37 = (bf16[144,2304]{1,0:T(8,128)(2,1)S(1)}, bf16[144,2304]{1,0:T(8,128)(2,1)S(1)}, u32[]{:S(2)}, u32[]{:S(2)}) collective-permute-start(bf16[144,2304]{1,0:T(8,128)(2,1)S(1)} %get-tuple-element.308), channel_id=1, source_target_pairs={{0,16},{8,24},{16,0},{24,8},{1,17},{9,25},{17,1},{25,9},{2,18},{10... | collective-permute-start | bytes 1990664 | tf_op jit(solution)/shard_map/up_first/hi/ppermute | solution.py:539
  147.7 41.5 %collective-permute-start.15 = (bf16[96,5248]{1,0:T(8,128)(2,1)S(1)}, bf16[96,5248]{1,0:T(8,128)(2,1)S(1)}, u32[]{:S(2)}, u32[]{:S(2)}) collective-permute-start(bf16[96,5248]{1,0:T(8,128)(2,1)S(1)} %get-tuple-element.226.refs_0_), channel_id=1, source_target_pairs={{0,8},{8,0},{16,24},{24,16},{1,9},{9,1},{17,25},{25,17},{2,10},{10... | collective-permute-start | bytes 3022856 | tf_op jit(solution)/shard_map/F_core/core/ppermute | solution.py:523
  158.6 17.8 %collective-permute-start.36 = (bf16[72,2304]{1,0:T(8,128)(2,1)S(1)}, bf16[72,2304]{1,0:T(8,128)(2,1)S(1)}, u32[]{:S(2)}, u32[]{:S(2)}) collective-permute-start(bf16[72,2304]{1,0:T(8,128)(2,1)S(1)} %get-tuple-element.307), channel_id=1, source_target_pairs={{0,4},{2,6},{4,0},{6,2},{1,5},{3,7},{5,1},{7,3},{8,12},{10,14},{12... | collective-permute-start | bytes 995336 | tf_op jit(solution)/shard_map/down_last/far/ppermute | solution.py:531
  159.7 36.3 %collective-permute-start.16 = (bf16[96,5248]{1,0:T(8,128)(2,1)}, bf16[96,5248]{1,0:T(8,128)(2,1)}, u32[]{:S(2)}, u32[]{:S(2)}) collective-permute-start(bf16[96,5248]{1,0:T(8,128)(2,1)} %collective-permute-done.14.refs_1_), channel_id=1, source_target_pairs={{0,8},{8,0},{16,24},{24,16},{1,9},{9,1},{17,25},{25,17},{2,10},{10... | collective-permute-start | bytes 3022856 | tf_op jit(solution)/shard_map/F_both/core/ppermute | solution.py:523
  183.2 14.9 %collective-permute-start.42 = (bf16[96,3456]{1,0:T(8,128)(2,1)}, bf16[96,3456]{1,0:T(8,128)(2,1)}, u32[]{:S(2)}, u32[]{:S(2)}) collective-permute-start(bf16[96,3456]{1,0:T(8,128)(2,1)} %collective-permute-done.34.refs_5_), channel_id=1, source_target_pairs={{0,8},{8,0},{16,24},{24,16},{1,9},{9,1},{17,25},{25,17},{2,10},{10... | collective-permute-start | bytes 1990664 | tf_op jit(solution)/shard_map/E_both/core/ppermute | solution.py:523
  187.0 17.2 %collective-permute-start.40 = (bf16[144,2304]{1,0:T(8,128)(2,1)}, bf16[144,2304]{1,0:T(8,128)(2,1)}, u32[]{:S(2)}, u32[]{:S(2)}) collective-permute-start(bf16[144,2304]{1,0:T(8,128)(2,1)} %get-tuple-element.313), channel_id=1, source_target_pairs={{0,16},{8,24},{16,0},{24,8},{1,17},{9,25},{17,1},{25,9},{2,18},{10... | collective-permute-start | bytes 1990664 | tf_op jit(solution)/shard_map/attn_first/hi/ppermute | solution.py:539
  194.3 19.9 %collective-permute-start.46 = (bf16[96,2944]{1,0:T(8,128)(2,1)}, bf16[96,2944]{1,0:T(8,128)(2,1)S(1)}, u32[]{:S(2)}, u32[]{:S(2)}) collective-permute-start(bf16[96,2944]{1,0:T(8,128)(2,1)} %get-tuple-element.303.refs_4_), channel_id=1, source_target_pairs={{0,2},{2,0},{4,6},{6,4},{1,3},{3,1},{5,7},{7,5},{8,10},{10,8},{12,... | collective-permute-start | bytes 1695752 | tf_op jit(solution)/shard_map/K_far/near/ppermute | solution.py:527
  195.9 19.2 %collective-permute-start.47 = (bf16[96,2944]{1,0:T(8,128)(2,1)}, bf16[96,2944]{1,0:T(8,128)(2,1)S(1)}, u32[]{:S(2)}, u32[]{:S(2)}) collective-permute-start(bf16[96,2944]{1,0:T(8,128)(2,1)} %get-tuple-element.303.refs_4_), channel_id=1, source_target_pairs={{0,8},{8,0},{16,24},{24,16},{1,9},{9,1},{17,25},{25,17},{2,10},{10... | collective-permute-start | bytes 1695752 | tf_op jit(solution)/shard_map/K_core/core/ppermute | solution.py:523
  196.0 32.0 %collective-permute-start.52 = (bf16[72,2304]{1,0:T(8,128)(2,1)}, bf16[72,2304]{1,0:T(8,128)(2,1)S(1)}, u32[]{:S(2)}, u32[]{:S(2)}) collective-permute-start(bf16[72,2304]{1,0:T(8,128)(2,1)} %copy-done.39), channel_id=1, source_target_pairs={{0,4},{2,6},{4,0},{6,2},{1,5},{3,7},{5,1},{7,3},{8,12},{10,14},{12... | collective-permute-start | bytes 995336 | tf_op jit(solution)/shard_map/up_last/far/ppermute | solution.py:531
  200.9 13.3 %collective-permute-start.57 = (f32[4,10,288]{2,1,0:T(8,128)S(1)}, f32[4,10,288]{2,1,0:T(8,128)S(1)}, u32[]{:S(2)}, u32[]{:S(2)}) collective-permute-start(f32[4,10,288]{2,1,0:T(8,128)S(1)} %all_images_kernel.1), channel_id=1, source_target_pairs={{0,16},{8,24},{16,0},{24,8},{1,17},{9,25},{17,1},{25,9},{2,18},{10... | collective-permute-start | bytes 138248 | tf_op jit(solution)/shard_map/modulation/hi/ppermute | solution.py:539
  205.6 20.3 %collective-permute-start.50 = (bf16[112,1152]{1,0:T(8,128)(2,1)S(1)}, bf16[112,1152]{1,0:T(8,128)(2,1)S(1)}, u32[]{:S(2)}, u32[]{:S(2)}) collective-permute-start(bf16[112,1152]{1,0:T(8,128)(2,1)S(1)} %pad_maximum_fusion.2), channel_id=1, source_target_pairs={{2,0},{0,2},{10,4},{8,6},{6,8},{4,10},{14,12},{12,14},{18,16},{16,... | collective-permute-start | bytes 774152 | tf_op jit(solution)/shard_map/parts/collect/ppermute | solution.py:564
  215.1 13.9 %collective-permute-start.51 = (bf16[144,2304]{1,0:T(8,128)(2,1)S(1)}, bf16[144,2304]{1,0:T(8,128)(2,1)S(1)}, u32[]{:S(2)}, u32[]{:S(2)}) collective-permute-start(bf16[144,2304]{1,0:T(8,128)(2,1)S(1)} %get-tuple-element.337.refs_9_), channel_id=1, source_target_pairs={{0,16},{8,24},{16,0},{24,8},{1,17},{9,25},{17,1},{25,9},{2,18},{10... | collective-permute-start | bytes 1990664 | tf_op jit(solution)/shard_map/enc_up_first/hi/ppermute | solution.py:539
  216.1 26.9 %collective-permute-start.56 = (bf16[72,2304]{1,0:T(8,128)(2,1)S(1)}, bf16[72,2304]{1,0:T(8,128)(2,1)S(1)}, u32[]{:S(2)}, u32[]{:S(2)}) collective-permute-start(bf16[72,2304]{1,0:T(8,128)(2,1)S(1)} %get-tuple-element.344.refs_9_), channel_id=1, source_target_pairs={{0,4},{2,6},{4,0},{6,2},{1,5},{3,7},{5,1},{7,3},{8,12},{10,14},{12... | collective-permute-start | bytes 995336 | tf_op jit(solution)/shard_map/attn_last/far/ppermute | solution.py:531
  225.9 18.1 %collective-permute-start.55 = (bf16[144,2304]{1,0:T(8,128)(2,1)S(1)}, bf16[144,2304]{1,0:T(8,128)(2,1)S(1)}, u32[]{:S(2)}, u32[]{:S(2)}) collective-permute-start(bf16[144,2304]{1,0:T(8,128)(2,1)S(1)} %get-tuple-element.338.refs_2_), channel_id=1, source_target_pairs={{0,16},{8,24},{16,0},{24,8},{1,17},{9,25},{17,1},{25,9},{2,18},{10... | collective-permute-start | bytes 1990664 | tf_op jit(solution)/shard_map/enc_down_first/hi/ppermute | solution.py:539
  227.5 30.5 %collective-permute-start.54 = (bf16[144,2304]{1,0:T(8,128)(2,1)S(1)}, bf16[144,2304]{1,0:T(8,128)(2,1)S(1)}, u32[]{:S(2)}, u32[]{:S(2)}) collective-permute-start(bf16[144,2304]{1,0:T(8,128)(2,1)S(1)} %get-tuple-element.354.refs_2_), channel_id=1, source_target_pairs={{0,16},{8,24},{16,0},{24,8},{1,17},{9,25},{17,1},{25,9},{2,18},{10... | collective-permute-start | bytes 1990664 | tf_op jit(solution)/shard_map/enc_attn_first/hi/ppermute | solution.py:539
  230.2 38.6 %collective-permute-start.53 = (bf16[72,2304]{1,0:T(8,128)(2,1)S(1)}, bf16[72,2304]{1,0:T(8,128)(2,1)S(1)}, u32[]{:S(2)}, u32[]{:S(2)}) collective-permute-start(bf16[72,2304]{1,0:T(8,128)(2,1)S(1)} %get-tuple-element.356.refs_2_), channel_id=1, source_target_pairs={{0,4},{2,6},{4,0},{6,2},{1,5},{3,7},{5,1},{7,3},{8,12},{10,14},{12... | collective-permute-start | bytes 995336 | tf_op jit(solution)/shard_map/enc_up_last/far/ppermute | solution.py:531
  245.2 33.3 %collective-permute-start.59 = (bf16[72,2304]{1,0:T(8,128)(2,1)S(1)}, bf16[72,2304]{1,0:T(8,128)(2,1)S(1)}, u32[]{:S(2)}, u32[]{:S(2)}) collective-permute-start(bf16[72,2304]{1,0:T(8,128)(2,1)S(1)} %get-tuple-element.363.refs_2_), channel_id=1, source_target_pairs={{0,4},{2,6},{4,0},{6,2},{1,5},{3,7},{5,1},{7,3},{8,12},{10,14},{12... | collective-permute-start | bytes 995336 | tf_op jit(solution)/shard_map/enc_down_last/far/ppermute | solution.py:531
  258.2 27.0 %collective-permute-start.58 = (bf16[72,2304]{1,0:T(8,128)(2,1)S(1)}, bf16[72,2304]{1,0:T(8,128)(2,1)S(1)}, u32[]{:S(2)}, u32[]{:S(2)}) collective-permute-start(bf16[72,2304]{1,0:T(8,128)(2,1)S(1)} %get-tuple-element.364.refs_2_), channel_id=1, source_target_pairs={{0,4},{2,6},{4,0},{6,2},{1,5},{3,7},{5,1},{7,3},{8,12},{10,14},{12... | collective-permute-start | bytes 995336 | tf_op jit(solution)/shard_map/enc_attn_last/far/ppermute | solution.py:531
  (99 other events, 895.5 us)

commit v4 on v3

--- a/solution.py
+++ b/solution.py
@@ -636,7 +636,7 @@
     "E far": "c4", "K far": "grads enc_attn", "mlp_other": "c4", "out_kernel": "modulation",
     "down grads": "b4", "down first": "c1x", "down halved": "c2", "down last": "c4",
     "up grads": "c2", "up first": "c4", "attn grads": "c4", "mlp_part": "c2",
-    "modulation": "finish enc_down", "silu": "e3", "images": "grads enc_down", "parts": "finish up",
+    "modulation": "finish enc_down", "silu": "e3", "enc_down first": "halve enc_up", "images": "grads enc_down", "parts": "finish up",
 }
 DEC_ALONG_DP, ENC_ALONG_DP, ENC_ROWS = False, False, "FEK"
 TAIL = (

time: 292 us -> 305 us (1.045)
  waiting for transfers between devices: 81 us -> 101 us
  starting transfers between devices: 84 us -> 77.1 us
    ppermute x8, waiting for transfers between devices: 26.8 us -> 37.3 us  [to_far(): return lax.ppermute(a, 'region', self.far)]
    ppermute x8, waiting for transfers between devices: 3.09 us -> 12.3 us  [to_hi(): return lax.ppermute(a, 'dp', [(d, d ^ 2) for d in range(self.ndp)])]
    ppermute x8, starting transfers between devices: 39.3 us -> 32.6 us  [to_far(): return lax.ppermute(a, 'region', self.far)]
  transfers between devices with their start and end apart: 60 -> 60, of which waited for: 25 -> 25; matrix products, arithmetic and copies ran while one was open for 3% -> 3% of each run, Pallas kernels for 31% -> 29%
where the time goes in v4:
time: 305 us; the launch traced here: 300 us
  waiting for transfers between devices  101 us (33%)
  Pallas kernels  91.5 us (30%)
  starting transfers between devices  77.1 us (25%)
  local copies, waits for them, and re-layouts  20.1 us (7%)
  other arithmetic  7.47 us (2%)
    pallas_call x32, Pallas kernels, call(): pl.pallas_call(body, out_shape=shapes, in_specs=[hbm if i in late else vm...  50.7 us
    ppermute x8, waiting for transfers between devices, to_far(): return lax.ppermute(a, 'region', self.far)  37.3 us
    ppermute x8, starting transfers between devices, to_far(): return lax.ppermute(a, 'region', self.far)  32.6 us
    ppermute x9, waiting for transfers between devices, to_near(): return lax.ppermute(a, 'region', self.near)  31.2 us
    pallas_call x8, Pallas kernels, load(): pl.pallas_call(load_kernel, out_shape=[jax.ShapeDtypeStruct(w.shape, w.dt...  21.4 us
    pallas_call x6, Pallas kernels, weight_grads(): pl.pallas_call(functools.partial(weight_grad_kernel, products, len(after)...  19.5 us
    unnamed x142, local copies, waits for them, and re-layouts  17.2 us
    ppermute x9, waiting for transfers between devices, to_heads(): return lax.ppermute(a, 'heads', [(0, 1), (1, 0)])  14.8 us
  transfers between devices with their start and end apart: 60, of which 25 were waited for; matrix products, arithmetic and copies ran while one was open for 3% of the time, Pallas kernels for 29%

profile of v4, /device:TPU:0, one launch (start us, length us, event | category | flops | bytes accessed | tf_op | source)
XLA Modules:
  0.0 300.3 jit_solution(461405441755465665)
XLA Ops:
  3.5 3.1 %collective-permute-start.3 = (bf16[48,1280]{1,0:T(8,128)(2,1)S(1)}, bf16[48,1280]{1,0:T(8,128)(2,1)S(1)}, u32[]{:S(2)}, u32[]{:S(2)}) collective-permute-start(bf16[48,1280]{1,0:T(8,128)(2,1)S(1)} %get-tuple-element.389), channel_id=1, source_target_pairs={{0,2},{2,0},{4,10},{6,8},{8,6},{10,4},{12,14},{14,12},{16,18},{18,... | collective-permute-start | bytes 368648 | tf_op jit(solution)/shard_map/spread/ppermute | solution.py:557
  7.3 3.5 %collective-permute-start = (bf16[2,1152]{1,0:T(2,128)(2,1)S(1)}, bf16[2,1152]{1,0:T(2,128)(2,1)S(1)}, u32[]{:S(2)}, u32[]{:S(2)}) collective-permute-start(bf16[2,1152]{1,0:T(2,128)(2,1)S(1)} %fusion.8), channel_id=1, source_target_pairs={{0,8},{8,0},{16,24},{24,16},{1,9},{9,1},{17,25},{25,17},{2,10},{10... | collective-permute-start | bytes 13832 | tf_op jit(solution)/shard_map/core/ppermute | solution.py:523
  16.5 3.1 %collective-permute-done.1 = f32[2,1728]{1,0:T(2,128)S(1)} collective-permute-done((f32[2,1728]{1,0:T(2,128)S(1)}, f32[2,1728]{1,0:T(2,128)S(1)}, u32[]{:S(2)}, u32[]{:S(2)}) %collective-permute-start.1) | collective-permute-done | bytes 13856 | tf_op jit(solution)/shard_map/near/ppermute | solution.py:527
  21.7 2.8 collective-permute-done.4
  29.2 3.6 %enc_qkv_kernel.1 = (f32[96,1152]{1,0:T(8,128)S(1)}, bf16[96,1152]{1,0:T(8,128)(2,1)S(1)}, bf16[96,576]{1,0:T(8,128)(2,1)S(1)}, bf16[96,1280]{1,0:T(8,128)(2,1)S(1)}) custom-call(bf16[48,1280]{1,0:T(8,128)(2,1)S(1)} %collective-permute-done.2.refs_0_, bf16[48,1280]{1,0:T(8,128)(2,1)S(1)} %collective-permute-done.3.refs_1_, ...), custom_call_target="tpu_custom_call" | custom-call | tf_op jit(solution)/shard_map/enc_qkv_kernel/pallas_call | solution.py:58
  39.3 4.1 %load.8 = (bf16[1152,2304]{1,0:T(8,128)(2,1)S(1)}, bf16[2304,1152]{1,0:T(8,128)(2,1)S(1)}) custom-call(bf16[1152,2304]{1,0:T(8,128)(2,1)} %refs_0_.3, bf16[2304,1152]{1,0:T(8,128)(2,1)} %refs_1_.2), custom_call_target="tpu_custom_call" | custom-call | tf_op jit(solution)/shard_map/load/pallas_call | solution.py:94
  51.8 4.6 %collective-permute-done.11.refs_2_.refs_7_ = bf16[96,1152]{1,0:T(8,128)(2,1)S(1)} collective-permute-done((bf16[96,1152]{1,0:T(8,128)(2,1)S(1)}, bf16[96,1152]{1,0:T(8,128)(2,1)S(1)}, u32[]{:S(2)}, u32[]{:S(2)}) %collective-permute-start.11) | collective-permute-done | bytes 221216 | tf_op jit(solution)/shard_map/heads/ppermute | solution.py:535
  64.5 4.1 %load.10 = (bf16[1152,2304]{1,0:T(8,128)(2,1)S(1)}, bf16[2304,1152]{1,0:T(8,128)(2,1)S(1)}) custom-call(bf16[1152,2304]{1,0:T(8,128)(2,1)} %refs_0_.1, bf16[2304,1152]{1,0:T(8,128)(2,1)} %refs_1_.1), custom_call_target="tpu_custom_call" | custom-call | tf_op jit(solution)/shard_map/load/pallas_call | solution.py:94
  68.7 3.9 %collective-permute-done.13.refs_2_.refs_5_ = bf16[128,1152]{1,0:T(8,128)(2,1)S(1)} collective-permute-done((bf16[128,1152]{1,0:T(8,128)(2,1)S(1)}, bf16[128,1152]{1,0:T(8,128)(2,1)S(1)}, u32[]{:S(2)}, u32[]{:S(2)}) %collective-permute-start.13) | collective-permute-done | bytes 294944 | tf_op jit(solution)/shard_map/heads/ppermute | solution.py:535
  76.1 3.3 %dec_mlp_back_kernel.1 = (bf16[128,2304]{1,0:T(8,128)(2,1)S(1)}, bf16[128,1152]{1,0:T(8,128)(2,1)S(1)}) custom-call(bf16[128,2944]{1,0:T(8,128)(2,1)S(1)} %get-tuple-element.244.refs_0_, f32[128,2304]{1,0:T(8,128)S(1)} %get-tuple-element.253.refs_1_, bf16[1152,2304]{1,0:T(8,128)(2,1)S(1)} %get-tuple-element.249.refs_4_.refs_2_, ...), custom_call_target="tpu_custom_call" | custom-call | tf_op jit(solution)/shard_map/dec_mlp_back_kernel/pallas_call | solution.py:58
  82.4 4.2 %collective-permute-done.18.refs_1_ = bf16[128,2944]{1,0:T(8,128)(2,1)S(1)} collective-permute-done((bf16[128,2944]{1,0:T(8,128)(2,1)S(1)}, bf16[128,2944]{1,0:T(8,128)(2,1)S(1)}, u32[]{:S(2)}, u32[]{:S(2)}) %collective-permute-start.18) | collective-permute-done | bytes 753696 | tf_op jit(solution)/shard_map/A_far/near/ppermute | solution.py:527
  89.2 5.3 %attention_back_kernel.2 = (f32[128,1152]{1,0:T(8,128)S(1)}, bf16[128,1152]{1,0:T(8,128)(2,1)S(1)}, bf16[128,576]{1,0:T(8,128)(2,1)S(1)}, f32[128,1152]{1,0:T(8,...) custom-call(bf16[128,1152]{1,0:T(8,128)(2,1)S(1)} %get-tuple-element.243.refs_0_.refs_4_, ...), custom_call_target="tpu_custom_call" | custom-call | tf_op jit(solution)/shard_map/attention_back_kernel/pallas_call | solution.py:58
  97.8 7.8 %collective-permute-done.20.refs_5_.refs_1_ = bf16[128,3456]{1,0:T(8,128)(2,1)S(1)} collective-permute-done((bf16[128,3456]{1,0:T(8,128)(2,1)S(1)}, bf16[128,3456]{1,0:T(8,128)(2,1)S(1)}, u32[]{:S(2)}, u32[]{:S(2)}) %collective-permute-start.20) | collective-permute-done | bytes 884768 | tf_op jit(solution)/shard_map/M_far/near/ppermute | solution.py:527
  115.4 2.9 weight_grads.6
  128.0 4.1 %load.13 = (bf16[1152,2304]{1,0:T(8,128)(2,1)S(1)}, bf16[2304,1152]{1,0:T(8,128)(2,1)S(1)}) custom-call(bf16[1152,2304]{1,0:T(8,128)(2,1)} %refs_0_.3, bf16[2304,1152]{1,0:T(8,128)(2,1)} %refs_1_.2), custom_call_target="tpu_custom_call" | custom-call | tf_op jit(solution)/shard_map/load/pallas_call | solution.py:94
  132.1 4.8 %enc_mlp_back_kernel.1 = (bf16[96,3456]{1,0:T(8,128)(2,1)S(1)}, bf16[96,1152]{1,0:T(8,128)(2,1)S(1)}) custom-call(f32[96,1152]{1,0:T(8,128)S(1)} %get-tuple-element.278.refs_0_.refs_5_, f32[96,2304]{1,0:T(8,128)} %copy-done.27, f32[6,1152]{1,0:T(8,128)S(1)} %reshape_squeeze.6.refs_2_.refs_3_.refs_6_.refs_4_, ...), custom_call_target="tpu_custom_call" | custom-call | tf_op jit(solution)/shard_map/enc_mlp_back_kernel/pallas_call | solution.py:58
  140.7 2.9 weight_grads.7
  149.8 5.0 %attention_back_kernel.3 = (f32[96,1152]{1,0:T(8,128)S(1)}, bf16[96,1152]{1,0:T(8,128)(2,1)S(1)}, bf16[96,576]{1,0:T(8,128)(2,1)S(1)}, f32[96,1152]{1,0:T(8,128)...) custom-call(f32[96,1152]{1,0:T(8,128)S(1)} %get-tuple-element.278.refs_0_.refs_5_, ...), custom_call_target="tpu_custom_call" | custom-call | tf_op jit(solution)/shard_map/attention_back_kernel/pallas_call | solution.py:58
  164.9 4.5 %weight_grads.8 = (bf16[144,2304]{1,0:T(8,128)(2,1)}, f32[144,2304]{1,0:T(8,128)S(1)}) custom-call(bf16[128,2944]{1,0:T(8,128)(2,1)} %copy-done.3, bf16[128,2944]{1,0:T(8,128)(2,1)} %copy-done.57, bf16[128,2944]{1,0:T(8,128)(2,1)} %copy-done.58, bf16[128,2944]{1,0:T(8,128)(2,1)} %copy-done.59, bf16[128,2944]{1,0:T(8,128)(2,1)} %copy-done.30, ...), custom_call_target="tpu_custom_call" | custom-call | tf_op jit(solution)/shard_map/weight_grads/pallas_call | solution.py:607
  169.4 7.1 %collective-permute-done.36.refs_1_ = bf16[72,2304]{1,0:T(8,128)(2,1)S(1)} collective-permute-done((bf16[72,2304]{1,0:T(8,128)(2,1)S(1)}, bf16[72,2304]{1,0:T(8,128)(2,1)S(1)}, u32[]{:S(2)}, u32[]{:S(2)}) %collective-permute-start.36) | collective-permute-done | bytes 331808 | tf_op jit(solution)/shard_map/down_last/far/ppermute | solution.py:531
  183.6 3.5 %collective-permute-done.44.refs_1_ = f32[2,10,288]{2,1,0:T(8,128)S(1)} collective-permute-done((f32[2,10,288]{2,1,0:T(8,128)S(1)}, f32[2,10,288]{2,1,0:T(8,128)S(1)}, u32[]{:S(2)}, u32[]{:S(2)}) %collective-permute-start.44) | collective-permute-done | bytes 23072 | tf_op jit(solution)/shard_map/images/near/ppermute | solution.py:527
  189.3 5.0 %collective-permute-done.45.refs_1_ = f32[2,10,288]{2,1,0:T(8,128)S(1)} collective-permute-done((f32[2,10,288]{2,1,0:T(8,128)S(1)}, f32[2,10,288]{2,1,0:T(8,128)S(1)}, u32[]{:S(2)}, u32[]{:S(2)}) %collective-permute-start.45) | collective-permute-done | bytes 23072 | tf_op jit(solution)/shard_map/images/far/ppermute | solution.py:531
  198.1 2.7 weight_grads.9
  201.5 2.7 weight_grads.10
  205.7 8.5 %collective-permute-done.46.refs_5_ = bf16[96,2944]{1,0:T(8,128)(2,1)S(1)} collective-permute-done((bf16[96,2944]{1,0:T(8,128)(2,1)}, bf16[96,2944]{1,0:T(8,128)(2,1)S(1)}, u32[]{:S(2)}, u32[]{:S(2)}) %collective-permute-start.46) | collective-permute-done | bytes 565280 | tf_op jit(solution)/shard_map/K_far/near/ppermute | solution.py:527
  217.2 3.8 %weight_grads.11 = (bf16[144,2304]{1,0:T(8,128)(2,1)S(1)}, f32[144,2304]{1,0:T(8,128)S(1)}) custom-call(bf16[96,5248]{1,0:T(8,128)(2,1)} %copy-done.2, bf16[96,5248]{1,0:T(8,128)(2,1)} %collective-permute-done.14.refs_1_, bf16[96,5248]{1,0:T(8,128)(2,1)} %copy-done.53, bf16[96,5248]{1,0:T(8,128)(2,1)} %collective-permute-done.16.refs_3_, ...), custom_call_target="tpu_custom_call" | custom-call | tf_op jit(solution)/shard_map/weight_grads/pallas_call | solution.py:607
  221.0 6.5 %collective-permute-start.56 = (bf16[72,2304]{1,0:T(8,128)(2,1)S(1)}, bf16[72,2304]{1,0:T(8,128)(2,1)S(1)}, u32[]{:S(2)}, u32[]{:S(2)}) collective-permute-start(bf16[72,2304]{1,0:T(8,128)(2,1)S(1)} %get-tuple-element.346.refs_9_), channel_id=1, source_target_pairs={{0,4},{2,6},{4,0},{6,2},{1,5},{3,7},{5,1},{7,3},{8,12},{10,14},{12... | collective-permute-start | bytes 995336 | tf_op jit(solution)/shard_map/attn_last/far/ppermute | solution.py:531
  229.3 12.3 %collective-permute-done.51.refs_1_ = bf16[144,2304]{1,0:T(8,128)(2,1)S(1)} collective-permute-done((bf16[144,2304]{1,0:T(8,128)(2,1)S(1)}, bf16[144,2304]{1,0:T(8,128)(2,1)S(1)}, u32[]{:S(2)}, u32[]{:S(2)}) %collective-permute-start.51) | collective-permute-done | bytes 663584 | tf_op jit(solution)/shard_map/enc_up_first/hi/ppermute | solution.py:539
  242.9 12.2 %collective-permute-start.54 = (bf16[72,2304]{1,0:T(8,128)(2,1)S(1)}, bf16[72,2304]{1,0:T(8,128)(2,1)S(1)}, u32[]{:S(2)}, u32[]{:S(2)}) collective-permute-start(bf16[72,2304]{1,0:T(8,128)(2,1)S(1)} %get-tuple-element.359.refs_2_), channel_id=1, source_target_pairs={{0,4},{2,6},{4,0},{6,2},{1,5},{3,7},{5,1},{7,3},{8,12},{10,14},{12... | collective-permute-start | bytes 995336 | tf_op jit(solution)/shard_map/enc_up_last/far/ppermute | solution.py:531
  257.5 8.9 %collective-permute-start.58 = (bf16[72,2304]{1,0:T(8,128)(2,1)S(1)}, bf16[72,2304]{1,0:T(8,128)(2,1)S(1)}, u32[]{:S(2)}, u32[]{:S(2)}) collective-permute-start(bf16[72,2304]{1,0:T(8,128)(2,1)S(1)} %get-tuple-element.368.refs_2_), channel_id=1, source_target_pairs={{0,4},{2,6},{4,0},{6,2},{1,5},{3,7},{5,1},{7,3},{8,12},{10,14},{12... | collective-permute-start | bytes 995336 | tf_op jit(solution)/shard_map/enc_attn_last/far/ppermute | solution.py:531
  268.8 14.9 %collective-permute-done.54.refs_1_ = bf16[72,2304]{1,0:T(8,128)(2,1)S(1)} collective-permute-done((bf16[72,2304]{1,0:T(8,128)(2,1)S(1)}, bf16[72,2304]{1,0:T(8,128)(2,1)S(1)}, u32[]{:S(2)}, u32[]{:S(2)}) %collective-permute-start.54) | collective-permute-done | bytes 331808 | tf_op jit(solution)/shard_map/enc_up_last/far/ppermute | solution.py:531
  285.8 5.1 %collective-permute-done.59.refs_1_ = bf16[72,2304]{1,0:T(8,128)(2,1)S(1)} collective-permute-done((bf16[72,2304]{1,0:T(8,128)(2,1)S(1)}, bf16[72,2304]{1,0:T(8,128)(2,1)S(1)}, u32[]{:S(2)}, u32[]{:S(2)}) %collective-permute-start.59) | collective-permute-done | bytes 331808 | tf_op jit(solution)/shard_map/enc_down_last/far/ppermute | solution.py:531
  (334 shorter events, 127.5 us)
Async XLA Ops:
  2.8 16.8 %collective-permute-start.2 = (bf16[48,1280]{1,0:T(8,128)(2,1)S(1)}, bf16[48,1280]{1,0:T(8,128)(2,1)S(1)}, u32[]{:S(2)}, u32[]{:S(2)}) collective-permute-start(bf16[48,1280]{1,0:T(8,128)(2,1)S(1)} %get-tuple-element.390), channel_id=1, source_target_pairs={{0,0},{2,2},{4,8},{6,10},{8,4},{10,6},{12,12},{14,14},{16,16},{18,... | collective-permute-start | bytes 368648 | tf_op jit(solution)/shard_map/spread/ppermute | solution.py:557
  3.5 16.2 %collective-permute-start.3 = (bf16[48,1280]{1,0:T(8,128)(2,1)S(1)}, bf16[48,1280]{1,0:T(8,128)(2,1)S(1)}, u32[]{:S(2)}, u32[]{:S(2)}) collective-permute-start(bf16[48,1280]{1,0:T(8,128)(2,1)S(1)} %get-tuple-element.389), channel_id=1, source_target_pairs={{0,2},{2,0},{4,10},{6,8},{8,6},{10,4},{12,14},{14,12},{16,18},{18,... | collective-permute-start | bytes 368648 | tf_op jit(solution)/shard_map/spread/ppermute | solution.py:557
  47.0 25.6 %collective-permute-start.14 = (bf16[96,5248]{1,0:T(8,128)(2,1)S(1)}, bf16[96,5248]{1,0:T(8,128)(2,1)}, u32[]{:S(2)}, u32[]{:S(2)}) collective-permute-start(bf16[96,5248]{1,0:T(8,128)(2,1)S(1)} %get-tuple-element.228.refs_0_), channel_id=1, source_target_pairs={{0,2},{2,0},{4,6},{6,4},{1,3},{3,1},{5,7},{7,5},{8,10},{10,8},{12,... | collective-permute-start | bytes 3022856 | tf_op jit(solution)/shard_map/F_far/near/ppermute | solution.py:527
  64.5 22.1 %collective-permute-start.18 = (bf16[128,2944]{1,0:T(8,128)(2,1)S(1)}, bf16[128,2944]{1,0:T(8,128)(2,1)S(1)}, u32[]{:S(2)}, u32[]{:S(2)}) collective-permute-start(bf16[128,2944]{1,0:T(8,128)(2,1)S(1)} %get-tuple-element.244.refs_0_), channel_id=1, source_target_pairs={{0,2},{2,0},{4,6},{6,4},{1,3},{3,1},{5,7},{7,5},{8,10},{10,8},{12,... | collective-permute-start | bytes 2261000 | tf_op jit(solution)/shard_map/A_far/near/ppermute | solution.py:527
  75.5 30.0 %collective-permute-start.20 = (bf16[128,3456]{1,0:T(8,128)(2,1)S(1)}, bf16[128,3456]{1,0:T(8,128)(2,1)S(1)}, u32[]{:S(2)}, u32[]{:S(2)}) collective-permute-start(bf16[128,3456]{1,0:T(8,128)(2,1)S(1)} %get-tuple-element.263.refs_4_.refs_0_), channel_id=1, source_target_pairs={{0,2},{2,0},{4,6},{6,4},{1,3},{3,1},{5,7},{7,5},{8,10},{10,8},{12,... | collective-permute-start | bytes 2654216 | tf_op jit(solution)/shard_map/M_far/near/ppermute | solution.py:527
  96.6 14.3 %collective-permute-start.22 = (bf16[128,2944]{1,0:T(8,128)(2,1)S(1)}, bf16[128,2944]{1,0:T(8,128)(2,1)S(1)}, u32[]{:S(2)}, u32[]{:S(2)}) collective-permute-start(bf16[128,2944]{1,0:T(8,128)(2,1)S(1)} %get-tuple-element.244.refs_0_), channel_id=1, source_target_pairs={{0,8},{8,0},{16,24},{24,16},{1,9},{9,1},{17,25},{25,17},{2,10},{10... | collective-permute-start | bytes 2261000 | tf_op jit(solution)/shard_map/A_core/core/ppermute | solution.py:523
  96.6 16.7 %collective-permute-start.24 = (bf16[128,3456]{1,0:T(8,128)(2,1)S(1)}, bf16[128,3456]{1,0:T(8,128)(2,1)S(1)}, u32[]{:S(2)}, u32[]{:S(2)}) collective-permute-start(bf16[128,3456]{1,0:T(8,128)(2,1)S(1)} %get-tuple-element.263.refs_4_.refs_0_), channel_id=1, source_target_pairs={{0,8},{8,0},{16,24},{24,16},{1,9},{9,1},{17,25},{25,17},{2,10},{10... | collective-permute-start | bytes 2654216 | tf_op jit(solution)/shard_map/M_core/core/ppermute | solution.py:523
  110.9 16.6 %collective-permute-start.26 = (bf16[128,2304]{1,0:T(8,128)(2,1)S(1)}, bf16[128,2304]{1,0:T(8,128)(2,1)S(1)}, u32[]{:S(2)}, u32[]{:S(2)}) collective-permute-start(bf16[128,2304]{1,0:T(8,128)(2,1)S(1)} %get-tuple-element.277.refs_4_), channel_id=1, source_target_pairs={{0,2},{2,0},{4,6},{6,4},{1,3},{3,1},{5,7},{7,5},{8,10},{10,8},{12,... | collective-permute-start | bytes 1769480 | tf_op jit(solution)/shard_map/G_far/near/ppermute | solution.py:527
  119.6 17.3 %collective-permute-start.27 = (bf16[144,2304]{1,0:T(8,128)(2,1)S(1)}, bf16[144,2304]{1,0:T(8,128)(2,1)S(1)}, u32[]{:S(2)}, u32[]{:S(2)}) collective-permute-start(bf16[144,2304]{1,0:T(8,128)(2,1)S(1)} %get-tuple-element.285), channel_id=1, source_target_pairs={{0,16},{8,24},{16,0},{24,8},{1,17},{9,25},{17,1},{25,9},{2,18},{10... | collective-permute-start | bytes 1990664 | tf_op jit(solution)/shard_map/down_first/hi/ppermute | solution.py:539
  121.1 18.0 %collective-permute-start.30 = (bf16[128,2304]{1,0:T(8,128)(2,1)S(1)}, bf16[128,2304]{1,0:T(8,128)(2,1)S(1)}, u32[]{:S(2)}, u32[]{:S(2)}) collective-permute-start(bf16[128,2304]{1,0:T(8,128)(2,1)S(1)} %get-tuple-element.277.refs_4_), channel_id=1, source_target_pairs={{0,8},{8,0},{16,24},{24,16},{1,9},{9,1},{17,25},{25,17},{2,10},{10... | collective-permute-start | bytes 1769480 | tf_op jit(solution)/shard_map/G_core/core/ppermute | solution.py:523
  121.1 23.5 %collective-permute-start.29 = (bf16[128,2944]{1,0:T(8,128)(2,1)S(1)}, bf16[128,2944]{1,0:T(8,128)(2,1)S(1)}, u32[]{:S(2)}, u32[]{:S(2)}) collective-permute-start(bf16[128,2944]{1,0:T(8,128)(2,1)S(1)} %get-tuple-element.288.refs_4_), channel_id=1, source_target_pairs={{0,2},{2,0},{4,6},{6,4},{1,3},{3,1},{5,7},{7,5},{8,10},{10,8},{12,... | collective-permute-start | bytes 2261000 | tf_op jit(solution)/shard_map/H_far/near/ppermute | solution.py:527
  127.5 20.5 %collective-permute-start.38 = (bf16[128,2944]{1,0:T(8,128)(2,1)S(1)}, bf16[128,2944]{1,0:T(8,128)(2,1)S(1)}, u32[]{:S(2)}, u32[]{:S(2)}) collective-permute-start(bf16[128,2944]{1,0:T(8,128)(2,1)S(1)} %get-tuple-element.288.refs_4_), channel_id=1, source_target_pairs={{0,8},{8,0},{16,24},{24,16},{1,9},{9,1},{17,25},{25,17},{2,10},{10... | collective-permute-start | bytes 2261000 | tf_op jit(solution)/shard_map/H_core/core/ppermute | solution.py:523
  136.9 20.2 %collective-permute-start.34 = (bf16[96,3456]{1,0:T(8,128)(2,1)S(1)}, bf16[96,3456]{1,0:T(8,128)(2,1)}, u32[]{:S(2)}, u32[]{:S(2)}) collective-permute-start(bf16[96,3456]{1,0:T(8,128)(2,1)S(1)} %get-tuple-element.307.refs_4_), channel_id=1, source_target_pairs={{0,2},{2,0},{4,6},{6,4},{1,3},{3,1},{5,7},{7,5},{8,10},{10,8},{12,... | collective-permute-start | bytes 1990664 | tf_op jit(solution)/shard_map/E_far/near/ppermute | solution.py:527
  146.2 17.2 %collective-permute-start.39 = (bf16[128,2944]{1,0:T(8,128)(2,1)S(1)}, bf16[128,2944]{1,0:T(8,128)(2,1)S(1)}, u32[]{:S(2)}, u32[]{:S(2)}) collective-permute-start(bf16[128,2944]{1,0:T(8,128)(2,1)S(1)} %collective-permute-done.29.refs_5_), channel_id=1, source_target_pairs={{0,8},{8,0},{16,24},{24,16},{1,9},{9,1},{17,25},{25,17},{2,10},{10... | collective-permute-start | bytes 2261000 | tf_op jit(solution)/shard_map/H_both/core/ppermute | solution.py:523
  146.2 30.2 %collective-permute-start.37 = (bf16[144,2304]{1,0:T(8,128)(2,1)S(1)}, bf16[144,2304]{1,0:T(8,128)(2,1)S(1)}, u32[]{:S(2)}, u32[]{:S(2)}) collective-permute-start(bf16[144,2304]{1,0:T(8,128)(2,1)S(1)} %get-tuple-element.310), channel_id=1, source_target_pairs={{0,16},{8,24},{16,0},{24,8},{1,17},{9,25},{17,1},{25,9},{2,18},{10... | collective-permute-start | bytes 1990664 | tf_op jit(solution)/shard_map/up_first/hi/ppermute | solution.py:539
  147.7 41.5 %collective-permute-start.15 = (bf16[96,5248]{1,0:T(8,128)(2,1)S(1)}, bf16[96,5248]{1,0:T(8,128)(2,1)S(1)}, u32[]{:S(2)}, u32[]{:S(2)}) collective-permute-start(bf16[96,5248]{1,0:T(8,128)(2,1)S(1)} %get-tuple-element.228.refs_0_), channel_id=1, source_target_pairs={{0,8},{8,0},{16,24},{24,16},{1,9},{9,1},{17,25},{25,17},{2,10},{10... | collective-permute-start | bytes 3022856 | tf_op jit(solution)/shard_map/F_core/core/ppermute | solution.py:523
  158.6 17.8 %collective-permute-start.36 = (bf16[72,2304]{1,0:T(8,128)(2,1)S(1)}, bf16[72,2304]{1,0:T(8,128)(2,1)S(1)}, u32[]{:S(2)}, u32[]{:S(2)}) collective-permute-start(bf16[72,2304]{1,0:T(8,128)(2,1)S(1)} %get-tuple-element.309), channel_id=1, source_target_pairs={{0,4},{2,6},{4,0},{6,2},{1,5},{3,7},{5,1},{7,3},{8,12},{10,14},{12... | collective-permute-start | bytes 995336 | tf_op jit(solution)/shard_map/down_last/far/ppermute | solution.py:531
  159.7 36.3 %collective-permute-start.16 = (bf16[96,5248]{1,0:T(8,128)(2,1)}, bf16[96,5248]{1,0:T(8,128)(2,1)}, u32[]{:S(2)}, u32[]{:S(2)}) collective-permute-start(bf16[96,5248]{1,0:T(8,128)(2,1)} %collective-permute-done.14.refs_1_), channel_id=1, source_target_pairs={{0,8},{8,0},{16,24},{24,16},{1,9},{9,1},{17,25},{25,17},{2,10},{10... | collective-permute-start | bytes 3022856 | tf_op jit(solution)/shard_map/F_both/core/ppermute | solution.py:523
  183.2 14.9 %collective-permute-start.42 = (bf16[96,3456]{1,0:T(8,128)(2,1)}, bf16[96,3456]{1,0:T(8,128)(2,1)}, u32[]{:S(2)}, u32[]{:S(2)}) collective-permute-start(bf16[96,3456]{1,0:T(8,128)(2,1)} %collective-permute-done.34.refs_5_), channel_id=1, source_target_pairs={{0,8},{8,0},{16,24},{24,16},{1,9},{9,1},{17,25},{25,17},{2,10},{10... | collective-permute-start | bytes 1990664 | tf_op jit(solution)/shard_map/E_both/core/ppermute | solution.py:523
  187.0 17.2 %collective-permute-start.40 = (bf16[144,2304]{1,0:T(8,128)(2,1)}, bf16[144,2304]{1,0:T(8,128)(2,1)}, u32[]{:S(2)}, u32[]{:S(2)}) collective-permute-start(bf16[144,2304]{1,0:T(8,128)(2,1)} %get-tuple-element.315), channel_id=1, source_target_pairs={{0,16},{8,24},{16,0},{24,8},{1,17},{9,25},{17,1},{25,9},{2,18},{10... | collective-permute-start | bytes 1990664 | tf_op jit(solution)/shard_map/attn_first/hi/ppermute | solution.py:539
  194.3 19.9 %collective-permute-start.46 = (bf16[96,2944]{1,0:T(8,128)(2,1)}, bf16[96,2944]{1,0:T(8,128)(2,1)S(1)}, u32[]{:S(2)}, u32[]{:S(2)}) collective-permute-start(bf16[96,2944]{1,0:T(8,128)(2,1)} %get-tuple-element.305.refs_4_), channel_id=1, source_target_pairs={{0,2},{2,0},{4,6},{6,4},{1,3},{3,1},{5,7},{7,5},{8,10},{10,8},{12,... | collective-permute-start | bytes 1695752 | tf_op jit(solution)/shard_map/K_far/near/ppermute | solution.py:527
  195.9 19.2 %collective-permute-start.47 = (bf16[96,2944]{1,0:T(8,128)(2,1)}, bf16[96,2944]{1,0:T(8,128)(2,1)S(1)}, u32[]{:S(2)}, u32[]{:S(2)}) collective-permute-start(bf16[96,2944]{1,0:T(8,128)(2,1)} %get-tuple-element.305.refs_4_), channel_id=1, source_target_pairs={{0,8},{8,0},{16,24},{24,16},{1,9},{9,1},{17,25},{25,17},{2,10},{10... | collective-permute-start | bytes 1695752 | tf_op jit(solution)/shard_map/K_core/core/ppermute | solution.py:523
  196.0 32.3 %collective-permute-start.52 = (bf16[72,2304]{1,0:T(8,128)(2,1)}, bf16[72,2304]{1,0:T(8,128)(2,1)S(1)}, u32[]{:S(2)}, u32[]{:S(2)}) collective-permute-start(bf16[72,2304]{1,0:T(8,128)(2,1)} %copy-done.39), channel_id=1, source_target_pairs={{0,4},{2,6},{4,0},{6,2},{1,5},{3,7},{5,1},{7,3},{8,12},{10,14},{12... | collective-permute-start | bytes 995336 | tf_op jit(solution)/shard_map/up_last/far/ppermute | solution.py:531
  200.9 13.3 %collective-permute-start.57 = (f32[4,10,288]{2,1,0:T(8,128)S(1)}, f32[4,10,288]{2,1,0:T(8,128)S(1)}, u32[]{:S(2)}, u32[]{:S(2)}) collective-permute-start(f32[4,10,288]{2,1,0:T(8,128)S(1)} %all_images_kernel.1), channel_id=1, source_target_pairs={{0,16},{8,24},{16,0},{24,8},{1,17},{9,25},{17,1},{25,9},{2,18},{10... | collective-permute-start | bytes 138248 | tf_op jit(solution)/shard_map/modulation/hi/ppermute | solution.py:539
  205.6 15.4 %collective-permute-start.50 = (bf16[112,1152]{1,0:T(8,128)(2,1)S(1)}, bf16[112,1152]{1,0:T(8,128)(2,1)S(1)}, u32[]{:S(2)}, u32[]{:S(2)}) collective-permute-start(bf16[112,1152]{1,0:T(8,128)(2,1)S(1)} %pad_maximum_fusion.2), channel_id=1, source_target_pairs={{2,0},{0,2},{10,4},{8,6},{6,8},{4,10},{14,12},{12,14},{18,16},{16,... | collective-permute-start | bytes 774152 | tf_op jit(solution)/shard_map/parts/collect/ppermute | solution.py:564
  215.1 14.2 %collective-permute-start.53 = (bf16[144,2304]{1,0:T(8,128)(2,1)S(1)}, bf16[144,2304]{1,0:T(8,128)(2,1)S(1)}, u32[]{:S(2)}, u32[]{:S(2)}) collective-permute-start(bf16[144,2304]{1,0:T(8,128)(2,1)S(1)} %get-tuple-element.340.refs_2_), channel_id=1, source_target_pairs={{0,16},{8,24},{16,0},{24,8},{1,17},{9,25},{17,1},{25,9},{2,18},{10... | collective-permute-start | bytes 1990664 | tf_op jit(solution)/shard_map/enc_down_first/hi/ppermute | solution.py:539
  216.1 25.5 %collective-permute-start.51 = (bf16[144,2304]{1,0:T(8,128)(2,1)S(1)}, bf16[144,2304]{1,0:T(8,128)(2,1)S(1)}, u32[]{:S(2)}, u32[]{:S(2)}) collective-permute-start(bf16[144,2304]{1,0:T(8,128)(2,1)S(1)} %get-tuple-element.339.refs_9_), channel_id=1, source_target_pairs={{0,16},{8,24},{16,0},{24,8},{1,17},{9,25},{17,1},{25,9},{2,18},{10... | collective-permute-start | bytes 1990664 | tf_op jit(solution)/shard_map/enc_up_first/hi/ppermute | solution.py:539
  221.0 34.0 %collective-permute-start.56 = (bf16[72,2304]{1,0:T(8,128)(2,1)S(1)}, bf16[72,2304]{1,0:T(8,128)(2,1)S(1)}, u32[]{:S(2)}, u32[]{:S(2)}) collective-permute-start(bf16[72,2304]{1,0:T(8,128)(2,1)S(1)} %get-tuple-element.346.refs_9_), channel_id=1, source_target_pairs={{0,4},{2,6},{4,0},{6,2},{1,5},{3,7},{5,1},{7,3},{8,12},{10,14},{12... | collective-permute-start | bytes 995336 | tf_op jit(solution)/shard_map/attn_last/far/ppermute | solution.py:531
  227.5 29.8 %collective-permute-start.55 = (bf16[144,2304]{1,0:T(8,128)(2,1)S(1)}, bf16[144,2304]{1,0:T(8,128)(2,1)S(1)}, u32[]{:S(2)}, u32[]{:S(2)}) collective-permute-start(bf16[144,2304]{1,0:T(8,128)(2,1)S(1)} %get-tuple-element.356.refs_2_), channel_id=1, source_target_pairs={{0,16},{8,24},{16,0},{24,8},{1,17},{9,25},{17,1},{25,9},{2,18},{10... | collective-permute-start | bytes 1990664 | tf_op jit(solution)/shard_map/enc_attn_first/hi/ppermute | solution.py:539
  242.9 40.9 %collective-permute-start.54 = (bf16[72,2304]{1,0:T(8,128)(2,1)S(1)}, bf16[72,2304]{1,0:T(8,128)(2,1)S(1)}, u32[]{:S(2)}, u32[]{:S(2)}) collective-permute-start(bf16[72,2304]{1,0:T(8,128)(2,1)S(1)} %get-tuple-element.359.refs_2_), channel_id=1, source_target_pairs={{0,4},{2,6},{4,0},{6,2},{1,5},{3,7},{5,1},{7,3},{8,12},{10,14},{12... | collective-permute-start | bytes 995336 | tf_op jit(solution)/shard_map/enc_up_last/far/ppermute | solution.py:531
  257.2 33.7 %collective-permute-start.59 = (bf16[72,2304]{1,0:T(8,128)(2,1)S(1)}, bf16[72,2304]{1,0:T(8,128)(2,1)S(1)}, u32[]{:S(2)}, u32[]{:S(2)}) collective-permute-start(bf16[72,2304]{1,0:T(8,128)(2,1)S(1)} %get-tuple-element.367.refs_2_), channel_id=1, source_target_pairs={{0,4},{2,6},{4,0},{6,2},{1,5},{3,7},{5,1},{7,3},{8,12},{10,14},{12... | collective-permute-start | bytes 995336 | tf_op jit(solution)/shard_map/enc_down_last/far/ppermute | solution.py:531
  257.5 40.5 %collective-permute-start.58 = (bf16[72,2304]{1,0:T(8,128)(2,1)S(1)}, bf16[72,2304]{1,0:T(8,128)(2,1)S(1)}, u32[]{:S(2)}, u32[]{:S(2)}) collective-permute-start(bf16[72,2304]{1,0:T(8,128)(2,1)S(1)} %get-tuple-element.368.refs_2_), channel_id=1, source_target_pairs={{0,4},{2,6},{4,0},{6,2},{1,5},{3,7},{5,1},{7,3},{8,12},{10,14},{12... | collective-permute-start | bytes 995336 | tf_op jit(solution)/shard_map/enc_attn_last/far/ppermute | solution.py:531
  (99 other events, 857.3 us)
